TPU v7x, 128 devices: a whole 4x4x4 slice. The times are simulated.
128 devices in a mesh: section: 2 (over core), tensor: 4 (over z), dp: 16 (over y, x).
Axes of the slice: x: 4, y: 4, z: 4, core: 2. Of those that a mesh axis runs over, the one named last changes fastest.
Arguments:
- tokens: bfloat16 [4096, 1536], P('dp'), may hold values from -6 to 6
- plan_order: int32 [16, 2], P('dp'), may hold values from 0 to 1, each once within a row
- cotangent: bfloat16 [4096, 1536], P('dp'), may hold values from -6 to 6
- norm_gains: float32 [2, 2, 1536], P('section'), may hold values from 0.5 to 1.5
- ffn_gate: bfloat16 [2, 1536, 4608], P('section', None, 'tensor'), may hold values from -0.15625 to 0.15625
- ffn_up: bfloat16 [2, 1536, 4608], P('section', None, 'tensor'), may hold values from -0.15625 to 0.15625
- ffn_down: bfloat16 [2, 4608, 1536], P('section', 'tensor'), may hold values from -0.09375 to 0.09375
- rec_in: bfloat16 [1536, 2, 2048], P('section', None, 'tensor'), may hold values from -0.15625 to 0.15625
- rec_gates: bfloat16 [128, 2, 2048], P('section', None, 'tensor'), may hold values from -0.5 to 0.5
- rec_conv: bfloat16 [4, 2048], P('section', 'tensor'), may hold values from -3 to 3
- rec_vec: bfloat16 [4, 2048], P('section', 'tensor'), may hold values from -8 to 2
- rec_out: bfloat16 [2048, 1536], P('tensor', 'section'), may hold values from -0.125 to 0.125
- att_q: bfloat16 [1536, 1536], P('section', 'tensor'), may hold values from -0.15625 to 0.15625
- att_kv: bfloat16 [1536, 256], P('section'), may hold values from -0.15625 to 0.15625
- att_out: bfloat16 [1536, 1536], P('tensor', 'section'), may hold values from -0.4375 to 0.4375
Outputs:
- boundary: float32 [2, 4096, 1536], P('section', 'dp')
- grad_gains: float32 [2, 2, 1536], P('section')
- grad_ffn_gate: float32 [2, 1536, 4608], P('section', None, 'tensor')
- grad_ffn_up: float32 [2, 1536, 4608], P('section', None, 'tensor')
- grad_ffn_down: float32 [2, 4608, 1536], P('section', 'tensor')
- grad_rec_in: float32 [1536, 2, 2048], P('section', None, 'tensor')
- grad_rec_gates: float32 [128, 2, 2048], P('section', None, 'tensor')
- grad_rec_conv: float32 [4, 2048], P('section', 'tensor')
- grad_rec_vec: float32 [4, 2048], P('section', 'tensor')
- grad_rec_out: float32 [2048, 1536], P('tensor', 'section')
- grad_att_q: float32 [1536, 1536], P('section', 'tensor')
- grad_att_kv: float32 [1536, 256], P('section')
- grad_att_out: float32 [1536, 1536], P('tensor', 'section')
Inputs may be any that keep to these rules, and one draw needn't show every extreme that they name: `plan_order`: each row is an order of the 2 micro-batches.
All inputs are finite; a program needn't handle non-finite values.
Results may differ from a plain program's by a relative error of at most 0.04.
Values may be sent and summed in bfloat16 or wider, within the bound.
A program may use at most 256 MiB of HBM per device.

v0:
```python
import jax
import jax.numpy as jnp
from jax import lax
from jax.sharding import PartitionSpec as P

HD = 128
BW = 128
SEQ = 128
MICRO = 2


NORM_EPS = 1e-06
RATE_FLOOR = 0.01


def from_behind(block, axis, distance):
    devices = range(lax.axis_size(axis))
    route = [(i - distance, i) for i in devices if i - distance in devices]
    return lax.ppermute(block, axis, route)


def rms_piece(values, gain):
    return values * lax.rsqrt(jnp.mean(values * values, -1, keepdims=True) + NORM_EPS) * gain


def softplus_fn(values):
    return jnp.maximum(values, 0.0) + jnp.log1p(jnp.exp(-jnp.abs(values)))


def geglu_piece(gate_pre, up_pre):
    return jax.nn.gelu(gate_pre, approximate=True) * up_pre


def conv_piece(inflow, conv_taps, offset):
    length = inflow.shape[0]
    padded = jnp.pad(inflow, ((3, 0), (0, 0)))
    result = offset[None, :] + conv_taps[0] * inflow
    for shift_by in range(1, 4):
        result = result + conv_taps[shift_by] * padded[3 - shift_by : 3 - shift_by + length]
    return result


def link_pairs(earlier, later):
    return (earlier[0] * later[0], later[0] * earlier[1] + later[1])


def lru_piece(conv_out, pre_input, pre_decay, branch, vectors):
    input_gate = jax.nn.sigmoid(pre_input + vectors[0])
    decay_gate = jax.nn.sigmoid(pre_decay + vectors[1])
    decay_rate = jnp.exp(-8.0 * decay_gate * softplus_fn(vectors[2]))
    scale_in = jnp.sqrt(jnp.maximum(1.0 - decay_rate * decay_rate, RATE_FLOOR))
    states = lax.associative_scan(
        link_pairs, (decay_rate, scale_in * input_gate * conv_out), axis=0
    )[1]
    return states * jax.nn.gelu(branch, approximate=True)


def attention_probs(raw_scores):
    length = raw_scores.shape[-1]
    row_ids = lax.broadcasted_iota(jnp.int32, (length, length), 0)
    col_ids = lax.broadcasted_iota(jnp.int32, (length, length), 1)
    allowed = col_ids <= row_ids
    scaled = jnp.where(allowed, raw_scores * HD ** (-0.5), -1e30)
    row_top = jnp.max(scaled, -1, keepdims=True)
    expo_terms = jnp.exp(scaled - row_top)
    return expo_terms / jnp.sum(expo_terms, -1, keepdims=True)


def dot_plain(left, right):
    return jnp.dot(left, right, preferred_element_type=jnp.float32)


def dot_right_t(left, right):
    return lax.dot_general(
        left, right, (((1,), (1,)), ((), ())), preferred_element_type=jnp.float32
    )


def dot_left_t(left, right):
    return lax.dot_general(
        left, right, (((0,), (0,)), ((), ())), preferred_element_type=jnp.float32
    )


def add_trees(first_tree, second_tree):
    return jax.tree.map(jnp.add, first_tree, second_tree)


def blank_recurrent(length, mixers):
    rec_width = mixers[4].shape[0]
    zero_rows = jnp.zeros((length, rec_width), jnp.float32)
    return (zero_rows, zero_rows, zero_rows, jnp.zeros((2, length, rec_width), jnp.float32))


def blank_attention(length, mixers):
    head_count = mixers[5].shape[1] // HD
    return (
        jnp.zeros((length, head_count, HD), jnp.bfloat16),
        jnp.zeros((length, 2 * HD), jnp.bfloat16),
        jnp.zeros((head_count, length, length), jnp.float32),
        jnp.zeros((length, head_count * HD), jnp.bfloat16),
    )


def gate_products(conv_bf, rec_gates):
    length = conv_bf.shape[0]
    rec_width = rec_gates.shape[2]
    head_count = rec_width // BW
    gate_mats = rec_gates.reshape(BW, 2, head_count, BW)
    conv_heads = conv_bf.reshape(length, head_count, BW)
    pre_both = jnp.einsum(
        "thi,iqhj->qthj", conv_heads, gate_mats, preferred_element_type=jnp.float32
    )
    return pre_both.reshape(2, length, rec_width)


def recurrent_forward(normed_bf, mixers):
    rec_in, rec_gates, rec_conv, rec_vec, rec_out, att_q, att_kv, att_out = mixers
    rec_width = rec_out.shape[0]
    both_proj = dot_plain(normed_bf, rec_in.reshape(rec_in.shape[0], 2 * rec_width))
    inflow = both_proj[:, :rec_width]
    branch = both_proj[:, rec_width:]
    vectors = rec_vec.astype(jnp.float32)
    conv_out = conv_piece(inflow, rec_conv.astype(jnp.float32), vectors[0])
    pre_both = gate_products(conv_out.astype(jnp.bfloat16), rec_gates)
    mixed_rec = lru_piece(conv_out, pre_both[0], pre_both[1], branch, vectors[1:])
    partial_value = dot_plain(mixed_rec.astype(jnp.bfloat16), rec_out)
    return (
        partial_value,
        (inflow, branch, conv_out, pre_both),
        blank_attention(normed_bf.shape[0], mixers),
    )


def attention_forward(normed_bf, mixers):
    rec_in, rec_gates, rec_conv, rec_vec, rec_out, att_q, att_kv, att_out = mixers
    length = normed_bf.shape[0]
    query_bf = dot_plain(normed_bf, att_q).astype(jnp.bfloat16).reshape(length, -1, HD)
    kv_bf = dot_plain(normed_bf, att_kv).astype(jnp.bfloat16)
    raw_scores = jnp.einsum(
        "ihd,jd->hij", query_bf, kv_bf[:, :HD], preferred_element_type=jnp.float32
    )
    attn_probs = attention_probs(raw_scores)
    attended = jnp.einsum(
        "hij,jd->ihd",
        attn_probs.astype(jnp.bfloat16),
        kv_bf[:, HD:],
        preferred_element_type=jnp.float32,
    )
    attended = attended.reshape(length, -1).astype(jnp.bfloat16)
    partial_value = dot_plain(attended, att_out)
    return (partial_value, blank_recurrent(length, mixers), (query_bf, kv_bf, attn_probs, attended))


def recurrent_backward(grad_mixed, normed_bf, mixers, rec_saved, att_saved):
    rec_in, rec_gates, rec_conv, rec_vec, rec_out, att_q, att_kv, att_out = mixers
    inflow, branch, conv_out, pre_both = rec_saved
    length = inflow.shape[0]
    rec_width = rec_out.shape[0]
    head_count = rec_width // BW
    vectors = rec_vec.astype(jnp.float32)
    mixed_rec, pull_lru = jax.vjp(
        lru_piece, conv_out, pre_both[0], pre_both[1], branch, vectors[1:]
    )
    g_rec_out = dot_left_t(mixed_rec.astype(jnp.bfloat16), grad_mixed)
    g_mixed_rec = dot_right_t(grad_mixed, rec_out)
    g_conv_direct, g_pre_input, g_pre_decay, g_branch, g_tail = pull_lru(g_mixed_rec)
    g_pre_heads = (
        jnp.stack([g_pre_input, g_pre_decay])
        .astype(jnp.bfloat16)
        .reshape(2, length, head_count, BW)
    )
    gate_mats = rec_gates.reshape(BW, 2, head_count, BW)
    g_conv_gates = jnp.einsum(
        "qthj,iqhj->thi", g_pre_heads, gate_mats, preferred_element_type=jnp.float32
    ).reshape(length, rec_width)
    conv_heads = conv_out.astype(jnp.bfloat16).reshape(length, head_count, BW)
    g_gates = jnp.einsum(
        "thi,qthj->iqhj", conv_heads, g_pre_heads, preferred_element_type=jnp.float32
    ).reshape(BW, 2, rec_width)
    _, pull_conv = jax.vjp(conv_piece, inflow, rec_conv.astype(jnp.float32), vectors[0])
    g_inflow, g_taps, g_bias = pull_conv(g_conv_direct + g_conv_gates)
    g_both = jnp.concatenate([g_inflow, g_branch], -1).astype(jnp.bfloat16)
    grad_normed = dot_right_t(g_both, rec_in.reshape(rec_in.shape[0], 2 * rec_width))
    g_rec_in = dot_left_t(normed_bf, g_both).reshape(rec_in.shape[0], 2, rec_width)
    g_vec = jnp.concatenate([g_bias[None, :], g_tail], 0)
    rec_grads = (g_rec_in, g_gates, g_taps, g_vec, g_rec_out)
    att_grads = (jnp.zeros(att_q.shape, jnp.float32), jnp.zeros(att_out.shape, jnp.float32))
    return (grad_normed, jnp.zeros((length, 2 * HD), jnp.float32), rec_grads, att_grads)


def attention_backward(grad_mixed, normed_bf, mixers, rec_saved, att_saved):
    rec_in, rec_gates, rec_conv, rec_vec, rec_out, att_q, att_kv, att_out = mixers
    query_bf, kv_bf, attn_probs, attended = att_saved
    length = query_bf.shape[0]
    g_att_out = dot_left_t(attended, grad_mixed)
    g_attended = dot_right_t(grad_mixed, att_out).astype(jnp.bfloat16).reshape(length, -1, HD)
    g_probs = jnp.einsum(
        "ihd,jd->hij", g_attended, kv_bf[:, HD:], preferred_element_type=jnp.float32
    )
    g_values = jnp.einsum(
        "hij,ihd->jd",
        attn_probs.astype(jnp.bfloat16),
        g_attended,
        preferred_element_type=jnp.float32,
    )
    row_totals = jnp.sum(attn_probs * g_probs, -1, keepdims=True)
    g_raw = (attn_probs * (g_probs - row_totals) * HD ** (-0.5)).astype(jnp.bfloat16)
    g_query = jnp.einsum("hij,jd->ihd", g_raw, kv_bf[:, :HD], preferred_element_type=jnp.float32)
    g_query = g_query.reshape(length, -1).astype(jnp.bfloat16)
    g_keys = jnp.einsum("hij,ihd->jd", g_raw, query_bf, preferred_element_type=jnp.float32)
    grad_normed = dot_right_t(g_query, att_q)
    g_att_q = dot_left_t(normed_bf, g_query)
    rec_grads = tuple((jnp.zeros(weight_part.shape, jnp.float32) for weight_part in mixers[:5]))
    return (grad_normed, jnp.concatenate([g_keys, g_values], -1), rec_grads, (g_att_q, g_att_out))


def tensor_total(partial_value):
    return lax.psum(partial_value.astype(jnp.bfloat16), "tensor").astype(jnp.float32)


def block_forward(section_in, section_id, mixers, ffn_parts, gain_pair):
    normed_bf = rms_piece(section_in, gain_pair[0]).astype(jnp.bfloat16)
    partial_value, rec_saved, att_saved = lax.cond(
        section_id == 0, recurrent_forward, attention_forward, normed_bf, mixers
    )
    mixed_sum = tensor_total(partial_value)
    middle = section_in + mixed_sum
    second_bf = rms_piece(middle, gain_pair[1]).astype(jnp.bfloat16)
    hidden_bf = geglu_piece(
        dot_plain(second_bf, ffn_parts[0]), dot_plain(second_bf, ffn_parts[1])
    ).astype(jnp.bfloat16)
    result = middle + tensor_total(dot_plain(hidden_bf, ffn_parts[2]))
    return (result, mixed_sum)


def block_backward(section_in, grad_out, section_id, mixers, ffn_parts, gain_pair):
    normed_bf = rms_piece(section_in, gain_pair[0]).astype(jnp.bfloat16)
    partial_value, rec_saved, att_saved = lax.cond(
        section_id == 0, recurrent_forward, attention_forward, normed_bf, mixers
    )
    mixed_sum = tensor_total(partial_value)
    middle = section_in + mixed_sum
    second_bf = rms_piece(middle, gain_pair[1]).astype(jnp.bfloat16)
    hidden, pull_geglu = jax.vjp(
        geglu_piece, dot_plain(second_bf, ffn_parts[0]), dot_plain(second_bf, ffn_parts[1])
    )
    grad_ffn_bf = grad_out.astype(jnp.bfloat16)
    g_down = dot_left_t(hidden.astype(jnp.bfloat16), grad_ffn_bf)
    g_gate, g_up = pull_geglu(dot_right_t(grad_ffn_bf, ffn_parts[2]))
    g_gate_bf = g_gate.astype(jnp.bfloat16)
    g_up_bf = g_up.astype(jnp.bfloat16)
    part_second = dot_right_t(g_gate_bf, ffn_parts[0]) + dot_right_t(g_up_bf, ffn_parts[1])
    g_ffn_gate = dot_left_t(second_bf, g_gate_bf)
    g_ffn_up = dot_left_t(second_bf, g_up_bf)
    g_second = lax.psum(part_second.astype(jnp.bfloat16), "tensor").astype(jnp.float32)
    _, pull_second = jax.vjp(rms_piece, middle, gain_pair[1])
    g_middle_norm, g_gain_second = pull_second(g_second)
    g_middle = grad_out + g_middle_norm
    part_first, part_kv, rec_grads, att_grads = lax.cond(
        section_id == 0,
        recurrent_backward,
        attention_backward,
        g_middle.astype(jnp.bfloat16),
        normed_bf,
        mixers,
        rec_saved,
        att_saved,
    )
    g_first, g_kv = (
        lax.psum(part_first.astype(jnp.bfloat16), "tensor").astype(jnp.float32),
        lax.psum(part_kv.astype(jnp.bfloat16), "tensor").astype(jnp.float32),
    )
    g_kv_bf = g_kv.astype(jnp.bfloat16)
    g_first = g_first + dot_right_t(g_kv_bf, mixers[6])
    g_att_kv = dot_left_t(normed_bf, g_kv_bf)
    _, pull_first = jax.vjp(rms_piece, section_in, gain_pair[0])
    g_in_norm, g_gain_first = pull_first(g_first)
    grad_in = g_middle + g_in_norm
    section_grads = (jnp.stack([g_gain_first, g_gain_second]), g_ffn_gate, g_ffn_up, g_down)
    mixer_grads = rec_grads + (att_grads[0], g_att_kv, att_grads[1])
    return (grad_in, section_grads, mixer_grads)


def per_device(
    tokens,
    plan_order,
    cotangent,
    norm_gains,
    ffn_gate,
    ffn_up,
    ffn_down,
    rec_in,
    rec_gates,
    rec_conv,
    rec_vec,
    rec_out,
    att_q,
    att_kv,
    att_out,
):
    section_id = lax.axis_index("section")
    mixers = (
        lax.all_gather(rec_in, "section", axis=0, tiled=True),
        lax.all_gather(rec_gates, "section", axis=0, tiled=True),
        lax.all_gather(rec_conv, "section", axis=0, tiled=True),
        lax.all_gather(rec_vec, "section", axis=0, tiled=True),
        lax.all_gather(rec_out, "section", axis=1, tiled=True),
        lax.all_gather(att_q, "section", axis=0, tiled=True),
        lax.all_gather(att_kv, "section", axis=0, tiled=True),
        lax.all_gather(att_out, "section", axis=1, tiled=True),
    )
    ffn_parts = (ffn_gate[0], ffn_up[0], ffn_down[0])
    gain_pair = norm_gains[0]
    model_width = tokens.shape[1]
    seq_tokens = tokens.reshape(MICRO, SEQ, model_width)
    seq_cot = cotangent.reshape(MICRO, SEQ, model_width)
    plan = plan_order[0]
    received = jnp.zeros((SEQ, model_width), jnp.bfloat16)
    inputs_kept = []
    sums_kept = []
    finished = []
    for tick_index in range(MICRO + 1):
        first_slot = min(tick_index, MICRO - 1)
        fresh_mb = lax.dynamic_index_in_dim(seq_tokens, plan[first_slot], 0, keepdims=False)
        section_in = jnp.where(section_id == 0, fresh_mb, received).astype(jnp.float32)
        result, mixed_sum = block_forward(section_in, section_id, mixers, ffn_parts, gain_pair)
        inputs_kept.append(section_in)
        sums_kept.append(mixed_sum)
        if tick_index >= 1:
            finished.append(result)
        if tick_index < MICRO:
            received = from_behind(result.astype(jnp.bfloat16), "section", 1)
    returned = jnp.zeros((SEQ, model_width), jnp.bfloat16)
    slot_ids = jnp.arange(MICRO, dtype=jnp.int32)
    grad_slots = jnp.zeros((MICRO, SEQ, model_width), jnp.float32)
    gain_acc = None
    ffn_acc = None
    mixer_acc = None
    for tick_index in range(MICRO + 1):
        kept_index = MICRO - tick_index
        last_slot = max(MICRO - 1 - tick_index, 0)
        grad_out = jnp.where(section_id == 1, seq_cot[last_slot], returned).astype(jnp.float32)
        live_flag = jnp.where(
            section_id == 1, float(tick_index < MICRO), float(tick_index >= 1)
        ).astype(jnp.float32)
        grad_in, section_grads, mixer_grads = block_backward(
            inputs_kept[kept_index], grad_out, section_id, mixers, ffn_parts, gain_pair
        )
        gain_term = live_flag * section_grads[0]
        gain_acc = gain_term if gain_acc is None else gain_acc + gain_term
        ffn_terms = (
            live_flag * section_grads[1],
            live_flag * section_grads[2],
            live_flag * section_grads[3],
        )
        ffn_acc = ffn_terms if ffn_acc is None else add_trees(ffn_acc, ffn_terms)
        mixer_terms = jax.tree.map(lambda grad_part: live_flag * grad_part, mixer_grads)
        mixer_acc = mixer_terms if mixer_acc is None else add_trees(mixer_acc, mixer_terms)
        if tick_index >= 1:
            slot_mb = plan[MICRO - tick_index]
            grad_slots = (
                grad_slots
                + (slot_ids == slot_mb).astype(jnp.float32)[:, None, None] * grad_in[None]
            )
        if tick_index < MICRO:
            returned = from_behind(grad_in.astype(jnp.bfloat16), "section", -1)
    shards = (
        lax.psum_scatter(
            ffn_acc[0].astype(jnp.bfloat16), "dp", scatter_dimension=0, tiled=True
        ).astype(jnp.float32),
        lax.psum_scatter(
            ffn_acc[1].astype(jnp.bfloat16), "dp", scatter_dimension=0, tiled=True
        ).astype(jnp.float32),
        lax.psum_scatter(
            ffn_acc[2].astype(jnp.bfloat16), "dp", scatter_dimension=1, tiled=True
        ).astype(jnp.float32),
    )
    ffn_full = (
        lax.all_gather(shards[0].astype(jnp.bfloat16), "dp", axis=0, tiled=True).astype(
            jnp.float32
        ),
        lax.all_gather(shards[1].astype(jnp.bfloat16), "dp", axis=0, tiled=True).astype(
            jnp.float32
        ),
        lax.all_gather(shards[2].astype(jnp.bfloat16), "dp", axis=1, tiled=True).astype(
            jnp.float32
        ),
    )
    mixer_half = (
        lax.psum_scatter(
            mixer_acc[0].astype(jnp.bfloat16), "section", scatter_dimension=0, tiled=True
        ).astype(jnp.float32),
        lax.psum_scatter(
            mixer_acc[1].astype(jnp.bfloat16), "section", scatter_dimension=0, tiled=True
        ).astype(jnp.float32),
        lax.psum_scatter(
            mixer_acc[2].astype(jnp.bfloat16), "section", scatter_dimension=0, tiled=True
        ).astype(jnp.float32),
        lax.psum_scatter(
            mixer_acc[3].astype(jnp.bfloat16), "section", scatter_dimension=0, tiled=True
        ).astype(jnp.float32),
        lax.psum_scatter(
            mixer_acc[4].astype(jnp.bfloat16), "section", scatter_dimension=1, tiled=True
        ).astype(jnp.float32),
        lax.psum_scatter(
            mixer_acc[5].astype(jnp.bfloat16), "section", scatter_dimension=0, tiled=True
        ).astype(jnp.float32),
        lax.psum_scatter(
            mixer_acc[6].astype(jnp.bfloat16), "section", scatter_dimension=0, tiled=True
        ).astype(jnp.float32),
        lax.psum_scatter(
            mixer_acc[7].astype(jnp.bfloat16), "section", scatter_dimension=1, tiled=True
        ).astype(jnp.float32),
    )
    summed = (
        lax.psum(gain_acc.astype(jnp.bfloat16), "dp").astype(jnp.float32),
        lax.psum(mixer_half[0].astype(jnp.bfloat16), "dp").astype(jnp.float32),
        lax.psum(mixer_half[1].astype(jnp.bfloat16), "dp").astype(jnp.float32),
        lax.psum(mixer_half[2].astype(jnp.bfloat16), "dp").astype(jnp.float32),
        lax.psum(mixer_half[3].astype(jnp.bfloat16), "dp").astype(jnp.float32),
        lax.psum(mixer_half[4].astype(jnp.bfloat16), "dp").astype(jnp.float32),
        lax.psum(mixer_half[5].astype(jnp.bfloat16), "dp").astype(jnp.float32),
        lax.psum(mixer_half[6].astype(jnp.bfloat16), "dp").astype(jnp.float32),
        lax.psum(mixer_half[7].astype(jnp.bfloat16), "dp").astype(jnp.float32),
    )
    boundary = jnp.where(section_id == 0, grad_slots, jnp.stack(finished)).reshape(
        1, MICRO * SEQ, model_width
    )
    return (
        boundary,
        summed[0][None],
        ffn_full[0][None],
        ffn_full[1][None],
        ffn_full[2][None],
        summed[1],
        summed[2],
        summed[3],
        summed[4],
        summed[5],
        summed[6],
        summed[7],
        summed[8],
    )


def solution(mesh):
    placed = (
        P("dp", None),
        P("dp", None),
        P("dp", None),
        P("section", None, None),
        P("section", None, "tensor"),
        P("section", None, "tensor"),
        P("section", "tensor", None),
        P("section", None, "tensor"),
        P("section", None, "tensor"),
        P("section", "tensor"),
        P("section", "tensor"),
        P("tensor", "section"),
        P("section", "tensor"),
        P("section", None),
        P("tensor", "section"),
    )
    return jax.shard_map(
        per_device,
        mesh=mesh,
        in_specs=placed,
        out_specs=(
            P("section", "dp", None),
            P("section", None, None),
            P("section", None, "tensor"),
            P("section", None, "tensor"),
            P("section", "tensor", None),
            P("section", None, "tensor"),
            P("section", None, "tensor"),
            P("section", "tensor"),
            P("section", "tensor"),
            P("tensor", "section"),
            P("section", "tensor"),
            P("section", None),
            P("tensor", "section"),
        ),
        check_vma=False,
    )
```

profile of v0, /device:TPU:1, one launch (start us, length us, event | category | flops | bytes accessed | tf_op | source)
XLA Modules:
  0.0 2730.5 jit_solution(7972687639087534241)
XLA Ops:
  29.7 10.6 all-gather.12.cloned.1.call-done
  40.3 15.5 all-gather.16.cloned.1.call-done
  55.8 17.7 all-gather.14.cloned.1.call-done
  73.5 14.6 conditional.9
  88.2 23.1 conditional.15
  111.4 261.9 %all-reduce.367.cloned.1.call-done = (bf16[128,1536]{1,0:T(8,128)(2,1)}, bf16[128,1536]{1,0:T(8,128)(2,1)}) async-done(((bf16[128,1536]{1,0:T(8,128)(2,1)}, bf16[128,1536]{1,0:T(8,128)(2,1)}), (bf16[128,1536]{1,0:T(8,128)(2,1)}, bf16[128,1536]{1,0:T(8,128)(2,1)})) %all-reduce.367.cloned.1.call-update) | async-done | bytes 786448 | tf_op jit(solution)/shard_map/psum | solution.py:219
  378.7 5.5 fusion.563
  385.5 41.6 %all-reduce.345.cloned.1.call-done = bf16[128,1536]{1,0:T(8,128)(2,1)} async-done(((bf16[128,1536]{1,0:T(8,128)(2,1)}), bf16[128,1536]{1,0:T(8,128)(2,1)}) %all-reduce.345.cloned.1.call-update) | async-done | bytes 393232 | tf_op jit(solution)/shard_map/psum | solution.py:219
  439.0 15.0 conditional.10
  454.1 22.9 conditional.13
  477.2 263.3 %all-reduce.365.cloned.1.call-done = (bf16[128,1536]{1,0:T(8,128)(2,1)}, bf16[128,1536]{1,0:T(8,128)(2,1)}) async-done(((bf16[128,1536]{1,0:T(8,128)(2,1)}, bf16[128,1536]{1,0:T(8,128)(2,1)}), (bf16[128,1536]{1,0:T(8,128)(2,1)}, bf16[128,1536]{1,0:T(8,128)(2,1)})) %all-reduce.365.cloned.1.call-update) | async-done | bytes 786448 | tf_op jit(solution)/shard_map/psum | solution.py:219
  745.9 5.5 fusion.566
  752.7 41.6 %all-reduce.347.cloned.1.call-done = bf16[128,1536]{1,0:T(8,128)(2,1)} async-done(((bf16[128,1536]{1,0:T(8,128)(2,1)}), bf16[128,1536]{1,0:T(8,128)(2,1)}) %all-reduce.347.cloned.1.call-update) | async-done | bytes 393232 | tf_op jit(solution)/shard_map/psum | solution.py:219
  803.5 22.5 conditional.11
  830.5 145.5 %all-reduce.349.cloned.1.call-done = bf16[128,1536]{1,0:T(8,128)(2,1)} async-done(((bf16[128,1536]{1,0:T(8,128)(2,1)}), bf16[128,1536]{1,0:T(8,128)(2,1)}) %all-reduce.349.cloned.1.call-update) | async-done | bytes 393232 | tf_op jit(solution)/shard_map/psum | solution.py:219
  988.5 14.7 conditional.17
  1003.1 28.3 %all-reduce.351.cloned.1.call-done = bf16[128,1536]{1,0:T(8,128)(2,1)} async-done(((bf16[128,1536]{1,0:T(8,128)(2,1)}), bf16[128,1536]{1,0:T(8,128)(2,1)}) %all-reduce.351.cloned.1.call-update) | async-done | bytes 393232 | tf_op jit(solution)/shard_map/psum | solution.py:256
  1037.3 36.8 %conditional.12 = (bf16[128,1536]{1,0:T(8,128)(2,1)}, bf16[128,256]{1,0:T(8,128)(2,1)}, f32[4,512]{1,0:T(4,128)}, f32[4,512]{1,0:T(4,128)}, f32[512,1536]{1,0:T(...) conditional(s32[]{:T(128)} %convert_element_type.621, ...), branch_computations={%region_25.27_spmd, %region_27.36_spmd} | conditional | flops 1286714368 | bytes 103250744 | solution.py:260
  1074.1 6.2 all-reduce.353.cloned.1.call-start
  1080.3 383.2 %all-reduce.363.cloned.1.call-done = (bf16[128,1536]{1,0:T(8,128)(2,1)}, bf16[128,256]{1,0:T(8,128)(2,1)}, bf16[128,1536]{1,0:T(8,128)(2,1)}) async-done(((bf16[128,1536]{1,0:T(8,128)(2,1)}, bf16[128,256]{1,0:T(8,128)(2,1)}, bf16[128,1536]{1,0:T(8,128)(2,1)}), (bf16[128,1536]{1,0:T(8,128)(2,1)}, bf16[128,256]{1,0:T(8,128)(2,1)}, bf16[128,1536]{1,0:T(8,128)(2,1)})) %all-reduce.363.cloned.1.call-update) | async-done | bytes 851984 | tf_op jit(solution)/shard_map/psum | solution.py:219
  1480.6 40.6 %all-reduce.353.cloned.1.call-done = bf16[128,1536]{1,0:T(8,128)(2,1)} async-done(((bf16[128,1536]{1,0:T(8,128)(2,1)}), bf16[128,1536]{1,0:T(8,128)(2,1)}) %all-reduce.353.cloned.1.call-update) | async-done | bytes 393232 | tf_op jit(solution)/shard_map/psum | solution.py:256
  1527.1 36.7 %conditional.14 = (bf16[128,1536]{1,0:T(8,128)(2,1)}, bf16[128,256]{1,0:T(8,128)(2,1)}, f32[4,512]{1,0:T(4,128)}, f32[4,512]{1,0:T(4,128)}, f32[512,1536]{1,0:T(...) conditional(s32[]{:T(128)} %convert_element_type.621, ...), branch_computations={%region_47.49_spmd, %region_49.58_spmd} | conditional | flops 1286714368 | bytes 103250744 | solution.py:260
  1563.8 7.6 all-reduce.355.cloned.1.call-start
  1575.6 292.9 %all-reduce.361.cloned.1.call-done = (bf16[128,256]{1,0:T(8,128)(2,1)}, bf16[128,1536]{1,0:T(8,128)(2,1)}) async-done(((bf16[128,256]{1,0:T(8,128)(2,1)}, bf16[128,1536]{1,0:T(8,128)(2,1)}), (bf16[128,256]{1,0:T(8,128)(2,1)}, bf16[128,1536]{1,0:T(8,128)(2,1)})) %all-reduce.361.cloned.1.call-update) | async-done | bytes 458768 | tf_op jit(solution)/shard_map/psum | solution.py:272
  1887.4 5.6 fusion.569
  1893.0 34.6 %all-reduce.355.cloned.1.call-done = bf16[128,1536]{1,0:T(8,128)(2,1)} async-done(((bf16[128,1536]{1,0:T(8,128)(2,1)}), bf16[128,1536]{1,0:T(8,128)(2,1)}) %all-reduce.355.cloned.1.call-update) | async-done | bytes 393232 | tf_op jit(solution)/shard_map/psum | solution.py:256
  1933.0 18.8 conditional.16
  1951.8 8.4 all-reduce.369.cloned.1.call-start
  1962.7 10.5 add_convert_fusion
  1986.7 134.0 %all-reduce.359.cloned.1.call-done = (bf16[128,1536]{1,0:T(8,128)(2,1)}, bf16[128,256]{1,0:T(8,128)(2,1)}, bf16[128,1536]{1,0:T(8,128)(2,1)}) async-done(((bf16[128,1536]{1,0:T(8,128)(2,1)}, bf16[128,256]{1,0:T(8,128)(2,1)}, bf16[128,1536]{1,0:T(8,128)(2,1)}), (bf16[128,1536]{1,0:T(8,128)(2,1)}, bf16[128,256]{1,0:T(8,128)(2,1)}, bf16[128,1536]{1,0:T(8,128)(2,1)})) %all-reduce.359.cloned.1.call-update) | async-done | bytes 851984 | tf_op jit(solution)/shard_map/psum | solution.py:219
  2123.5 5.2 add_convert_fusion.1
  2161.3 10.2 reduce-scatter.16.cloned.1.call-done
  2171.6 15.6 reduce-scatter.20.cloned.1.call-done
  2187.2 14.7 reduce-scatter.18.cloned.1.call-done
  2201.9 16.0 reduce-scatter.14.cloned.1.call-done
  2217.9 79.4 %reduce-scatter.12.cloned.1.call-done = bf16[1152,96]{0,1:T(8,128)(2,1)} async-done(((bf16[1152,1536]{0,1:T(8,128)(2,1)}), bf16[1152,96]{0,1:T(8,128)(2,1)}) %reduce-scatter.12.cloned.1.call-update) | async-done | bytes 221200 | tf_op jit(solution)/shard_map/reduce_scatter | solution.py:375
  2297.4 79.4 %reduce-scatter.8.cloned.1.call-done = bf16[96,1152]{1,0:T(8,128)(2,1)} async-done(((bf16[1536,1152]{1,0:T(8,128)(2,1)}), bf16[96,1152]{1,0:T(8,128)(2,1)}) %reduce-scatter.8.cloned.1.call-update) | async-done | bytes 221200 | tf_op jit(solution)/shard_map/reduce_scatter | solution.py:369
  2378.0 78.5 %reduce-scatter.10.cloned.1.call-done = bf16[96,1152]{1,0:T(8,128)(2,1)} async-done(((bf16[1536,1152]{1,0:T(8,128)(2,1)}), bf16[96,1152]{1,0:T(8,128)(2,1)}) %reduce-scatter.10.cloned.1.call-update) | async-done | bytes 221200 | tf_op jit(solution)/shard_map/reduce_scatter | solution.py:372
  2467.7 5.2 all-reduce.329
  2480.0 58.9 %all-reduce.322 = (bf16[1,2,1536]{2,1,0:T(2,128)(2,1)}, bf16[2,512]{1,0:T(2,128)(2,1)}, bf16[2,512]{1,0:T(2,128)(2,1)}) all-reduce(bf16[1,2,1536]{2,1,0:T(2,128)(2,1)} %fusion.680, bf16[2,512]{1,0:T(2,128)(2,1)} %constant_dynamic-slice_fusion.1, ...), channel_id=1, replica_groups=mesh['section'=2,'tensor'=4,'dp'=16] {'dp'}, use_global_device_ids=true, to_apply=%region_96.97 | all-reduce | flops 5120 | bytes 20480 | tf_op jit(solution)/shard_map/psum | solution.py:417
  2547.6 18.3 all-reduce.357.cloned.1.call-done
  2575.4 41.6 %all-gather.22.cloned.1.call-done = bf16[1152,1536]{0,1:T(8,128)(2,1)} async-done(((bf16[1152,96]{0,1:T(8,128)(2,1)}), bf16[1152,1536]{0,1:T(8,128)(2,1)}) %all-gather.22.cloned.1.call-update) | async-done | bytes 3538960 | tf_op jit(solution)/shard_map/all_gather | solution.py:386
  2617.0 5.4 bitcast_convert_fusion
  2622.4 8.0 copy.369
  2630.5 37.0 %all-gather.18.cloned.1.call-done = bf16[1536,1152]{1,0:T(8,128)(2,1)} async-done(((bf16[96,1152]{1,0:T(8,128)(2,1)}), bf16[1536,1152]{1,0:T(8,128)(2,1)}) %all-gather.18.cloned.1.call-update) | async-done | bytes 3538960 | tf_op jit(solution)/shard_map/all_gather | solution.py:380
  2667.4 5.6 bitcast_convert_fusion.2
  2673.0 44.8 %all-gather.20.cloned.1.call-done = bf16[1536,1152]{1,0:T(8,128)(2,1)} async-done(((bf16[96,1152]{1,0:T(8,128)(2,1)}), bf16[1536,1152]{1,0:T(8,128)(2,1)}) %all-gather.20.cloned.1.call-update) | async-done | bytes 3538960 | tf_op jit(solution)/shard_map/all_gather | solution.py:383
  2717.8 5.4 bitcast_convert_fusion.1
  (505 shorter events, 417.1 us)
Async XLA Ops:
  7.2 368.7 %copy-start = (bf16[1,1536,1152]{2,1,0:T(8,128)(2,1)S(1)}, bf16[1,1536,1152]{2,1,0:T(8,128)(2,1)}, u32[]{:S(2)}) copy-start(bf16[1,1536,1152]{2,1,0:T(8,128)(2,1)} %param.37) | copy-start | bytes 10616836
  7.2 22.5 all-gather.10.cloned.1.call-start
  8.0 32.3 %all-gather.12.cloned.1.call-start = ((), (), s32[]{:S(2)}) async-start(), calls=%async_computation.8 | async-start | bytes 1769472 | tf_op jit(solution)/shard_map/all_gather | solution.py:311
  8.7 47.1 %all-gather.16.cloned.1.call-start = ((), (), s32[]{:S(2)}) async-start(), calls=%async_computation.10 | async-start | bytes 2359296 | tf_op jit(solution)/shard_map/all_gather | solution.py:308
  9.4 64.1 %all-gather.14.cloned.1.call-start = ((), (), s32[]{:S(2)}) async-start(), calls=%async_computation.9 | async-start | bytes 4718592 | tf_op jit(solution)/shard_map/all_gather | solution.py:304
  10.0 363.2 %all-reduce.367.cloned.1.call-start = ((), (), s32[]{:S(2)}) async-start(), calls=%async_computation.32 | async-start | bytes 1572864 | tf_op jit(solution)/shard_map/psum | solution.py:219
  111.3 315.8 %all-reduce.345.cloned.1.call-start = ((), (), s32[]{:S(2)}) async-start(), calls=%async_computation.11 | async-start | bytes 786432 | tf_op jit(solution)/shard_map/psum | solution.py:219
  384.2 356.4 %all-reduce.365.cloned.1.call-start = ((), (), s32[]{:S(2)}) async-start(), calls=%async_computation.31 | async-start | bytes 1572864 | tf_op jit(solution)/shard_map/psum | solution.py:219
  429.6 5.6 collective-permute-start
  477.0 317.2 %all-reduce.347.cloned.1.call-start = ((), (), s32[]{:S(2)}) async-start(), calls=%async_computation.12 | async-start | bytes 786432 | tf_op jit(solution)/shard_map/psum | solution.py:219
  751.5 224.5 %all-reduce.349.cloned.1.call-start = ((), (), s32[]{:S(2)}) async-start(), calls=%async_computation.13 | async-start | bytes 786432 | tf_op jit(solution)/shard_map/psum | solution.py:219
  794.3 9.3 copy-start.7
  797.0 5.3 collective-permute-start.1
  826.1 205.4 %all-reduce.351.cloned.1.call-start = ((), (), s32[]{:S(2)}) async-start(), calls=%async_computation.14 | async-start | bytes 786432 | tf_op jit(solution)/shard_map/psum | solution.py:256
  988.4 475.1 %all-reduce.363.cloned.1.call-start = ((), (), s32[]{:S(2)}) async-start(), calls=%async_computation.30 | async-start | bytes 1703936 | tf_op jit(solution)/shard_map/psum | solution.py:219
  1074.1 447.2 %all-reduce.353.cloned.1.call-start = ((), (), s32[]{:S(2)}) async-start(), calls=%async_computation.15 | async-start | bytes 786432 | tf_op jit(solution)/shard_map/psum | solution.py:256
  1463.5 9.2 copy-start.36
  1468.4 5.7 collective-permute-start.2
  1480.6 387.9 %all-reduce.361.cloned.1.call-start = ((), (), s32[]{:S(2)}) async-start(), calls=%async_computation.29 | async-start | bytes 917504 | tf_op jit(solution)/shard_map/psum | solution.py:272
  1563.8 363.8 %all-reduce.355.cloned.1.call-start = ((), (), s32[]{:S(2)}) async-start(), calls=%async_computation.16 | async-start | bytes 786432 | tf_op jit(solution)/shard_map/psum | solution.py:256
  1868.5 10.9 copy-start.227
  1868.5 10.9 copy-start.19
  1868.5 10.9 copy-start.79
  1874.6 6.5 collective-permute-start.3
  1887.4 233.4 %all-reduce.359.cloned.1.call-start = ((), (), s32[]{:S(2)}) async-start(), calls=%async_computation.28 | async-start | bytes 1703936 | tf_op jit(solution)/shard_map/psum | solution.py:219
  1887.4 45.6 %copy-start.13 = (bf16[128,1536]{1,0:T(8,128)(2,1)S(1)}, bf16[128,1536]{1,0:T(8,128)(2,1)}, u32[]{:S(2)}) copy-start(bf16[128,1536]{1,0:T(8,128)(2,1)} %fusion.600) | copy-start | bytes 1179652
  1893.0 40.0 %copy-start.6 = (bf16[1536,2,512]{2,1,0:T(2,128)(2,1)S(1)}, bf16[1536,2,512]{2,1,0:T(2,128)(2,1)}, u32[]{:S(2)}) copy-start(bf16[1536,2,512]{2,1,0:T(2,128)(2,1)} %all-gather.14.cloned.1.call-done) | copy-start | bytes 9437188
  1951.8 204.2 %all-reduce.369.cloned.1.call-start = ((), (), s32[]{:S(2)}) async-start(), calls=%async_computation.33 | async-start | bytes 6815744
  1973.2 198.4 %reduce-scatter.16.cloned.1.call-start = ((), (), s32[]{:S(2)}) async-start(), calls=%async_computation.24 | async-start | bytes 1769472 | tf_op jit(solution)/shard_map/reduce_scatter | solution.py:406
  1977.8 209.4 %reduce-scatter.20.cloned.1.call-start = ((), (), s32[]{:S(2)}) async-start(), calls=%async_computation.26 | async-start | bytes 1769472 | tf_op jit(solution)/shard_map/reduce_scatter | solution.py:412
  1982.8 219.1 %reduce-scatter.18.cloned.1.call-start = ((), (), s32[]{:S(2)}) async-start(), calls=%async_computation.25 | async-start | bytes 1179648 | tf_op jit(solution)/shard_map/reduce_scatter | solution.py:409
  2123.5 94.3 %reduce-scatter.14.cloned.1.call-start = ((), (), s32[]{:S(2)}) async-start(), calls=%async_computation.23 | async-start | bytes 2359296 | tf_op jit(solution)/shard_map/reduce_scatter | solution.py:403
  2128.7 168.6 %reduce-scatter.12.cloned.1.call-start = ((), (), s32[]{:S(2)}) async-start(), calls=%async_computation.21 | async-start | bytes 3760128 | tf_op jit(solution)/shard_map/reduce_scatter | solution.py:375
  2136.4 240.4 %reduce-scatter.8.cloned.1.call-start = ((), (), s32[]{:S(2)}) async-start(), calls=%async_computation.17 | async-start | bytes 3760128 | tf_op jit(solution)/shard_map/reduce_scatter | solution.py:369
  2142.8 313.8 %reduce-scatter.10.cloned.1.call-start = ((), (), s32[]{:S(2)}) async-start(), calls=%async_computation.19 | async-start | bytes 3760128 | tf_op jit(solution)/shard_map/reduce_scatter | solution.py:372
  2148.9 417.0 %all-reduce.357.cloned.1.call-start = ((), (), s32[]{:S(2)}) async-start(), calls=%async_computation.27 | async-start | bytes 8126464 | tf_op jit(solution)/shard_map/psum | solution.py:418
  2161.3 314.2 %copy-start.12 = (bf16[1536,256]{1,0:T(8,128)(2,1)S(1)}, bf16[1536,256]{1,0:T(8,128)(2,1)}, u32[]{:S(2)}) copy-start(bf16[1536,256]{1,0:T(8,128)(2,1)} %all_gather.33) | copy-start | bytes 2359300
  2161.3 314.2 %copy-start.23 = (bf16[256,1536]{1,0:T(8,128)(2,1)S(1)}, bf16[256,1536]{1,0:T(8,128)(2,1)}, u32[]{:S(2)}) copy-start(bf16[256,1536]{1,0:T(8,128)(2,1)} %param.33) | copy-start | bytes 2359300
  2161.3 314.2 %copy-start.125 = (f32[1536]{0:T(1024)S(1)}, f32[1536]{0:T(1024)}, u32[]{:S(2)}) copy-start(f32[1536]{0:T(1024)} %copy-done.123) | copy-start | bytes 18436
  2217.8 325.6 %copy-start.20 = (bf16[128,1536]{1,0:T(8,128)(2,1)S(1)}, bf16[128,1536]{1,0:T(8,128)(2,1)}, u32[]{:S(2)}) copy-start(bf16[128,1536]{1,0:T(8,128)(2,1)} %copy-done.17) | copy-start | bytes 1179652
  2217.8 325.6 %copy-start.80 = (bf16[128,1536]{1,0:T(8,128)(2,1)S(1)}, bf16[128,1536]{1,0:T(8,128)(2,1)}, u32[]{:S(2)}) copy-start(bf16[128,1536]{1,0:T(8,128)(2,1)} %get-tuple-element.880) | copy-start | bytes 1179652
  2217.9 326.8 %copy-start.62 = (f32[1,128,1536]{2,1,0:T(8,128)S(1)}, f32[1,128,1536]{2,1,0:T(8,128)}, u32[]{:S(2)}) copy-start(f32[1,128,1536]{2,1,0:T(8,128)} %get-tuple-element.1362) | copy-start | bytes 2359300
  2217.9 399.1 %all-gather.22.cloned.1.call-start = ((), (), s32[]{:S(2)}) async-start(), calls=%async_computation.22 | async-start | bytes 3760128 | tf_op jit(solution)/shard_map/all_gather | solution.py:386
  2297.3 370.1 %all-gather.18.cloned.1.call-start = ((), (), s32[]{:S(2)}) async-start(), calls=%async_computation.18 | async-start | bytes 3760128 | tf_op jit(solution)/shard_map/all_gather | solution.py:380
  2376.8 341.0 %all-gather.20.cloned.1.call-start = ((), (), s32[]{:S(2)}) async-start(), calls=%async_computation.20 | async-start | bytes 3760128 | tf_op jit(solution)/shard_map/all_gather | solution.py:383
  2478.5 66.3 %copy-start.34 = (bf16[128,1536]{1,0:T(8,128)(2,1)S(1)}, bf16[128,1536]{1,0:T(8,128)(2,1)}, u32[]{:S(2)}) copy-start(bf16[128,1536]{1,0:T(8,128)(2,1)} %get-tuple-element.886) | copy-start | bytes 1179652
  2478.5 66.3 %copy-start.55 = (bf16[128,1536]{1,0:T(8,128)(2,1)S(1)}, bf16[128,1536]{1,0:T(8,128)(2,1)}, u32[]{:S(2)}) copy-start(bf16[128,1536]{1,0:T(8,128)(2,1)} %all-reduce.355.cloned.1.call-done) | copy-start | bytes 1179652
  2667.4 55.8 %copy-start.1 = (bf16[1,1536,1152]{2,1,0:T(8,128)(2,1)S(1)}, bf16[1,1536,1152]{2,1,0:T(8,128)(2,1)}, u32[]{:S(2)}) copy-start(bf16[1,1536,1152]{2,1,0:T(8,128)(2,1)} %param.37) | copy-start | bytes 10616836
  (87 other events, 235.9 us)
Sparse Core Ops, SparseCore 0:
  9.7 15.5 all-gather.9
  27.0 13.2 all-gather.11
  41.9 13.8 all-gather.15
  57.3 16.1 all-gather.13
  111.5 261.7 all-reduce.366
  384.3 42.7 all-reduce.344
  477.1 263.3 all-reduce.364
  751.6 42.6 all-reduce.346
  826.2 149.7 all-reduce.348
  988.5 42.8 all-reduce.350
  1074.2 389.2 all-reduce.362
  1480.7 40.5 all-reduce.352
  1564.0 304.4 all-reduce.360
  1887.5 40.1 all-reduce.354
  1952.0 168.7 all-reduce.358
  2123.8 32.1 all-reduce.368
  2158.8 12.6 reduce-scatter.15
  2174.5 12.6 reduce-scatter.19
  2189.5 12.2 reduce-scatter.17
  2204.8 13.0 reduce-scatter.13
  2221.8 75.4 reduce-scatter.11
  2301.3 75.5 reduce-scatter.7
  2380.8 75.7 reduce-scatter.9
  2461.6 104.2 all-reduce.356
  2568.3 48.6 all-gather.21
  2619.2 48.1 all-gather.17
  2669.6 48.1 all-gather.19
where the time goes:
time: 2780 us; the launch traced here: 2730 us
  waiting for transfers between devices  2160 us (78%)
  matrix products  196 us (7%)
  local copies, waits for them, and re-layouts  119 us (4%)
  other arithmetic  119 us (4%)
  blocking collectives  76.6 us (3%)
  starting transfers between devices  35.4 us (1%)
    psum x7, waiting for transfers between devices, tensor_total(): lax.psum(partial_value.astype(jnp.bfloat16), 'tensor').astype(jnp.float32)  1270 us
    psum x1, waiting for transfers between devices, block_backward(): lax.psum(part_kv.astype(jnp.bfloat16), 'tensor').astype(jnp.float32)  293 us
    psum x3, waiting for transfers between devices, block_backward(): lax.psum(part_second.astype(jnp.bfloat16), 'tensor').astype(jnp.float32)  104 us
    reduce_scatter x1, waiting for transfers between devices, per_device(): lax.psum_scatter(ffn_acc[0].astype(jnp.bfloat16), 'dp', scatter_dimension...  79.4 us
    reduce_scatter x1, waiting for transfers between devices, per_device(): lax.psum_scatter(ffn_acc[2].astype(jnp.bfloat16), 'dp', scatter_dimension...  79.4 us
    reduce_scatter x1, waiting for transfers between devices, per_device(): lax.psum_scatter(ffn_acc[1].astype(jnp.bfloat16), 'dp', scatter_dimension...  78.5 us
    dot_general x30, matrix products, dot_plain(): return jnp.dot(left, right, preferred_element_type=jnp.float32)  75.7 us
    another operation x45, local copies, waits for them, and re-layouts  64.1 us
  transfers between devices with their start and end apart: 31, of which 28 were waited for; matrix products, arithmetic and copies ran while one was open for 6% of the time, Pallas kernels for 0%

commit v1 on v0

v1 whole, which is shorter than its diff:
```python
import jax
import jax.numpy as jnp
from jax import lax
from jax.experimental import pallas as pl
from jax.experimental.pallas import tpu as pltpu
from jax.sharding import PartitionSpec as P

HD = 128
SEQ = 128
NORM_EPS = 1e-06
RATE_FLOOR = 0.01
BF = jnp.bfloat16
F32 = jnp.float32
MESH = pl.DeviceIdType.MESH
NT = (((1,), (1,)), ((), ()))

D = 1536
FQ = 1152
RQ = 512
AQ = 384
SH = 32
CR = 144
CC = 384
RR = 64
HALF_A = 80
N_ITEMS = 8
ITEM_ATT = 6
ITEM_REC = 7


def mm(left, right):
    return jnp.dot(left, right, preferred_element_type=F32)


def mm_nt(left, right):
    return lax.dot_general(left, right, NT, preferred_element_type=F32)


def rms(values, gain):
    return values * lax.rsqrt(jnp.mean(values * values, -1, keepdims=True) + NORM_EPS) * gain


def rms_back(values, gain, dn):
    r = lax.rsqrt(jnp.mean(values * values, -1, keepdims=True) + NORM_EPS)
    dng = dn * gain
    dv = r * (dng - values * (r * r) * jnp.mean(dng * values, -1, keepdims=True))
    return dv, jnp.sum(dn * values * r, 0, keepdims=True)


GC = 0.7978845608028654
GA = 0.044715


def gelu(x):
    return 0.5 * x * (1.0 + jnp.tanh(GC * (x + GA * x * x * x)))


def gelu_both(x):
    th = jnp.tanh(GC * (x + GA * x * x * x))
    value = 0.5 * x * (1.0 + th)
    slope = 0.5 * (1.0 + th) + 0.5 * x * (1.0 - th * th) * GC * (1.0 + 3.0 * GA * x * x)
    return value, slope


def sigmoid(x):
    return 1.0 / (1.0 + jnp.exp(-x))


def softplus(x):
    return jnp.maximum(x, 0.0) + jnp.log(1.0 + jnp.exp(-jnp.abs(x)))


def rows_back(values, rows, k):
    return jnp.where(rows >= k, pltpu.roll(values, k, 0), 0.0)


def rows_ahead(values, rows, k):
    return jnp.where(rows < SEQ - k, pltpu.roll(values, SEQ - k, 0), 0.0)


def blocks_kernel(
    x_ref, cot_ref, sm_in, win, wgt, wro, wg, wu, wd, wq, wkv, wao,
    y_o, dx_o, gp, gr,
    s_in, s_gt, s_ro, s_sm, s_g, s_u, s_d, s_q, s_kv, s_ao,
    ag, sb, rb, res, n1_s, uv_s, c_s, ig_s, rg_s, a_s, h_s, o_s,
    q_s, kv_s, p_s, at_s, gate_s, up_s, hid_s, dg_s, du_s, both_s,
    dkvb, gnb, stg, stg_r, yb, xb,
    wl_sem, ws_sem, wr_sem, ags_sem, agr_sem, rss_sem, rsr_sem,
    kvs_sem, kvr_sem, gns_sem, gnr_sem, st_sem, dl_sem, dls_sem, dlr_sem,
):
    s = lax.axis_index("section")
    t = lax.axis_index("tensor")
    d = lax.axis_index("dp")
    peers = [lax.rem(t + k, 4) for k in range(4)]
    mine = pl.ds(pl.multiple_of(t * SH, SH), SH)

    barrier = pltpu.get_barrier_semaphore()
    for k in range(4):
        if k:
            pl.semaphore_signal(barrier, inc=1, device_id=(s, peers[k], d), device_id_type=MESH)
        pl.semaphore_signal(barrier, inc=1, device_id=(1 - s, peers[k], d), device_id_type=MESH)

    half_in = pl.ds(pl.multiple_of(s * 768, 768), 768)
    half_gt = pl.ds(pl.multiple_of(s * 64, 64), 64)
    moves = [
        (win, s_in.at[half_in, :]),
        (sm_in, s_sm.at[s]),
        (wgt, s_gt.at[half_gt, :]),
        (wro, s_ro.at[s]),
        (wg.at[0], s_g.at[s]),
        (wu.at[0], s_u.at[s]),
        (wd.at[0], s_d.at[s]),
        (wq, s_q.at[half_in, :]),
        (wkv, s_kv.at[half_in, :]),
        (wao, s_ao.at[s]),
    ]
    local = [pltpu.make_async_copy(a, b, wl_sem.at[i]) for i, (a, b) in enumerate(moves)]
    swap = [
        pltpu.make_async_remote_copy(
            src_ref=a, dst_ref=b, send_sem=ws_sem.at[i], recv_sem=wr_sem.at[i],
            device_id=(1 - s, t, d), device_id_type=MESH,
        )
        for i, (a, b) in enumerate(moves)
    ]
    for copy in local:
        copy.start()
    pl.semaphore_wait(barrier, 7)
    for copy in swap:
        copy.start()

    def weights(*which):
        for i in which:
            local[i].wait()
            swap[i].wait_recv()

    def gather(p):
        return [
            pltpu.make_async_remote_copy(
                src_ref=ag.at[p, mine], dst_ref=ag.at[p, mine],
                send_sem=ags_sem.at[p, k], recv_sem=agr_sem.at[p, k],
                device_id=(s, peers[k], d), device_id_type=MESH,
            )
            for k in range(1, 4)
        ]

    def gather_start(p, shard):
        ag[p, mine, :] = shard.astype(BF)
        for copy in gather(p):
            copy.start()

    def gather_wait(p):
        for copy in gather(p):
            copy.wait()

    def scatter(p):
        return [
            pltpu.make_async_remote_copy(
                src_ref=sb.at[p, pl.ds(pl.multiple_of(peers[k] * SH, SH), SH)],
                dst_ref=rb.at[p, k - 1],
                send_sem=rss_sem.at[p, k], recv_sem=rsr_sem.at[p, k],
                device_id=(s, peers[k], d), device_id_type=MESH,
            )
            for k in range(1, 4)
        ]

    def scatter_start(p):
        for copy in scatter(p):
            copy.start()

    def scatter_wait(p):
        for copy in scatter(p):
            copy.wait()
        total = sb[p, mine, :].astype(F32)
        for k in range(3):
            total = total + rb[p, k].astype(F32)
        return total

    def deliver(shard, buf, out, core, which):
        buf[...] = shard.astype(BF)

        @pl.when(s == core)
        def _():
            own = pltpu.make_async_copy(buf, out.at[s, mine], dl_sem.at[which])
            own.start()
            for k in range(1, 4):
                deliver_copy(buf, out, core, which, k).start()
            own.wait()

        @pl.when(s != core)
        def _():
            for k in range(4):
                deliver_copy(buf, out, core, which, k).start()

    def deliver_copy(buf, out, core, which, k):
        return pltpu.make_async_remote_copy(
            src_ref=buf, dst_ref=out.at[s, mine],
            send_sem=dls_sem.at[which, k], recv_sem=dlr_sem.at[which, s, k],
            device_id=(core, peers[k], d), device_id_type=MESH,
        )

    def deliver_wait(buf, out, core, which):
        def landed(sender, k):
            pltpu.make_async_remote_copy(
                src_ref=buf, dst_ref=out.at[sender, mine],
                send_sem=dls_sem.at[which, k], recv_sem=dlr_sem.at[which, sender, k],
                device_id=(core, peers[k], d), device_id_type=MESH,
            ).wait_recv()

        @pl.when(s == core)
        def _():
            for k in range(1, 4):
                deliver_copy(buf, out, core, which, k).wait_send()
                landed(core, k)
            for k in range(4):
                landed(1 - core, k)

        @pl.when(s != core)
        def _():
            for k in range(4):
                deliver_copy(buf, out, core, which, k).wait_send()

    pending = [None, None]
    count = [0]

    def stage(item, half, fill):
        slot = count[0] % 2
        count[0] += 1
        if pending[slot] is not None:
            pending[slot].wait()
        fill(stg.at[slot])
        copy = pltpu.make_async_copy(stg.at[slot], gp.at[item, half], st_sem.at[slot])
        copy.start()
        pending[slot] = copy

    def gain(block, which):
        return s_sm[block, which : which + 1, :]

    rows = lax.broadcasted_iota(jnp.int32, (SEQ, RQ), 0)

    weights(0, 1)
    n1 = rms(x_ref[...].astype(F32), gain(0, 0)).astype(BF)
    n1_s[...] = n1
    uv_s[...] = mm(n1, s_in[...])
    taps = [s_sm[k // 2, 2 + k % 2 : 3 + k % 2, :RQ] for k in range(4)]
    vec = [s_sm[k // 2, 2 + k % 2 : 3 + k % 2, RQ : 2 * RQ] for k in range(4)]
    u = uv_s[:, :RQ]
    c = vec[0] + taps[0] * u
    for k in range(1, 4):
        c = c + taps[k] * rows_back(u, rows, k)
    c_s[...] = c
    weights(2, 3)
    for head in range(4):
        cols = slice(head * HD, head * HD + HD)
        cb = c_s[:, cols].astype(BF)
        ig_s[:, cols] = sigmoid(mm(cb, s_gt[:, cols]) + vec[1][:, cols])
        rg_s[:, cols] = sigmoid(
            mm(cb, s_gt[:, RQ + head * HD : RQ + head * HD + HD]) + vec[2][:, cols]
        )
    speed = softplus(vec[3])
    a = jnp.exp(-8.0 * rg_s[...] * speed)
    a_s[...] = a
    run = jnp.sqrt(jnp.maximum(1.0 - a * a, RATE_FLOOR)) * ig_s[...] * c_s[...]
    step = 1
    while step < SEQ:
        run = run + a * rows_back(run, rows, step)
        if 2 * step < SEQ:
            a = a * jnp.where(rows >= step, pltpu.roll(a, step, 0), 1.0)
        step *= 2
    h_s[...] = run
    o = (run * gelu(uv_s[:, RQ:])).astype(BF)
    o_s[...] = o
    for half in range(2):
        sb[0, :, half * 768 : half * 768 + 768] = mm(o, s_ro[half]).astype(BF)
    scatter_start(0)
    x_mine = x_ref[mine, :].astype(F32)
    x1 = x_mine + scatter_wait(0)
    res[0] = x1
    gather_start(0, rms(x1, gain(0, 1)))

    def ffn_forward(block, p_in, p_out):
        gather_wait(p_in)
        n2 = ag[p_in]
        for j in range(3):
            cols = slice(j * CC, j * CC + CC)
            gate = mm(n2, s_g[block, :, cols])
            up = mm(n2, s_u[block, :, cols])
            gate_s[block, :, cols] = gate
            up_s[block, :, cols] = up
            hid_s[block, :, cols] = (gelu(gate) * up).astype(BF)
        if block == 0:
            weights(6)
        hid = hid_s[block]
        for j in range(4):
            cols = slice(j * CC, j * CC + CC)
            sb[p_out, :, cols] = mm(hid, s_d[block, :, cols]).astype(BF)
        scatter_start(p_out)

    weights(4, 5)
    ffn_forward(0, 0, 1)
    mid = (res[0] + scatter_wait(1)).astype(BF).astype(F32)
    res[1] = mid
    gather_start(1, rms(mid, gain(1, 0)))

    weights(7, 8, 9)
    gather_wait(1)
    na = ag[1]
    q_s[...] = mm(na, s_q[...]).astype(BF)
    kv_s[...] = mm(na, s_kv[...]).astype(BF)
    keys = kv_s[:, :HD]
    vals = kv_s[:, HD:]
    allowed = lax.broadcasted_iota(jnp.int32, (SEQ, SEQ), 1) <= lax.broadcasted_iota(
        jnp.int32, (SEQ, SEQ), 0
    )
    for head in range(3):
        cols = slice(head * HD, head * HD + HD)
        score = jnp.where(allowed, mm_nt(q_s[:, cols], keys) * HD ** (-0.5), -1e30)
        expo = jnp.exp(score - jnp.max(score, -1, keepdims=True))
        p = expo / jnp.sum(expo, -1, keepdims=True)
        p_s[head] = p
        at_s[:, cols] = mm(p.astype(BF), vals).astype(BF)
    att = at_s[...]
    for half in range(2):
        sb[2, :, half * 768 : half * 768 + 768] = mm(att, s_ao[half]).astype(BF)
    scatter_start(2)
    x1 = res[1] + scatter_wait(2)
    res[2] = x1
    gather_start(2, rms(x1, gain(1, 1)))
    ffn_forward(1, 2, 3)
    y = res[2] + scatter_wait(3)
    deliver(y, yb, y_o, 1, 0)

    def ffn_backward(block, dF, p_n2, p_out):
        for j in range(3):
            cols = slice(j * CC, j * CC + CC)
            dhid = mm_nt(dF, s_d[block, cols, :])
            value, slope = gelu_both(gate_s[block, :, cols])
            dg_s[:, cols] = (dhid * up_s[block, :, cols] * slope).astype(BF)
            du_s[:, cols] = (dhid * value).astype(BF)
        dg = dg_s[...]
        du = du_s[...]
        for j in range(4):
            cols = slice(j * CC, j * CC + CC)
            sb[p_out, :, cols] = (
                mm_nt(dg, s_g[block, cols, :]) + mm_nt(du, s_u[block, cols, :])
            ).astype(BF)
        scatter_start(p_out)
        n2t = ag[p_n2].T
        for item, right in ((3 * block, dg_s), (3 * block + 1, du_s)):
            for half in range(2):

                def fill(ref, right=right, half=half):
                    for j in range(3):
                        part = mm(n2t[half * 768 : half * 768 + 768], right[:, j * CC : j * CC + CC])
                        ref[:, j * 48 : j * 48 + 48, :] = part.astype(BF).reshape(16, 48, CC)

                stage(item, half, fill)
        hidt = hid_s[block].T
        for half in range(2):

            def fill_down(ref, half=half):
                for j in range(4):
                    part = mm(hidt[half * 576 : half * 576 + 576], dF[:, j * CC : j * CC + CC])
                    part = part.astype(BF).reshape(4, CR, CC)
                    for i in range(4):
                        ref[i * 4 + j] = part[i]

            stage(3 * block + 2, half, fill_down)

    cot = cot_ref[...]
    ffn_backward(1, cot, 2, 4)
    dn = scatter_wait(4)
    dv, gg11 = rms_back(res[2], gain(1, 1), dn)
    dx1 = cot_ref[mine, :].astype(F32) + dv
    res[3] = dx1
    gather_start(3, dx1)

    gather_wait(3)
    dA = ag[3]
    datt_s = both_s.at[:, :AQ]
    dq_s = both_s.at[:, AQ : 2 * AQ]
    datt_s[...] = (mm_nt(dA[:, :768], s_ao[0]) + mm_nt(dA[:, 768:], s_ao[1])).astype(BF)
    dk = jnp.zeros((SEQ, HD), F32)
    dw = jnp.zeros((SEQ, HD), F32)
    for head in range(3):
        cols = slice(head * HD, head * HD + HD)
        p = p_s[head]
        datt = datt_s[:, cols]
        dpr = mm_nt(datt, kv_s[:, HD:])
        dw = dw + mm(p.astype(BF).T, datt)
        ds = (p * (dpr - jnp.sum(p * dpr, -1, keepdims=True)) * HD ** (-0.5)).astype(BF)
        dq_s[:, cols] = mm(ds, kv_s[:, :HD]).astype(BF)
        dk = dk + mm(ds.T, q_s[:, cols])
    dkvb[0, :, :HD] = dk.astype(BF)
    dkvb[0, :, HD:] = dw.astype(BF)
    kv_copies = [
        pltpu.make_async_remote_copy(
            src_ref=dkvb.at[0], dst_ref=dkvb.at[k], send_sem=kvs_sem.at[k], recv_sem=kvr_sem.at[k],
            device_id=(s, peers[k], d), device_id_type=MESH,
        )
        for k in range(1, 4)
    ]
    for copy in kv_copies:
        copy.start()
    dq = dq_s[...]
    for j in range(4):
        cols = slice(j * CC, j * CC + CC)
        sb[5, :, cols] = mm_nt(dq, s_q[cols, :]).astype(BF)
    scatter_start(5)
    for copy in kv_copies:
        copy.wait()
    total = dkvb[0].astype(F32)
    for k in range(1, 4):
        total = total + dkvb[k].astype(F32)
    dkv_s = both_s.at[:, 2 * AQ : 2 * AQ + 256]
    dkv_s[...] = total.astype(BF)
    nat = ag[1].T
    attt = at_s[...].T
    for half in range(2):

        def fill_att(ref, half=half):
            top = nat[half * 768 : half * 768 + 768]
            ref[:, :48, :] = mm(top, dq_s[...]).astype(BF).reshape(16, 48, CC)
            ref[:, 96:144, :256] = mm(top, dkv_s[...]).astype(BF).reshape(16, 48, 256)
            ref[:, 96:144, 256:] = jnp.zeros((16, 48, 128), BF)
            for j in range(2):
                at = half * 768 + j * CC
                part = mm(attt, dA[:, at : at + CC]).astype(BF).reshape(8, 48, CC)
                for i in range(8):
                    ref[i * 2 + j, 48:96, :] = part[i]

        stage(ITEM_ATT, half, fill_att)
    dn = scatter_wait(5) + mm_nt(dkv_s[mine, :], s_kv[...])
    dv, gg10 = rms_back(res[1], gain(1, 0), dn)
    dmid = res[3] + dv
    big_g = dmid.astype(BF).astype(F32)
    gather_start(4, big_g)
    res[3] = big_g
    gather_wait(4)
    ffn_backward(0, ag[4], 0, 6)
    dn = scatter_wait(6)
    dv, gg01 = rms_back(res[0], gain(0, 1), dn)
    dx1 = res[3] + dv
    res[3] = dx1
    gather_start(5, dx1)

    gather_wait(5)
    dA = ag[5]
    dO = mm_nt(dA[:, :768], s_ro[0]) + mm_nt(dA[:, 768:], s_ro[1])
    value, slope = gelu_both(uv_s[:, RQ:])
    h = h_s[...]
    both_s[:, RQ:] = (dO * h * slope).astype(BF)
    e = dO * value
    a = a_s[...]
    coef = rows_ahead(a, rows, 1)
    step = 1
    while step < SEQ:
        e = e + coef * rows_ahead(e, rows, step)
        if 2 * step < SEQ:
            coef = coef * rows_ahead(coef, rows, step)
        step *= 2
    ig = ig_s[...]
    rg = rg_s[...]
    c = c_s[...]
    room = 1.0 - a * a
    m = jnp.sqrt(jnp.maximum(room, RATE_FLOOR))
    ga = e * rows_back(h, rows, 1) - jnp.where(room > RATE_FLOOR, e * ig * c * a / m, 0.0)
    dl = ga * a
    gv3 = jnp.sum(dl * rg, 0, keepdims=True) * (-8.0) * sigmoid(vec[3])
    er = -8.0 * dl * speed * rg * (1.0 - rg)
    ei = e * m * c * ig * (1.0 - ig)
    gv1 = jnp.sum(ei, 0, keepdims=True)
    gv2 = jnp.sum(er, 0, keepdims=True)
    c_s[...] = e * m * ig
    ig_s[...] = ei
    rg_s[...] = er
    gts = []
    for head in range(4):
        cols = slice(head * HD, head * HD + HD)
        dpin = ig_s[:, cols].astype(BF)
        dprec = rg_s[:, cols].astype(BF)
        cbt = c[:, cols].astype(BF).T
        gts.append((mm(cbt, dpin), mm(cbt, dprec)))
        c_s[:, cols] += mm_nt(dpin, s_gt[:, cols]) + mm_nt(
            dprec, s_gt[:, RQ + head * HD : RQ + head * HD + HD]
        )
    dc = c_s[...]
    u = uv_s[:, :RQ]
    du = taps[0] * dc
    gtap = [jnp.sum(u * dc, 0, keepdims=True)]
    for k in range(1, 4):
        du = du + taps[k] * rows_ahead(dc, rows, k)
        gtap.append(jnp.sum(rows_back(u, rows, k) * dc, 0, keepdims=True))
    gv0 = jnp.sum(dc, 0, keepdims=True)
    both_s[:, :RQ] = du.astype(BF)
    both = both_s[...]
    for j in range(4):
        cols = slice(j * CC, j * CC + CC)
        sb[7, :, cols] = mm_nt(both, s_in[cols, :]).astype(BF)
    scatter_start(7)
    ot = o_s[...].T
    n1t = n1_s[...].T
    for half in range(2):
        for j in range(2):
            at = half * 768 + j * CC
            part = mm(ot, dA[:, at : at + CC]).astype(BF).reshape(8, RR, CC)
            for i in range(8):
                stg_r[half, i * 2 + j] = part[i]
        out_r = pltpu.make_async_copy(stg_r.at[half], gr.at[half], dl_sem.at[2 + half])
        out_r.start()

    dn = scatter_wait(7)
    dv, gg00 = rms_back(x_mine, gain(0, 0), dn)
    deliver(res[3] + dv, xb, dx_o, 0, 1)
    gnb[0, 0:1] = gg00
    gnb[0, 1:2] = gg01
    gnb[0, 2:3] = gg10
    gnb[0, 3:4] = gg11
    gnb[0, 4:8] = jnp.zeros((4, D), F32)
    gn_copies = [
        pltpu.make_async_remote_copy(
            src_ref=gnb.at[0], dst_ref=gnb.at[k], send_sem=gns_sem.at[k], recv_sem=gnr_sem.at[k],
            device_id=(s, peers[k], d), device_id_type=MESH,
        )
        for k in range(1, 4)
    ]
    for copy in gn_copies:
        copy.start()
    for copy in gn_copies:
        copy.wait()
    gains = gnb[0] + gnb[1] + gnb[2] + gnb[3]
    gvec = [gv0, gv1, gv2, gv3]
    for half in range(2):

        def fill_rec(ref, half=half):
            top = n1t[half * 768 : half * 768 + 768]
            for j, width in enumerate((CC, CC, 256)):
                part = mm(top, both_s[:, j * CC : j * CC + width])
                ref[:, j * 48 : j * 48 + 48, :width] = part.astype(BF).reshape(16, 48, width)
            for q in range(2):
                for head in range(4):
                    part = gts[head][q][half * 64 : half * 64 + 64].astype(BF)
                    for r in range(2):
                        ref[(q * 4 + head) * 2 + r, 96:128, 256:] = part[r * 32 : r * 32 + 32]
            ref[:, 128:144, 256:] = jnp.zeros((16, 16, HD), BF)
            blank = jnp.zeros((10, HD), F32)
            for i in range(12):
                lanes = slice(i * HD, i * HD + HD)
                pieces = [gains[2 * half : 2 * half + 2, lanes]]
                if i < 4:
                    pieces += [gtap[2 * half][:, lanes], gtap[2 * half + 1][:, lanes]]
                    pieces += [gvec[2 * half][:, lanes], gvec[2 * half + 1][:, lanes]]
                else:
                    pieces.append(jnp.zeros((4, HD), F32))
                ref[i, 128:144, 256:] = jnp.concatenate(pieces + [blank], 0).astype(BF)

        stage(ITEM_REC, half, fill_rec)
    for half in range(2):
        pltpu.make_async_copy(stg_r.at[half], gr.at[half], dl_sem.at[2 + half]).wait()
    for copy in pending:
        copy.wait()
    for copy in swap:
        copy.wait_send()
    deliver_wait(yb, y_o, 1, 0)
    deliver_wait(xb, dx_o, 0, 1)


def blocks_call(x, cot, small, weights):
    vm = pl.BlockSpec(memory_space=pltpu.VMEM)
    hbm = pl.BlockSpec(memory_space=pl.ANY)
    V = pltpu.VMEM
    dma = pltpu.SemaphoreType.DMA
    return pl.pallas_call(
        blocks_kernel,
        name="blocks",
        out_shape=[
            jax.ShapeDtypeStruct((2, SEQ, D), BF),
            jax.ShapeDtypeStruct((2, SEQ, D), BF),
            jax.ShapeDtypeStruct((N_ITEMS, 2, 16, CR, CC), BF),
            jax.ShapeDtypeStruct((2, 16, RR, CC), BF),
        ],
        in_specs=[vm, vm, hbm] + [hbm] * 9,
        out_specs=[hbm] * 4,
        scratch_shapes=[
            V((D, 2 * RQ), BF), V((HD, 2 * RQ), BF), V((2, RQ, 768), BF), V((2, 8, D), F32),
            V((2, D, FQ), BF), V((2, D, FQ), BF), V((2, FQ, D), BF),
            V((D, AQ), BF), V((D, 256), BF), V((2, AQ, 768), BF),
            V((6, SEQ, D), BF), V((8, SEQ, D), BF), V((8, 3, SH, D), BF), V((4, SH, D), F32),
            V((SEQ, D), BF), V((SEQ, 2 * RQ), F32),
            V((SEQ, RQ), F32), V((SEQ, RQ), F32), V((SEQ, RQ), F32), V((SEQ, RQ), F32), V((SEQ, RQ), F32),
            V((SEQ, RQ), BF),
            V((SEQ, AQ), BF), V((SEQ, 256), BF), V((3, SEQ, SEQ), F32), V((SEQ, AQ), BF),
            V((2, SEQ, FQ), F32), V((2, SEQ, FQ), F32), V((2, SEQ, FQ), BF),
            V((SEQ, FQ), BF), V((SEQ, FQ), BF), V((SEQ, 2 * RQ), BF),
            V((4, SEQ, 256), BF), V((4, 8, D), F32), V((2, 16, CR, CC), BF), V((2, 16, RR, CC), BF),
            V((SH, D), BF), V((SH, D), BF),
            dma((10,)), dma((10,)), dma((10,)), dma((6, 4)), dma((6, 4)), dma((8, 4)), dma((8, 4)),
            dma((4,)), dma((4,)), dma((4,)), dma((4,)), dma((2,)), dma((4,)), dma((2, 4)), dma((2, 2, 4)),
        ],
        compiler_params=pltpu.CompilerParams(
            collective_id=0, has_side_effects=True, vmem_limit_bytes=62 * 2**20
        ),
    )(x, cot, small, *weights)


def reduce_kernel(
    gp, gr, fo, mo, ro,
    g, gx, hb, hx, r1a, r1b, r2a, r2b, x1a, x1b, x2a, x2b,
    l_sem, cs_sem, cr_sem, s_sem, r_sem, o_sem, ps_sem, pr_sem,
):
    s = lax.axis_index("section")
    t = lax.axis_index("tensor")
    d = lax.axis_index("dp")
    px = lax.rem(d, 4)
    py = d // 4

    def along(axis, k):
        if axis == 0:
            return (s, t, py * 4 + lax.rem(px + k, 4))
        return (s, t, lax.rem(py + k, 4) * 4 + px)

    other = (1 - s, t, d)
    barrier = pltpu.get_barrier_semaphore()
    for target in (other, along(0, 1), along(0, 3), along(1, 1), along(1, 3)):
        pl.semaphore_signal(barrier, inc=1, device_id=target, device_id_type=MESH)

    n_all = N_ITEMS + 1
    place = [px, py]

    class Item:
        pass

    items = []
    for i in range(n_all):
        it = Item()
        it.i = i
        big = i < N_ITEMS
        it.g = g.at[i] if big else gx
        it.h = hb.at[i] if big else hx
        it.r1a = r1a.at[i] if big else x1a
        it.r1b = r1b.at[i] if big else x1b
        it.r2a = r2a.at[i] if big else x2a
        it.r2b = r2b.at[i] if big else x2b
        it.src = gp.at[i] if big else gr
        it.rows = CR if big else RR
        it.cut = HALF_A if big else 32
        it.first = i % 2
        it.m = place[it.first]
        it.n = place[1 - it.first]
        it.waits = []
        items.append(it)

    def pos(base, k):
        return lax.rem(base + k, 4)

    def send(it, step, side, axis, src, dst):
        copy = pltpu.make_async_remote_copy(
            src_ref=src, dst_ref=dst,
            send_sem=s_sem.at[it.i, step, side], recv_sem=r_sem.at[it.i, step, side],
            device_id=along(axis, 1 if side == 0 else 3), device_id_type=MESH,
        )
        copy.start()
        it.waits.append(copy)

    def settle(it):
        for copy in it.waits:
            copy.wait()
        it.waits = []

    def quarter(ref, it, k, lo=0, n=4):
        return ref.at[pl.ds(pos(it.m, k) * 4 + lo, n)]

    def chunk(ref, it, k, lo, n):
        return ref.at[it.m * 4 + pos(it.n, k), pl.ds(lo, n)]

    def add_into(ref, start, n, *others):
        def body(j, carry):
            total = ref[start + j].astype(F32)
            for o in others:
                total = total + o[j].astype(F32)
            ref[start + j] = total.astype(BF)
            return carry

        lax.fori_loop(0, n, body, 0)

    own = []
    for it in items:
        copy = pltpu.make_async_copy(it.src.at[s], it.g, l_sem.at[it.i])
        copy.start()
        own.append(copy)
    pl.semaphore_wait(barrier, 5)
    swap = []
    for it in items:
        copy = pltpu.make_async_remote_copy(
            src_ref=it.src.at[1 - s], dst_ref=it.h, send_sem=cs_sem.at[it.i], recv_sem=cr_sem.at[it.i],
            device_id=other, device_id_type=MESH,
        )
        copy.start()
        swap.append(copy)

    for it in items:
        own[it.i].wait()
        swap[it.i].wait()
        add_into(it.g, 0, 16, it.h)
        send(it, 0, 0, it.first, quarter(it.g, it, 2, 0, 2), it.r1a.at[0])
        send(it, 0, 1, it.first, quarter(it.g, it, 2, 2, 2), it.r1a.at[1])
    for it in items:
        settle(it)
        add_into(it.g, pos(it.m, 1) * 4, 2, it.r1a.at[0])
        add_into(it.g, pos(it.m, 3) * 4 + 2, 2, it.r1a.at[1])
        send(it, 1, 0, it.first, quarter(it.g, it, 1), it.r1b.at[0])
        send(it, 1, 1, it.first, quarter(it.g, it, 3), it.r1b.at[1])
    for it in items:
        settle(it)
        add_into(it.g, it.m * 4, 4, it.r1b.at[0], it.r1b.at[1])
        send(it, 2, 0, 1 - it.first, chunk(it.g, it, 2, 0, it.cut), it.r2a.at[pl.ds(0, it.cut)])
        send(
            it, 2, 1, 1 - it.first, chunk(it.g, it, 2, it.cut, it.rows - it.cut),
            it.r2a.at[pl.ds(it.cut, it.rows - it.cut)],
        )
    for it in items:
        settle(it)
        at = it.m * 4 + pos(it.n, 1)
        it.g[at, : it.cut] = it.g[at, : it.cut] + it.r2a[: it.cut]
        at = it.m * 4 + pos(it.n, 3)
        it.g[at, it.cut :] = it.g[at, it.cut :] + it.r2a[it.cut :]
        send(it, 3, 0, 1 - it.first, chunk(it.g, it, 1, 0, it.rows), it.r2b.at[0])
        send(it, 3, 1, 1 - it.first, chunk(it.g, it, 3, 0, it.rows), it.r2b.at[1])
    for it in items:
        settle(it)
        here = it.m * 4 + it.n
        it.h[here] = (
            it.g[here].astype(F32) + it.r2b[0].astype(F32) + it.r2b[1].astype(F32)
        ).astype(BF)
        here = chunk(it.h, it, 0, 0, it.rows)
        send(it, 4, 0, 1 - it.first, here, here)
        send(it, 4, 1, 1 - it.first, here, here)
    for it in items:
        settle(it)
        part = chunk(it.h, it, 3, 0, it.cut)
        send(it, 5, 0, 1 - it.first, part, part)
        part = chunk(it.h, it, 1, it.cut, it.rows - it.cut)
        send(it, 5, 1, 1 - it.first, part, part)
    for it in items:
        settle(it)
        here = quarter(it.h, it, 0)
        send(it, 6, 0, it.first, here, here)
        send(it, 6, 1, it.first, here, here)
    for it in items:
        settle(it)
        part = quarter(it.h, it, 3, 0, 2)
        send(it, 7, 0, it.first, part, part)
        part = quarter(it.h, it, 1, 2, 2)
        send(it, 7, 1, it.first, part, part)
    outs = []
    for it in items:
        settle(it)
        if it.i == ITEM_ATT or it.i == ITEM_REC:
            copy = pltpu.make_async_copy(it.h, mo.at[it.i - ITEM_ATT], o_sem.at[it.i])
            copy.start()
            outs.append(copy)
        elif it.i == N_ITEMS:
            copy = pltpu.make_async_copy(it.h, ro, o_sem.at[it.i])
            copy.start()
            outs.append(copy)
    for m in range(3):
        copy = pltpu.make_async_copy(hb.at[3 * s + m], fo.at[m, s], o_sem.at[m])
        copy.start()
        outs.append(copy)
        copy = pltpu.make_async_remote_copy(
            src_ref=hb.at[3 * (1 - s) + m], dst_ref=fo.at[m, s], send_sem=ps_sem.at[m], recv_sem=pr_sem.at[m],
            device_id=other, device_id_type=MESH,
        )
        copy.start()
        outs.append(copy)
    for copy in outs:
        copy.wait()


def reduce_call(gp, gr):
    hbm = pl.BlockSpec(memory_space=pl.ANY)
    V = pltpu.VMEM
    dma = pltpu.SemaphoreType.DMA
    n = N_ITEMS
    return pl.pallas_call(
        reduce_kernel,
        name="reduce",
        out_shape=[
            jax.ShapeDtypeStruct((3, 2, 16, CR, CC), BF),
            jax.ShapeDtypeStruct((2, 16, CR, CC), BF),
            jax.ShapeDtypeStruct((16, RR, CC), BF),
        ],
        in_specs=[hbm, hbm],
        out_specs=[hbm] * 3,
        scratch_shapes=[
            V((n, 16, CR, CC), BF), V((16, RR, CC), BF),
            V((n, 16, CR, CC), BF), V((16, RR, CC), BF),
            V((n, 2, 2, CR, CC), BF), V((n, 2, 4, CR, CC), BF), V((n, CR, CC), BF), V((n, 2, CR, CC), BF),
            V((2, 2, RR, CC), BF), V((2, 4, RR, CC), BF), V((RR, CC), BF), V((2, RR, CC), BF),
            dma((n + 1,)), dma((n + 1,)), dma((n + 1,)), dma((n + 1, 8, 2)), dma((n + 1, 8, 2)),
            dma((n + 1,)), dma((3,)), dma((3,)),
        ],
        compiler_params=pltpu.CompilerParams(
            collective_id=1, has_side_effects=True, vmem_limit_bytes=62 * 2**20
        ),
    )(gp, gr)


def per_device(
    tokens, plan_order, cotangent, norm_gains, ffn_gate, ffn_up, ffn_down,
    rec_in, rec_gates, rec_conv, rec_vec, rec_out, att_q, att_kv, att_out,
):
    s = lax.axis_index("section")
    plan = plan_order[0]
    seqs = tokens.reshape(2, SEQ, D)
    x = jnp.where(plan[s] == 0, seqs[0], seqs[1])
    cot = lax.dynamic_index_in_dim(cotangent.reshape(2, SEQ, D), s, 0, keepdims=False)
    small = jnp.zeros((8, D), F32)
    small = small.at[0:2].set(norm_gains[0])
    small = small.at[2:4, :RQ].set(rec_conv.astype(F32))
    small = small.at[2:4, RQ : 2 * RQ].set(rec_vec.astype(F32))
    y, dx, gp, gr = blocks_call(
        x, cot, small,
        (
            rec_in.reshape(768, 2 * RQ), rec_gates.reshape(64, 2 * RQ), rec_out,
            ffn_gate, ffn_up, ffn_down, att_q, att_kv, att_out,
        ),
    )
    fo, mo, ro = reduce_call(gp, gr)
    in_order = jnp.where(plan[0] == 0, dx, dx[::-1])
    boundary = jnp.where(s == 0, in_order, y).astype(F32).reshape(1, 2 * SEQ, D)

    def wide(part):
        return part.reshape(2, 16, 3, 48, CC).transpose(0, 1, 3, 2, 4).reshape(1, D, FQ).astype(F32)

    g_gate = wide(fo[0])
    g_up = wide(fo[1])
    g_down = (
        fo[2].reshape(2, 4, 4, CR, CC).transpose(0, 1, 3, 2, 4).reshape(1, FQ, D).astype(F32)
    )
    att, rec = mo[0], mo[1]
    g_q = att[:, :48].reshape(768, AQ).astype(F32)
    g_kv = att[:, 96:, :256].reshape(768, 256).astype(F32)
    g_ao = att[:, 48:96].reshape(8, 2, 48, CC).transpose(0, 2, 1, 3).reshape(AQ, 768).astype(F32)
    g_ro = ro.reshape(8, 2, RR, CC).transpose(0, 2, 1, 3).reshape(RQ, 768).astype(F32)
    g_in = jnp.concatenate(
        [rec[:, :48].reshape(768, CC), rec[:, 48:96].reshape(768, CC), rec[:, 96:, :256].reshape(768, 256)], 1
    )
    g_in = g_in.reshape(768, 2, RQ).astype(F32)
    g_gt = rec[:, 96:128, 256:].reshape(8, 64, HD).transpose(1, 0, 2).reshape(64, 2, RQ).astype(F32)
    tiny = rec[:12, 128:144, 256:].transpose(1, 0, 2).reshape(16, D).astype(F32)
    return (
        boundary, tiny[0:2][None], g_gate, g_up, g_down, g_in, g_gt,
        tiny[2:4, :RQ], tiny[4:6, :RQ], g_ro, g_q, g_kv, g_ao,
    )


def solution(mesh):
    placed = (
        P("dp", None),
        P("dp", None),
        P("dp", None),
        P("section", None, None),
        P("section", None, "tensor"),
        P("section", None, "tensor"),
        P("section", "tensor", None),
        P("section", None, "tensor"),
        P("section", None, "tensor"),
        P("section", "tensor"),
        P("section", "tensor"),
        P("tensor", "section"),
        P("section", "tensor"),
        P("section", None),
        P("tensor", "section"),
    )
    return jax.shard_map(
        per_device,
        mesh=mesh,
        in_specs=placed,
        out_specs=(
            P("section", "dp", None),
            P("section", None, None),
            P("section", None, "tensor"),
            P("section", None, "tensor"),
            P("section", "tensor", None),
            P("section", None, "tensor"),
            P("section", None, "tensor"),
            P("section", "tensor"),
            P("section", "tensor"),
            P("tensor", "section"),
            P("section", "tensor"),
            P("section", None),
            P("tensor", "section"),
        ),
        check_vma=False,
    )
```

time: 2780 us -> 423 us (0.15); the launches traced: 2730 us -> 417 us
  waiting for transfers between devices: 2160 us -> 0 us
  Pallas kernels: 0 us -> 319 us
  matrix products: 196 us -> 0 us
  other arithmetic: 119 us -> 11.6 us
  blocking collectives: 76.6 us -> 0 us
  starting transfers between devices: 35.4 us -> 0 us
  local copies, waits for them, and re-layouts: 119 us -> 83.8 us
    psum x12 -> x0, waiting for transfers between devices: 1690 us -> none  [the longest x7 1270 us: tensor_total(): lax.psum(partial_value.astype(jnp.bfloat16), 'tensor').astype(jnp.float32)]
    pallas_call x0 -> x2, Pallas kernels: none -> 319 us  [the longest x1 190 us: reduce_call(): pl.pallas_call(reduce_kernel, name='reduce', out_shape=[jax.ShapeDtypeStr...]
    reduce_scatter x7 -> x0, waiting for transfers between devices: 294 us -> none  [the longest x1 79.4 us: per_device(): lax.psum_scatter(ffn_acc[0].astype(jnp.bfloat16), 'dp', scatter_dimension...]
    dot_general x87 -> x0, matrix products: 184 us -> none  [the longest x30 75.7 us: dot_plain(): return jnp.dot(left, right, preferred_element_type=jnp.float32)]
    all_gather x7 -> x0, waiting for transfers between devices: 167 us -> none  [the longest x1 44.8 us: per_device(): lax.all_gather(shards[1].astype(jnp.bfloat16), 'dp', axis=0, tiled=True)]
    another operation x45 -> x0, local copies, waits for them, and re-layouts: 64.1 us -> none
    psum x1 -> x0, blocking collectives: 58.9 us -> none  [per_device(): lax.psum(gain_acc.astype(jnp.bfloat16), 'dp').astype(jnp.float32)]
    convert_element_type x26 -> x7, other arithmetic: 62.5 us -> 5.05 us  [the longest x1 2.08 us: per_device(): g_in = g_in.reshape(768, 2, RQ).astype(F32)]
  transfers between devices with their start and end apart: 31 -> 0, of which waited for: 28 -> 0; matrix products, arithmetic and copies ran while one was open for 6% -> 0% of each run, Pallas kernels for 0% -> 0%
where the time goes in v1:
time: 423 us; the launch traced here: 417 us
  Pallas kernels  319 us (75%)
  local copies, waits for them, and re-layouts  83.8 us (20%)
  other arithmetic  11.6 us (3%)
    pallas_call x1, Pallas kernels, reduce_call(): pl.pallas_call(reduce_kernel, name='reduce', out_shape=[jax.ShapeDtypeStr...  190 us
    pallas_call x1, Pallas kernels, blocks_call(): pl.pallas_call(blocks_kernel, name='blocks', out_shape=[jax.ShapeDtypeStr...  129 us
    convert_element_type x4, local copies, waits for them, and re-layouts, wide(): part.reshape(2, 16, 3, 48, CC).transpose(0, 1, 3, 2, 4).reshape(1, D, FQ)  38.3 us
    convert_element_type x2, local copies, waits for them, and re-layouts, per_device(): fo[2].reshape(2, 4, 4, CR, CC).transpose(0, 1, 3, 2, 4).reshape(1, FQ, D)  14.9 us

profile of v1, /device:TPU:1, one launch (start us, length us, event | category | flops | bytes accessed | tf_op | source)
XLA Modules:
  0.0 416.8 jit_solution(1028384517705557321)
XLA Ops:
  0.6 0.0 copy-start
  0.7 0.0 copy-start.3
  0.7 1.1 copy-done
  1.8 1.3 fusion.5
  4.4 0.7 scatter.10
  5.1 0.7 convert_dynamic-update-slice_fusion.1
  5.8 0.7 convert_dynamic-update-slice_fusion.sm_in
  6.5 0.0 copy-start.5
  6.5 1.6 copy.43
  8.1 1.9 slice_select_fusion.x_ref
  10.0 0.8 dynamic-slice_bitcast_fusion.cot_ref
  10.8 0.0 copy-done.3
  10.8 1.6 copy.42
  12.3 0.0 copy-done.5
  12.3 129.0 %blocks.1 = (bf16[2,128,1536]{2,1,0:T(8,128)(2,1)}, bf16[2,128,1536]{2,1,0:T(8,128)(2,1)}, bf16[8,2,16,144,384]{4,3,2,1,0:T(8,128)(2,1)}, bf16[2,16,64,384]{3,2,1,0:T(8,128)(2,1)}) custom-call(bf16[128,1536]{1,0:T(8,128)(2,1)} %slice_select_fusion.x_ref, bf16[128,1536]{1,0:T(8,128)(2,1)} %dynamic-slice_bitcast_fusion.cot_ref, f32[8,1536]{1,0:T(8,128)} %copy-done.5, ...), custom_call_target="tpu_custom_call" | custom-call | tf_op jit(solution)/shard_map/blocks/pallas_call | solution.py:572
  141.3 1.9 fusion
  143.2 1.3 bitcast_convert_fusion
  144.6 190.1 %reduce.7 = (bf16[3,2,16,144,384]{4,3,2,1,0:T(8,128)(2,1)}, bf16[2,16,144,384]{3,2,1,0:T(8,128)(2,1)}, bf16[16,64,384]{2,1,0:T(8,128)(2,1)}) custom-call(bf16[8,2,16,144,384]{4,3,2,1,0:T(8,128)(2,1)} %get-tuple-element.58.gp, bf16[2,16,64,384]{3,2,1,0:T(8,128)(2,1)} %get-tuple-element.59.gr), custom_call_target="tpu_custom_call" | custom-call | tf_op jit(solution)/shard_map/reduce/pallas_call | solution.py:784
  334.7 3.6 slice_bitcast_fusion
  338.3 0.2 copy.37
  338.5 0.8 reshape.249
  339.3 0.0 copy-start.2
  339.3 0.6 fusion.4
  339.9 0.6 slice_bitcast_fusion.2
  340.5 1.0 slice.151
  341.6 1.0 bitcast_convert_fusion.2
  342.6 0.0 copy-done.2
  342.6 0.2 fusion.2
  342.8 0.1 convert_bitcast_fusion.2
  342.9 0.6 copy.40
  343.5 1.1 copy.45
  344.6 1.1 bitcast_convert_fusion.1
  345.8 2.1 maximum_convert_fusion
  347.8 0.0 copy-start.4
  347.8 5.7 %reshape.248 = f32[768,2,512]{2,1,0:T(2,128)} reshape(f32[768,1024]{1,0:T(8,128)} %maximum_convert_fusion) | data formatting | bytes 6291456 | tf_op jit(solution)/shard_map/convert_element_type | solution.py:848
  353.5 0.0 copy-done.4
  353.5 0.2 convert_bitcast_fusion.1
  353.7 1.2 copy.39
  354.9 1.2 copy.44
  356.1 6.7 %fusion.1 = (bf16[1,2,16,144,384]{4,3,2,1,0:T(8,128)(2,1)S(1)}, bf16[1,2,16,144,384]{4,3,2,1,0:T(8,128)(2,1)}, bf16[1,2,16,144,384]{4,3,2,1,0:T(8,128)(2,1)}) fusion(bf16[3,2,16,144,384]{4,3,2,1,0:T(8,128)(2,1)} %get-tuple-element.61), kind=kLoop, calls=%fused_computation.23 | loop fusion | bytes 21233664 | tf_op jit(solution)/shard_map/slice | solution.py:838
  362.8 0.6 convert_bitcast_fusion
  363.4 5.7 %copy.36 = f32[2,4,144,4,384]{4,3,2,1,0:T(4,128)} copy(f32[2,4,144,4,384]{4,2,3,1,0:T(8,128)S(1)} %convert_bitcast_fusion) | data formatting | bytes 14155776 | tf_op jit(solution)/shard_map/convert_element_type | solution.py:838
  369.1 9.2 %reshape.247 = f32[1,1152,1536]{2,1,0:T(8,128)} reshape(f32[2,4,144,4,384]{4,3,2,1,0:T(4,128)} %copy.36) | data formatting | bytes 14155776 | tf_op jit(solution)/shard_map/convert_element_type | solution.py:838
  378.3 7.5 %copy.49 = f32[2,16,3,48,384]{4,2,3,1,0:T(4,128)} copy(bf16[2,16,3,48,384]{4,3,2,1,0:T(8,128)(2,1)} %bitcast.74) | data formatting | bytes 10616832 | tf_op jit(solution)/shard_map/convert_element_type | solution.py:833
  385.8 11.6 %reshape.246 = f32[1,1536,1152]{2,1,0:T(8,128)} reshape(f32[2,16,48,3,384]{4,3,2,1,0:T(4,128)} %bitcast.71) | data formatting | bytes 14155776 | tf_op jit(solution)/shard_map/convert_element_type | solution.py:833
  397.4 7.5 %copy.50 = f32[2,16,3,48,384]{4,2,3,1,0:T(4,128)} copy(bf16[2,16,3,48,384]{4,3,2,1,0:T(8,128)(2,1)} %bitcast.73) | data formatting | bytes 10616832 | tf_op jit(solution)/shard_map/convert_element_type | solution.py:833
  404.9 11.7 %reshape.245 = f32[1,1536,1152]{2,1,0:T(8,128)} reshape(f32[2,16,48,3,384]{4,3,2,1,0:T(4,128)} %bitcast.72) | data formatting | bytes 14155776 | tf_op jit(solution)/shard_map/convert_element_type | solution.py:833
  416.6 0.0 copy-done.1
  (6 shorter events, 0.1 us)
Async XLA Ops:
  0.6 1.1 copy-start
  0.7 10.1 %copy-start.3 = (bf16[768,2,512]{2,1,0:T(2,128)(2,1)S(1)}, bf16[768,2,512]{2,1,0:T(2,128)(2,1)}, u32[]{:S(2)}) copy-start(bf16[768,2,512]{2,1,0:T(2,128)(2,1)} %param.28) | copy-start | bytes 4718596
  6.5 5.8 %copy-start.5 = (f32[8,1536]{1,0:T(8,128)}, f32[8,1536]{1,0:T(8,128)S(1)}, u32[]{:S(2)}) copy-start(f32[8,1536]{1,0:T(8,128)S(1)} %convert_dynamic-update-slice_fusion.sm_in) | copy-start | bytes 147460
  339.3 3.3 copy-start.2
  347.8 5.7 %copy-start.4 = (bf16[16,64,384]{2,1,0:T(8,128)(2,1)S(1)}, bf16[16,64,384]{2,1,0:T(8,128)(2,1)}, u32[]{:S(2)}) copy-start(bf16[16,64,384]{2,1,0:T(8,128)(2,1)} %get-tuple-element.62) | copy-start | bytes 2359300
  404.9 11.7 %copy-start.1 = (bf16[256,1536]{1,0:T(8,128)(2,1)S(1)}, bf16[256,1536]{1,0:T(8,128)(2,1)}, u32[]{:S(2)}) copy-start(bf16[256,1536]{1,0:T(8,128)(2,1)} %param.23) | copy-start | bytes 2359300

commit v2 on v1

v2 whole, which is shorter than its diff:
```python
import jax
import jax.numpy as jnp
from jax import lax
from jax.experimental import pallas as pl
from jax.experimental.pallas import tpu as pltpu
from jax.sharding import PartitionSpec as P

HD = 128
SEQ = 128
NORM_EPS = 1e-06
RATE_FLOOR = 0.01
BF = jnp.bfloat16
F32 = jnp.float32
MESH = pl.DeviceIdType.MESH
NT = (((1,), (1,)), ((), ()))

D = 1536
FQ = 1152
RQ = 512
AQ = 384
SH = 32
CC = 384
HW = 768
X_AXIS = 0
Y_AXIS = 1
GU1, DN1, GU2, DN2, QKV, AO, IN, RO, MISC = range(9)
PLAN = {
    GU1: ("r", 2 * FQ, Y_AXIS),
    DN1: ("c", FQ, X_AXIS),
    GU2: ("r", 2 * FQ, X_AXIS),
    DN2: ("c", FQ, Y_AXIS),
    QKV: ("r", 640, Y_AXIS),
    AO: ("c", AQ, Y_AXIS),
    IN: ("r", 1024, X_AXIS),
    RO: ("c", RQ, X_AXIS),
    MISC: ("r", HD, Y_AXIS),
}
RING_AXIS = (X_AXIS, Y_AXIS, Y_AXIS, X_AXIS)


def mm(left, right):
    return jnp.dot(left, right, preferred_element_type=F32)


def mm_nt(left, right):
    return lax.dot_general(left, right, NT, preferred_element_type=F32)


def rms(values, gain):
    return values * lax.rsqrt(jnp.mean(values * values, -1, keepdims=True) + NORM_EPS) * gain


def rms_back(values, gain, dn):
    r = lax.rsqrt(jnp.mean(values * values, -1, keepdims=True) + NORM_EPS)
    dng = dn * gain
    dv = r * (dng - values * (r * r) * jnp.mean(dng * values, -1, keepdims=True))
    return dv, jnp.sum(dn * values * r, 0, keepdims=True)


GC = 0.7978845608028654
GA = 0.044715


def gelu(x):
    return 0.5 * x * (1.0 + jnp.tanh(GC * (x + GA * x * x * x)))


def gelu_both(x):
    th = jnp.tanh(GC * (x + GA * x * x * x))
    value = 0.5 * x * (1.0 + th)
    slope = 0.5 * (1.0 + th) + 0.5 * x * (1.0 - th * th) * GC * (1.0 + 3.0 * GA * x * x)
    return value, slope


def sigmoid(x):
    return 1.0 / (1.0 + jnp.exp(-x))


def softplus(x):
    return jnp.maximum(x, 0.0) + jnp.log(1.0 + jnp.exp(-jnp.abs(x)))


def rows_back(values, rows, k):
    return jnp.where(rows >= k, pltpu.roll(values, k, 0), 0.0)


def rows_ahead(values, rows, k):
    return jnp.where(rows < SEQ - k, pltpu.roll(values, SEQ - k, 0), 0.0)


class Item:
    pass


def whole_kernel(
    tok_ref, plan_ref, cot_ref, gain_ref, conv_ref, vec_ref,
    win, wgt, wro, wg, wu, wd, wq, wkv, wao,
    y_o, dx_o, ra, f_gu, f_dn, f_qkv, f_ao, f_in, f_ro, f_misc,
    s_in, s_gt, s_ro, s_sm, s_g, s_u, s_d, s_q, s_kv, s_ao,
    ag, sb, rb, res, x_s, n1_s, uv_s, c_s, ig_s, rg_s, a_s, h_s,
    q_s, kv_s, p_s, at_s, gate_s, up_s, hid_s, du_s, both_s,
    dkvb, gnb, yb, xb, smb,
    work, hid_t, o_t, att_t, gu_t, qkv_t, in_t, misc_t,
    la1, la2, la_o, la_a, rc1, rc2, rc_o, rc_a, l_gu1, l_gu2, l_qkv, l_in, l_misc,
    a_gu1, a_dn1, a_gu2, a_dn2, a_qkv, a_ao, a_in, a_ro, a_misc,
    r_gu1, r_dn1, r_gu2, r_dn2, r_qkv, r_ao, r_in, r_ro, r_misc,
    e_gu1, e_dn1, e_gu2, e_dn2, e_qkv, e_ao, e_in, e_ro, e_misc,
    wl_sem, ws_sem, wr_sem, ags_sem, agr_sem, rss_sem, rsr_sem,
    kvs_sem, kvr_sem, gns_sem, gnr_sem, dl_sem, dls_sem, dlr_sem,
    rgs_sem, rgr_sem, wk_sem, xs_sem, xr_sem, ys_sem, yr_sem, gs_sem, gr_sem, loc_sem,
):
    s = lax.axis_index("section")
    t = lax.axis_index("tensor")
    d = lax.axis_index("dp")
    place = (lax.rem(d, 4), d // 4)
    peers = [lax.rem(t + k, 4) for k in range(4)]
    mine = pl.ds(pl.multiple_of(t * SH, SH), SH)

    def pos(base, k):
        return lax.rem(base + k, 4)

    def along(axis, k, core):
        if axis == X_AXIS:
            return (core, t, place[1] * 4 + pos(place[0], k))
        return (core, t, pos(place[1], k) * 4 + place[0])

    barrier = pltpu.get_barrier_semaphore()
    for k in range(4):
        for core in (s, 1 - s):
            if k:
                for axis in (X_AXIS, Y_AXIS):
                    pl.semaphore_signal(
                        barrier, inc=1, device_id=along(axis, k, core), device_id_type=MESH
                    )
                pl.semaphore_signal(
                    barrier, inc=1, device_id=(core, peers[k], d), device_id_type=MESH
                )
    other = (1 - s, t, d)
    pl.semaphore_signal(barrier, inc=1, device_id=other, device_id_type=MESH)

    def push(src, dst, send_sem, recv_sem, target):
        return pltpu.make_async_remote_copy(
            src_ref=src, dst_ref=dst, send_sem=send_sem, recv_sem=recv_sem,
            device_id=target, device_id_type=MESH,
        )

    smb[...] = jnp.zeros((8, D), F32)
    smb[0:2, :] = gain_ref[0]
    smb[2:4, :RQ] = conv_ref[...].astype(F32)
    smb[2:4, RQ : 2 * RQ] = vec_ref[...].astype(F32)
    half_in = pl.ds(pl.multiple_of(s * HW, HW), HW)
    half_gt = pl.ds(pl.multiple_of(s * 64, 64), 64)
    moves = [
        (win, s_in.at[half_in, :]),
        (smb, s_sm.at[s]),
        (wgt, s_gt.at[half_gt, :]),
        (wro, s_ro.at[s]),
        (wg.at[0], s_g.at[s]),
        (wu.at[0], s_u.at[s]),
        (wd.at[0], s_d.at[s]),
        (wq, s_q.at[half_in, :]),
        (wkv, s_kv.at[half_in, :]),
        (wao, s_ao.at[s]),
    ]
    local = [pltpu.make_async_copy(a, b, wl_sem.at[i]) for i, (a, b) in enumerate(moves)]
    swap = [push(a, b, ws_sem.at[i], wr_sem.at[i], other) for i, (a, b) in enumerate(moves)]
    for copy in local:
        copy.start()
    pl.semaphore_wait(barrier, 19)
    for copy in swap:
        copy.start()

    def weights(*which):
        for i in which:
            local[i].wait()
            swap[i].wait_recv()


    def gather(p):
        return [
            push(ag.at[p, mine], ag.at[p, mine], ags_sem.at[p, k], agr_sem.at[p, k], (s, peers[k], d))
            for k in range(1, 4)
        ]

    def gather_start(p, shard):
        ag[p, mine, :] = shard.astype(BF)
        for copy in gather(p):
            copy.start()

    def gather_wait(p):
        for copy in gather(p):
            copy.wait()

    def scatter(p):
        return [
            push(
                sb.at[p % 2, pl.ds(pl.multiple_of(peers[k] * SH, SH), SH)], rb.at[p % 2, k - 1],
                rss_sem.at[p, k], rsr_sem.at[p, k], (s, peers[k], d),
            )
            for k in range(1, 4)
        ]

    def scatter_start(p):
        for copy in scatter(p):
            copy.start()

    def scatter_wait(p):
        for copy in scatter(p):
            copy.wait()
        total = sb[p % 2, mine, :].astype(F32)
        for k in range(3):
            total = total + rb[p % 2, k].astype(F32)
        return total

    def deliver(shard, buf, out, core, which):
        buf[...] = shard.astype(BF)

        @pl.when(s == core)
        def _():
            own = pltpu.make_async_copy(buf, out.at[s, mine], dl_sem.at[which])
            own.start()
            for k in range(1, 4):
                deliver_copy(buf, out, core, which, k).start()
            own.wait()

        @pl.when(s != core)
        def _():
            for k in range(4):
                deliver_copy(buf, out, core, which, k).start()

    def deliver_copy(buf, out, core, which, k):
        return push(
            buf, out.at[s, mine], dls_sem.at[which, k], dlr_sem.at[which, s, k], (core, peers[k], d)
        )

    def deliver_wait(buf, out, core, which):
        def landed(sender, k):
            push(
                buf, out.at[sender, mine], dls_sem.at[which, k], dlr_sem.at[which, sender, k],
                (core, peers[k], d),
            ).wait_recv()

        @pl.when(s == core)
        def _():
            for k in range(1, 4):
                deliver_copy(buf, out, core, which, k).wait_send()
                landed(core, k)
            for k in range(4):
                landed(1 - core, k)

        @pl.when(s != core)
        def _():
            for k in range(4):
                deliver_copy(buf, out, core, which, k).wait_send()


    sends = []

    def slot(place_at, core):
        return pl.ds(pl.multiple_of((place_at * 2 + core) * SEQ, SEQ), SEQ)

    def ring(g, src):
        m = place[RING_AXIS[g]]
        here = ra.at[g, slot(m, s)]
        copies = [push(src, here, rgs_sem.at[g, 1], rgr_sem.at[g, 1], other)]
        for k in range(1, 4):
            copies.append(
                push(src, here, rgs_sem.at[g, 2 * k], rgr_sem.at[g, 2 * k], along(RING_AXIS[g], k, s))
            )
        return copies

    def ring_start(g, src):
        own = pltpu.make_async_copy(src, ra.at[g, slot(place[RING_AXIS[g]], s)], wk_sem.at[g])
        own.start()
        copies = ring(g, src)
        for copy in copies:
            copy.start()
        sends.extend(copies)
        ring_own[g] = own
        ring_got[g] = copies

    ring_own = [None] * 4
    ring_got = [None] * 4

    def ring_pass(g):
        m = place[RING_AXIS[g]]
        for k in range(1, 4):
            ring_got[g][k].wait_recv()
            part = ra.at[g, slot(pos(m, 4 - k), s)]
            copy = push(part, part, rgs_sem.at[g, 2 * k + 1], rgr_sem.at[g, 2 * k + 1], other)
            copy.start()
            sends.append(copy)
            ring_got[g].append(copy)

    def ring_load(g):
        ring_own[g].wait()
        ring_got[g][0].wait_recv()
        for copy in ring_got[g][4:]:
            copy.wait_recv()
        copy = pltpu.make_async_copy(ra.at[g], work, wk_sem.at[4 + g])
        copy.start()
        return copy


    acc = (a_gu1, a_dn1, a_gu2, a_dn2, a_qkv, a_ao, a_in, a_ro, a_misc)
    got = (r_gu1, r_dn1, r_gu2, r_dn2, r_qkv, r_ao, r_in, r_ro, r_misc)
    fin = (e_gu1, e_dn1, e_gu2, e_dn2, e_qkv, e_ao, e_in, e_ro, e_misc)
    full = {QKV: f_qkv, AO: f_ao, IN: f_in, RO: f_ro, MISC: f_misc}
    owner = {GU1: 0, DN1: 0, GU2: 1, DN2: 1}
    items = []
    for i in range(9):
        it = Item()
        it.i = i
        it.style, it.total, it.axis = PLAN[i]
        it.n8 = it.total // 8
        it.m = place[it.axis]
        it.n = place[1 - it.axis]
        it.acc, it.got, it.fin = acc[i], got[i], fin[i]
        if i in owner:
            base = f_gu if i in (GU1, GU2) else f_dn
            it.full = base.at[s if owner[i] == 0 else 1 - s]
            it.home = base.at[0]
        else:
            it.full = full[i]
            it.home = full[i]
        it.waits = []
        items.append(it)

    def mult(x, by):
        return pl.multiple_of(x * by, by)

    def spread(i, which, axis, source, target):
        m = place[axis]
        copies = []
        for k in range(4):
            for c in range(2):
                j = 2 * k + c
                core = s if c == 0 else 1 - s
                if j == 0:
                    continue
                copy = push(
                    source(pos(m, k), core), target(m, s, j),
                    xs_sem.at[i, which, j], xr_sem.at[i, which, j], along(axis, k, core),
                )
                copy.start()
                copies.append(copy)
        sends.extend(copies)
        return copies

    def lanes(place_at, core):
        return pl.ds(mult(place_at * 2 + core, SEQ), SEQ)

    def spread_rows(i, parts, into):
        it = items[i]
        into[:, lanes(it.m, s)] = parts[it.m * 2 + s]
        it.waits += spread(
            i, 0, it.axis, lambda f, c: parts.at[f * 2 + c], lambda f, c, j: into.at[:, lanes(f, c)]
        )

    def spread_left(i, parts, into):
        it = items[i]
        into[:, lanes(it.m, s)] = parts[s]
        it.waits += spread(
            i, 0, it.axis, lambda f, c: parts.at[c], lambda f, c, j: into.at[:, lanes(f, c)]
        )

    def spread_cols(i, src, into):
        it = items[i]

        def cut(f):
            return pl.ds(mult(f, CC), CC)

        into[slot(it.m, s), :] = src[:, cut(it.m)]
        it.waits += spread(
            i, 1, it.axis, lambda f, c: src.at[:, cut(f)], lambda f, c, j: into.at[slot(f, c), :]
        )

    def arrived(it):
        for copy in it.waits:
            copy.wait_recv()
        it.waits = []

    def settle(it):
        for copy in it.waits:
            copy.wait()
        it.waits = []

    def piece(it, q):
        if it.style == "r":
            return it.acc.at[:, pl.ds(mult(q, CC), CC)]
        return it.acc.at[pl.ds(mult(q, it.n8), it.n8), :]

    def sum_start(it):
        for k in range(1, 4):
            copy = push(
                piece(it, pos(it.n, k)), it.got.at[k - 1], ys_sem.at[it.i, k], yr_sem.at[it.i, k],
                along(1 - it.axis, k, s),
            )
            copy.start()
            it.waits.append(copy)

    def rect(it, ref, f, q):
        if it.style == "r":
            return ref.at[pl.ds(mult(f * 2 + s, it.n8), it.n8), pl.ds(mult(q, CC), CC)]
        return ref.at[pl.ds(mult(s * 4 + q, it.n8), it.n8), pl.ds(mult(f, CC), CC)]

    def quarter(it, ref, f, part=None):
        if it.style == "r":
            rows = pl.ds(mult(f * 2 + s, it.n8), it.n8)
            if part is None:
                return ref.at[rows, :]
            return ref.at[rows, part * HW : part * HW + HW]
        cols = pl.ds(mult(f, CC), CC)
        if part is None:
            return ref.at[pl.ds(mult(s, 4 * it.n8), 4 * it.n8), cols]
        return ref.at[pl.ds(mult(s * 2 + part, 2 * it.n8), 2 * it.n8), cols]

    def e2_rows(i, left, load):
        it = items[i]
        arrived(it)
        load.wait()
        for j in range(4):
            cols = slice(j * CC, j * CC + CC)
            it.acc[:, cols] = mm(left[...], work[:, cols]).astype(BF)
        sum_start(it)

    def e2_cols(i, left, right):
        it = items[i]
        arrived(it)
        it.acc[...] = mm(left[...], right[...]).astype(BF)
        sum_start(it)

    def e3(i):
        it = items[i]
        settle(it)
        total = piece(it, it.n)[...].astype(F32)
        for k in range(3):
            total = total + it.got[k].astype(F32)
        it.fin[...] = total.astype(BF)
        spot = rect(it, it.full, it.m, it.n)
        for k in range(1, 4):
            copy = push(
                it.fin, spot, gs_sem.at[i, k], gr_sem.at[i, k], along(1 - it.axis, k, s)
            )
            copy.start()
            it.waits.append(copy)
        own = pltpu.make_async_copy(it.fin, spot, loc_sem.at[i])
        own.start()
        it.waits.append(own)

    def both_ways(it, at, right, left):
        for side, part in ((1, right), (3, left)):
            copy = push(
                part, part, gs_sem.at[it.i, at + side // 2], gr_sem.at[it.i, at + side // 2],
                along(it.axis, side, s),
            )
            copy.start()
            it.waits.append(copy)

    def e4(i):
        it = items[i]
        settle(it)
        part = quarter(it, it.full, it.m)
        both_ways(it, 4, part, part)

    def e5(i):
        it = items[i]
        settle(it)
        both_ways(
            it, 6, quarter(it, it.full, pos(it.m, 3), 0), quarter(it, it.full, pos(it.m, 1), 1)
        )

    def to_other(it):
        if it.style == "c":
            rows = [pl.ds(mult(s, 4 * it.n8), 4 * it.n8)]
        else:
            rows = [pl.ds(mult(f * 2 + s, it.n8), it.n8) for f in range(4)]
        cols = pl.ds(0, D)
        if it.i in (QKV, AO, IN, RO):
            cols = pl.ds(mult(1 - s, HW), HW)
        return [
            push(
                it.full.at[r, cols], it.home.at[r, cols],
                gs_sem.at[it.i, 8 + j], gr_sem.at[it.i, 8 + j], other,
            )
            for j, r in enumerate(rows)
        ]

    def e6(i):
        it = items[i]
        settle(it)
        if i in owner:

            @pl.when(s != owner[i])
            def _():
                for copy in to_other(it):
                    copy.start()
        else:
            for copy in to_other(it):
                copy.start()

    def e7(i):
        it = items[i]
        if i in owner:

            @pl.when(s != owner[i])
            def _():
                for copy in to_other(it):
                    copy.wait_send()

            @pl.when(s == owner[i])
            def _():
                for copy in to_other(it):
                    copy.wait_recv()
        else:
            for copy in to_other(it):
                copy.wait()

    def gain(block, which):
        return s_sm[block, which : which + 1, :]

    rows = lax.broadcasted_iota(jnp.int32, (SEQ, RQ), 0)

    first = plan_ref[0, s] == 0
    x_s[...] = jnp.where(first, tok_ref[:SEQ, :], tok_ref[SEQ:, :])
    cot_at = pl.ds(mult(s, SEQ), SEQ)
    spread_cols(DN2, cot_ref.at[cot_at], rc2)
    weights(0, 1)
    n1 = rms(x_s[...].astype(F32), gain(0, 0)).astype(BF)
    n1_s[...] = n1
    ring_start(0, n1_s)
    uv_s[...] = mm(n1, s_in[...])
    taps = [s_sm[k // 2, 2 + k % 2 : 3 + k % 2, :RQ] for k in range(4)]
    vec = [s_sm[k // 2, 2 + k % 2 : 3 + k % 2, RQ : 2 * RQ] for k in range(4)]
    u = uv_s[:, :RQ]
    c = vec[0] + taps[0] * u
    for k in range(1, 4):
        c = c + taps[k] * rows_back(u, rows, k)
    c_s[...] = c
    weights(2, 3)
    for head in range(4):
        cols = slice(head * HD, head * HD + HD)
        cb = c_s[:, cols].astype(BF)
        ig_s[:, cols] = sigmoid(mm(cb, s_gt[:, cols]) + vec[1][:, cols])
        rg_s[:, cols] = sigmoid(
            mm(cb, s_gt[:, RQ + head * HD : RQ + head * HD + HD]) + vec[2][:, cols]
        )
    speed = softplus(vec[3])
    a = jnp.exp(-8.0 * rg_s[...] * speed)
    a_s[...] = a
    run = jnp.sqrt(jnp.maximum(1.0 - a * a, RATE_FLOOR)) * ig_s[...] * c_s[...]
    step = 1
    while step < SEQ:
        run = run + a * rows_back(run, rows, step)
        if 2 * step < SEQ:
            a = a * jnp.where(rows >= step, pltpu.roll(a, step, 0), 1.0)
        step *= 2
    h_s[...] = run
    o = (run * gelu(uv_s[:, RQ:])).astype(BF)
    for half in range(2):
        sb[0, :, half * HW : half * HW + HW] = mm(o, s_ro[half]).astype(BF)
    scatter_start(0)
    ot = o.T
    for half in range(2):
        o_t[half] = ot[half * 256 : half * 256 + 256]
    spread_left(RO, o_t, la_o)
    x_mine = x_s[mine, :].astype(F32)
    x1 = x_mine + scatter_wait(0)
    res[0] = x1
    gather_start(0, rms(x1, gain(0, 1)))

    def ffn_forward(block, p_in, p_out):
        n2 = ag[p_in]
        for j in range(3):
            cols = slice(j * CC, j * CC + CC)
            gate = mm(n2, s_g[block, :, cols])
            up = mm(n2, s_u[block, :, cols])
            gate_s[block, :, cols] = gate
            up_s[block, :, cols] = up
            hid_s[:, cols] = (gelu(gate) * up).astype(BF)
        if block == 0:
            weights(6)
        hid = hid_s[...]
        for j in range(4):
            cols = slice(j * CC, j * CC + CC)
            sb[p_out % 2, :, cols] = mm(hid, s_d[block, :, cols]).astype(BF)
        scatter_start(p_out)
        hidt = hid_s[...].T
        for half in range(2):
            hid_t[block, half] = hidt[half * 576 : half * 576 + 576]

    weights(4, 5)
    gather_wait(0)
    ring_start(1, ag.at[0])
    ffn_forward(0, 0, 1)
    spread_left(DN1, hid_t.at[0], la1)
    mid = (res[0] + scatter_wait(1)).astype(BF).astype(F32)
    res[1] = mid
    gather_start(1, rms(mid, gain(1, 0)))
    weights(7, 8, 9)
    ring_pass(0)

    gather_wait(1)
    ring_start(2, ag.at[1])
    na = ag[1]
    q_s[...] = mm(na, s_q[...]).astype(BF)
    kv_s[...] = mm(na, s_kv[...]).astype(BF)
    keys = kv_s[:, :HD]
    vals = kv_s[:, HD:]
    allowed = lax.broadcasted_iota(jnp.int32, (SEQ, SEQ), 1) <= lax.broadcasted_iota(
        jnp.int32, (SEQ, SEQ), 0
    )
    for head in range(3):
        cols = slice(head * HD, head * HD + HD)
        score = jnp.where(allowed, mm_nt(q_s[:, cols], keys) * HD ** (-0.5), -1e30)
        expo = jnp.exp(score - jnp.max(score, -1, keepdims=True))
        p = expo / jnp.sum(expo, -1, keepdims=True)
        p_s[head] = p
        at_s[:, cols] = mm(p.astype(BF), vals).astype(BF)
    att = at_s[...]
    for half in range(2):
        sb[0, :, half * HW : half * HW + HW] = mm(att, s_ao[half]).astype(BF)
    scatter_start(2)
    attt = att.T
    for half in range(2):
        att_t[half] = attt[half * 192 : half * 192 + 192]
    spread_left(AO, att_t, la_a)
    x1 = res[1] + scatter_wait(2)
    res[2] = x1
    gather_start(2, rms(x1, gain(1, 1)))
    ring_pass(1)
    gather_wait(2)
    ring_start(3, ag.at[2])
    ffn_forward(1, 2, 3)
    spread_left(DN2, hid_t.at[1], la2)
    ring_pass(2)
    y = res[2] + scatter_wait(3)
    deliver(y, yb, y_o, 1, 0)

    def ffn_backward(block, dF, p_out, item):
        for j in range(3):
            cols = slice(j * CC, j * CC + CC)
            dhid = mm_nt(dF, s_d[block, cols, :])
            value, slope = gelu_both(gate_s[block, :, cols])
            hid_s[:, cols] = (dhid * up_s[block, :, cols] * slope).astype(BF)
            du_s[:, cols] = (dhid * value).astype(BF)
        dg = hid_s[...]
        du = du_s[...]
        for j in range(4):
            cols = slice(j * CC, j * CC + CC)
            sb[p_out % 2, :, cols] = (
                mm_nt(dg, s_g[block, cols, :]) + mm_nt(du, s_u[block, cols, :])
            ).astype(BF)
        scatter_start(p_out)
        gu_t[block, :, :144] = dg.T.reshape(8, 144, SEQ)
        gu_t[block, :, 144:] = du.T.reshape(8, 144, SEQ)
        spread_rows(item, gu_t.at[block], l_gu1 if block == 0 else l_gu2)

    cot = cot_ref[cot_at, :]
    ffn_backward(1, cot, 4, GU2)
    e2_cols(DN2, la2, rc2)
    ring_pass(3)
    dn = scatter_wait(4)
    dv, gg11 = rms_back(res[2], gain(1, 1), dn)
    dx1 = cot_ref[pl.ds(pl.multiple_of(s * SEQ + t * SH, SH), SH), :].astype(F32) + dv
    res[3] = dx1
    gather_start(3, dx1)
    load = ring_load(3)
    e2_rows(GU2, l_gu2, load)
    load = ring_load(2)

    gather_wait(3)
    spread_cols(AO, ag.at[3], rc_a)
    dA = ag[3]
    datt_s = both_s.at[:, :AQ]
    dq_s = both_s.at[:, AQ : 2 * AQ]
    datt_s[...] = (mm_nt(dA[:, :HW], s_ao[0]) + mm_nt(dA[:, HW:], s_ao[1])).astype(BF)
    dk = jnp.zeros((SEQ, HD), F32)
    dw = jnp.zeros((SEQ, HD), F32)
    for head in range(3):
        cols = slice(head * HD, head * HD + HD)
        p = p_s[head]
        datt = datt_s[:, cols]
        dpr = mm_nt(datt, kv_s[:, HD:])
        dw = dw + mm(p.astype(BF).T, datt)
        ds = (p * (dpr - jnp.sum(p * dpr, -1, keepdims=True)) * HD ** (-0.5)).astype(BF)
        dq_s[:, cols] = mm(ds, kv_s[:, :HD]).astype(BF)
        dk = dk + mm(ds.T, q_s[:, cols])
    dkvb[0, :, :HD] = dk.astype(BF)
    dkvb[0, :, HD:] = dw.astype(BF)
    kv_copies = [
        push(dkvb.at[0], dkvb.at[k], kvs_sem.at[k], kvr_sem.at[k], (s, peers[k], d))
        for k in range(1, 4)
    ]
    for copy in kv_copies:
        copy.start()
    dq = dq_s[...]
    for j in range(4):
        cols = slice(j * CC, j * CC + CC)
        sb[1, :, cols] = mm_nt(dq, s_q[cols, :]).astype(BF)
    scatter_start(5)
    e3(DN2)
    for copy in kv_copies:
        copy.wait()
    total = dkvb[0].astype(F32)
    for k in range(1, 4):
        total = total + dkvb[k].astype(F32)
    dkv_s = both_s.at[:, 2 * AQ : 2 * AQ + 256]
    dkv_s[...] = total.astype(BF)
    qkv_t[:, :48] = dq_s[...].T.reshape(8, 48, SEQ)
    qkv_t[:, 48:] = dkv_s[...].T.reshape(8, 32, SEQ)
    spread_rows(QKV, qkv_t, l_qkv)
    dn = scatter_wait(5) + mm_nt(dkv_s[mine, :], s_kv[...])
    dv, gg10 = rms_back(res[1], gain(1, 0), dn)
    dmid = res[3] + dv
    big_g = dmid.astype(BF).astype(F32)
    gather_start(4, big_g)
    res[3] = big_g
    e3(GU2)
    e2_cols(AO, la_a, rc_a)
    e4(DN2)
    gather_wait(4)
    spread_cols(DN1, ag.at[4], rc1)
    ffn_backward(0, ag[4], 6, GU1)
    e2_rows(QKV, l_qkv, load)
    load = ring_load(1)
    e4(GU2)
    dn = scatter_wait(6)
    dv, gg01 = rms_back(res[0], gain(0, 1), dn)
    dx1 = res[3] + dv
    res[3] = dx1
    gather_start(5, dx1)
    e5(DN2)
    e3(AO)
    e2_cols(DN1, la1, rc1)

    gather_wait(5)
    spread_cols(RO, ag.at[5], rc_o)
    dA = ag[5]
    dO = mm_nt(dA[:, :HW], s_ro[0]) + mm_nt(dA[:, HW:], s_ro[1])
    value, slope = gelu_both(uv_s[:, RQ:])
    h = h_s[...]
    both_s[:, RQ:] = (dO * h * slope).astype(BF)
    e = dO * value
    a = a_s[...]
    coef = rows_ahead(a, rows, 1)
    step = 1
    while step < SEQ:
        e = e + coef * rows_ahead(e, rows, step)
        if 2 * step < SEQ:
            coef = coef * rows_ahead(coef, rows, step)
        step *= 2
    ig = ig_s[...]
    rg = rg_s[...]
    c = c_s[...]
    room = 1.0 - a * a
    m = jnp.sqrt(jnp.maximum(room, RATE_FLOOR))
    ga = e * rows_back(h, rows, 1) - jnp.where(room > RATE_FLOOR, e * ig * c * a / m, 0.0)
    dl = ga * a
    gv3 = jnp.sum(dl * rg, 0, keepdims=True) * (-8.0) * sigmoid(vec[3])
    er = -8.0 * dl * speed * rg * (1.0 - rg)
    ei = e * m * c * ig * (1.0 - ig)
    gv1 = jnp.sum(ei, 0, keepdims=True)
    gv2 = jnp.sum(er, 0, keepdims=True)
    c_s[...] = e * m * ig
    ig_s[...] = ei
    rg_s[...] = er
    for head in range(4):
        cols = slice(head * HD, head * HD + HD)
        late = slice(RQ + head * HD, RQ + head * HD + HD)
        dpin = ig_s[:, cols].astype(BF)
        dprec = rg_s[:, cols].astype(BF)
        cbt = c[:, cols].astype(BF).T
        misc_t[:, cols] = mm(cbt, dpin).astype(BF)
        misc_t[:, late] = mm(cbt, dprec).astype(BF)
        c_s[:, cols] += mm_nt(dpin, s_gt[:, cols]) + mm_nt(dprec, s_gt[:, late])
    dc = c_s[...]
    u = uv_s[:, :RQ]
    du = taps[0] * dc
    gtap = [jnp.sum(u * dc, 0, keepdims=True)]
    for k in range(1, 4):
        du = du + taps[k] * rows_ahead(dc, rows, k)
        gtap.append(jnp.sum(rows_back(u, rows, k) * dc, 0, keepdims=True))
    gv0 = jnp.sum(dc, 0, keepdims=True)
    both_s[:, :RQ] = du.astype(BF)
    both = both_s[...]
    for j in range(4):
        cols = slice(j * CC, j * CC + CC)
        sb[1, :, cols] = mm_nt(both, s_in[cols, :]).astype(BF)
    scatter_start(7)
    in_t[...] = both.T.reshape(8, SEQ, SEQ)
    spread_rows(IN, in_t, l_in)
    e2_rows(GU1, l_gu1, load)
    load = ring_load(0)
    dn = scatter_wait(7)
    dv, gg00 = rms_back(x_mine, gain(0, 0), dn)
    deliver(res[3] + dv, xb, dx_o, 0, 1)
    gnb[0, 0:1] = gg00
    gnb[0, 1:2] = gg01
    gnb[0, 2:3] = gg10
    gnb[0, 3:4] = gg11
    gnb[0, 4:8] = jnp.zeros((4, D), F32)
    gn_copies = [
        push(gnb.at[0], gnb.at[k], gns_sem.at[k], gnr_sem.at[k], (s, peers[k], d))
        for k in range(1, 4)
    ]
    for copy in gn_copies:
        copy.start()
    e3(QKV)
    e5(GU2)
    e4(AO)
    e2_cols(RO, la_o, rc_o)
    e2_rows(IN, l_in, load)
    for copy in gn_copies:
        copy.wait()
    gains = gnb[0] + gnb[1] + gnb[2] + gnb[3]
    small = gtap + [gv0, gv1, gv2, gv3]
    for g in range(4):
        for part in range(3):
            small.append(gains[g : g + 1, part * RQ : part * RQ + RQ])
    small.append(jnp.zeros((HD - len(small), RQ), F32))
    misc_t[:, 2 * RQ :] = jnp.concatenate(small, 0).astype(BF)
    it = items[MISC]
    l_misc[0] = misc_t[pl.ds(mult(it.m * 2 + s, 16), 16), :]
    it.waits += spread(
        MISC, 0, it.axis, lambda f, c: misc_t.at[pl.ds(mult(f * 2 + c, 16), 16), :],
        lambda f, c, j: l_misc.at[j],
    )
    e3(DN1)
    e6(DN2)
    e3(GU1)
    e4(QKV)
    arrived(it)
    total = l_misc[0].astype(F32)
    for j in range(1, 8):
        total = total + l_misc[j].astype(F32)
    it.acc[...] = total.astype(BF)
    sum_start(it)
    e5(AO)
    e3(RO)
    e3(IN)
    e4(DN1)
    e4(GU1)
    e6(GU2)
    e5(QKV)
    e3(MISC)
    e6(AO)
    e4(RO)
    e4(IN)
    e5(DN1)
    e5(GU1)
    e4(MISC)
    e6(QKV)
    e5(RO)
    e5(IN)
    e5(MISC)
    e6(DN1)
    e6(GU1)
    e6(RO)
    e6(IN)
    e6(MISC)
    deliver_wait(yb, y_o, 1, 0)
    deliver_wait(xb, dx_o, 0, 1)
    for copy in swap:
        copy.wait_send()
    for copy in sends:
        copy.wait_send()
    for i in (DN2, GU2, AO, QKV, DN1, GU1, RO, IN, MISC):
        e7(i)


def whole_call(tokens, plan, cot, gains, conv, vec, weights):
    vm = pl.BlockSpec(memory_space=pltpu.VMEM)
    hbm = pl.BlockSpec(memory_space=pl.ANY)
    V = pltpu.VMEM
    dma = pltpu.SemaphoreType.DMA
    accs, gots, fins = [], [], []
    for i in range(9):
        style, total, _ = PLAN[i]
        n8 = total // 8
        accs.append(V((n8, D) if style == "r" else (4 * n8, CC), BF))
        gots.append(V((3, n8, CC), BF))
        fins.append(V((n8, CC), BF))
    shapes = [
        (2, SEQ, D), (2, SEQ, D), (4, 8 * SEQ, D),
        (2, 2 * FQ, D), (2, FQ, D), (640, D), (AQ, D), (1024, D), (RQ, D), (HD, D),
    ]
    return pl.pallas_call(
        whole_kernel,
        name="whole",
        out_shape=[jax.ShapeDtypeStruct(shape, BF) for shape in shapes],
        in_specs=[vm, pl.BlockSpec(memory_space=pltpu.SMEM), vm, vm, vm, vm] + [hbm] * 9,
        out_specs=[hbm] * 10,
        scratch_shapes=[
            V((D, 2 * RQ), BF), V((HD, 2 * RQ), BF), V((2, RQ, HW), BF), V((2, 8, D), F32),
            V((2, D, FQ), BF), V((2, D, FQ), BF), V((2, FQ, D), BF),
            V((D, AQ), BF), V((D, 256), BF), V((2, AQ, HW), BF),
            V((6, SEQ, D), BF), V((2, SEQ, D), BF), V((2, 3, SH, D), BF), V((4, SH, D), F32),
            V((SEQ, D), BF), V((SEQ, D), BF), V((SEQ, 2 * RQ), F32),
            V((SEQ, RQ), F32), V((SEQ, RQ), F32), V((SEQ, RQ), F32), V((SEQ, RQ), F32), V((SEQ, RQ), F32),
            V((SEQ, AQ), BF), V((SEQ, 256), BF), V((3, SEQ, SEQ), F32), V((SEQ, AQ), BF),
            V((2, SEQ, FQ), F32), V((2, SEQ, FQ), F32), V((SEQ, FQ), BF),
            V((SEQ, FQ), BF), V((SEQ, 2 * RQ), BF),
            V((4, SEQ, 256), BF), V((4, 8, D), F32), V((SH, D), BF), V((SH, D), BF), V((8, D), F32),
            V((8 * SEQ, D), BF), V((2, 2, 576, SEQ), BF), V((2, 256, SEQ), BF), V((2, 192, SEQ), BF),
            V((2, 8, 288, SEQ), BF), V((8, 80, SEQ), BF), V((8, SEQ, SEQ), BF), V((HD, D), BF),
            V((576, 1024), BF), V((576, 1024), BF), V((256, 1024), BF), V((192, 1024), BF),
            V((1024, CC), BF), V((1024, CC), BF), V((1024, CC), BF), V((1024, CC), BF),
            V((288, 1024), BF), V((288, 1024), BF), V((80, 1024), BF), V((SEQ, 1024), BF), V((8, 16, D), BF),
            *accs, *gots, *fins,
            dma((10,)), dma((10,)), dma((10,)), dma((6, 4)), dma((6, 4)), dma((8, 4)), dma((8, 4)),
            dma((4,)), dma((4,)), dma((4,)), dma((4,)), dma((2,)), dma((2, 4)), dma((2, 2, 4)),
            dma((4, 8)), dma((4, 8)), dma((8,)), dma((9, 2, 8)), dma((9, 2, 8)),
            dma((9, 4)), dma((9, 4)), dma((9, 12)), dma((9, 12)), dma((9,)),
        ],
        compiler_params=pltpu.CompilerParams(
            collective_id=0, has_side_effects=True, vmem_limit_bytes=63 * 2**20
        ),
    )(tokens, plan, cot, gains, conv, vec, *weights)


def unpack_kernel(s_ref, gu, dn, qkv, ao, rin, ro, g_gate, g_up, g_dn, g_q, g_kv, g_ao, g_in, g_ro):
    i = pl.program_id(0)
    for b in range(8):
        cols = slice(b * 144, b * 144 + 144)
        part = gu[0, b * 288 : b * 288 + 288, :].T.astype(F32)
        g_gate[0, :, cols] = part[:, :144]
        g_up[0, :, cols] = part[:, 144:]
    g_dn[0] = dn[0].astype(F32)
    for b in range(8):
        part = qkv[b * 80 : b * 80 + 80, :].T.astype(F32)
        g_q[:, b * 48 : b * 48 + 48] = part[:, :48]
        g_kv[:, b * 32 : b * 32 + 32] = part[:, 48:]
    g_in[...] = rin[...].T.astype(F32)

    @pl.when(i == 0)
    def _():
        g_ao[...] = ao[...].astype(F32)
        g_ro[...] = ro[...].astype(F32)


def unpack_call(s, gu, dn, qkv, ao, rin, ro):
    n = 6
    wide = D // n
    part = HW // n
    sds = jax.ShapeDtypeStruct
    return pl.pallas_call(
        unpack_kernel,
        name="unpack",
        out_shape=[
            sds((1, D, FQ), F32), sds((1, D, FQ), F32), sds((1, FQ, D), F32),
            sds((HW, AQ), F32), sds((HW, 256), F32), sds((AQ, HW), F32),
            sds((HW, 1024), F32), sds((RQ, HW), F32),
        ],
        grid_spec=pltpu.PrefetchScalarGridSpec(
            num_scalar_prefetch=1,
            grid=(n,),
            in_specs=[
                pl.BlockSpec((1, 2 * FQ, wide), lambda i, s: (0, 0, i)),
                pl.BlockSpec((1, FQ // n, D), lambda i, s: (0, i, 0)),
                pl.BlockSpec((640, part), lambda i, s: (0, s[0] * n + i)),
                pl.BlockSpec((AQ, HW), lambda i, s: (0, s[0])),
                pl.BlockSpec((1024, part), lambda i, s: (0, s[0] * n + i)),
                pl.BlockSpec((RQ, HW), lambda i, s: (0, s[0])),
            ],
            out_specs=[
                pl.BlockSpec((1, wide, FQ), lambda i, s: (0, i, 0)),
                pl.BlockSpec((1, wide, FQ), lambda i, s: (0, i, 0)),
                pl.BlockSpec((1, FQ // n, D), lambda i, s: (0, i, 0)),
                pl.BlockSpec((part, AQ), lambda i, s: (i, 0)),
                pl.BlockSpec((part, 256), lambda i, s: (i, 0)),
                pl.BlockSpec((AQ, HW), lambda i, s: (0, 0)),
                pl.BlockSpec((part, 1024), lambda i, s: (i, 0)),
                pl.BlockSpec((RQ, HW), lambda i, s: (0, 0)),
            ],
        ),
        compiler_params=pltpu.CompilerParams(vmem_limit_bytes=40 * 2**20),
    )(s, gu, dn, qkv, ao, rin, ro)


def per_device(
    tokens, plan_order, cotangent, norm_gains, ffn_gate, ffn_up, ffn_down,
    rec_in, rec_gates, rec_conv, rec_vec, rec_out, att_q, att_kv, att_out,
):
    s = lax.axis_index("section")
    plan = plan_order[0]
    y, dx, _, gu, dn, qkv, ao, rin, ro, misc = whole_call(
        tokens, plan_order, cotangent, norm_gains, rec_conv, rec_vec,
        (
            rec_in.reshape(HW, 2 * RQ), rec_gates.reshape(64, 2 * RQ), rec_out,
            ffn_gate, ffn_up, ffn_down, att_q, att_kv, att_out,
        ),
    )
    in_order = jnp.where(plan[0] == 0, dx, dx[::-1])
    boundary = jnp.where(s == 0, in_order, y).astype(F32).reshape(1, 2 * SEQ, D)
    g_gate, g_up, g_dn, g_q, g_kv, g_ao, g_in, g_ro = unpack_call(
        s.astype(jnp.int32).reshape(1), gu, dn, qkv, ao, rin, ro
    )
    misc = misc.astype(F32)
    g_gt = lax.dynamic_slice_in_dim(misc[:, : 2 * RQ], s * 64, 64, 0).reshape(64, 2, RQ)
    small = misc[:, 2 * RQ :]
    g_conv = lax.dynamic_slice_in_dim(small, s * 2, 2, 0)
    g_vec = lax.dynamic_slice_in_dim(small, 4 + s * 2, 2, 0)
    g_gain = lax.dynamic_slice_in_dim(small, 8 + s * 6, 6, 0).reshape(1, 2, D)
    return (
        boundary, g_gain, g_gate, g_up, g_dn, g_in.reshape(HW, 2, RQ), g_gt,
        g_conv, g_vec, g_ro, g_q, g_kv, g_ao,
    )


def solution(mesh):
    placed = (
        P("dp", None),
        P("dp", None),
        P("dp", None),
        P("section", None, None),
        P("section", None, "tensor"),
        P("section", None, "tensor"),
        P("section", "tensor", None),
        P("section", None, "tensor"),
        P("section", None, "tensor"),
        P("section", "tensor"),
        P("section", "tensor"),
        P("tensor", "section"),
        P("section", "tensor"),
        P("section", None),
        P("tensor", "section"),
    )
    return jax.shard_map(
        per_device,
        mesh=mesh,
        in_specs=placed,
        out_specs=(
            P("section", "dp", None),
            P("section", None, None),
            P("section", None, "tensor"),
            P("section", None, "tensor"),
            P("section", "tensor", None),
            P("section", None, "tensor"),
            P("section", None, "tensor"),
            P("section", "tensor"),
            P("section", "tensor"),
            P("tensor", "section"),
            P("section", "tensor"),
            P("section", None),
            P("tensor", "section"),
        ),
        check_vma=False,
    )
```

time: 423 us -> 277 us (0.65); the launches traced: 417 us -> 276 us
  local copies, waits for them, and re-layouts: 83.8 us -> 17.5 us
  Pallas kernels: 319 us -> 254 us
  other arithmetic: 11.6 us -> 3.28 us
    pallas_call x2, Pallas kernels: 319 us -> 254 us  [the longest x1 238 us: whole_call(): pl.pallas_call(whole_kernel, name='whole', out_shape=[jax.ShapeDtypeStruc...]
    convert_element_type x12 -> x0, local copies, waits for them, and re-layouts: 61.6 us -> none  [the longest x4 38.3 us: wide(): part.reshape(2, 16, 3, 48, CC).transpose(0, 1, 3, 2, 4).reshape(1, D, FQ)]
    slice x7 -> x2, local copies, waits for them, and re-layouts: 9.89 us -> 0.97 us  [the longest x1 0.92 us: per_device(): small = misc[:, 2 * RQ:]]
    reshape x0 -> x3, local copies, waits for them, and re-layouts: none -> 5.27 us  [the longest x1 3.73 us: per_device(): g_in.reshape(HW, 2, RQ)]
    convert_element_type x7 -> x0, other arithmetic: 5.05 us -> none  [the longest x1 2.08 us: per_device(): g_in = g_in.reshape(768, 2, RQ).astype(F32)]
    squeeze x2 -> x0, local copies, waits for them, and re-layouts: 4.34 us -> none  [the longest x1 3.57 us: per_device(): att, rec = (mo[0], mo[1])]
    unnamed x16 -> x12, local copies, waits for them, and re-layouts: 6.63 us -> 10.7 us
where the time goes in v2:
time: 277 us; the launch traced here: 276 us
  Pallas kernels  254 us (92%)
  local copies, waits for them, and re-layouts  17.5 us (6%)
  other arithmetic  3.28 us (1%)
    pallas_call x1, Pallas kernels, whole_call(): pl.pallas_call(whole_kernel, name='whole', out_shape=[jax.ShapeDtypeStruc...  238 us
    pallas_call x1, Pallas kernels, unpack_call(): pl.pallas_call(unpack_kernel, name='unpack', out_shape=[sds((1, D, FQ), F...  16 us
    unnamed x12, local copies, waits for them, and re-layouts  10.7 us

profile of v2, /device:TPU:1, one launch (start us, length us, event | category | flops | bytes accessed | tf_op | source)
XLA Modules:
  0.0 276.4 jit_solution(9616687054109061393)
XLA Ops:
  1.3 1.6 copy.29
  2.9 3.0 %copy.28 = bf16[96,8,2,512]{3,1,2,0:T(8,128)(2,1)} copy(bf16[96,8,2,512]{3,2,1,0:T(2,128)(2,1)} %bitcast.13) | data formatting | bytes 3145728
  5.8 238.2 %whole.1 = (bf16[2,128,1536]{2,1,0:T(8,128)(2,1)}, bf16[2,128,1536]{2,1,0:T(8,128)(2,1)}, bf16[4,1024,1536]{2,1,0:T(8,128)(2,1)}, bf16[2,2304,1536]{2,1,0:T(8,12...) custom-call(bf16[256,1536]{1,0:T(8,128)(2,1)} %tok_ref.1, ...), custom_call_target="tpu_custom_call" | custom-call | tf_op jit(solution)/shard_map/whole/pallas_call | solution.py:888
  244.0 0.0 copy-start.4
  244.1 1.9 fusion
  246.0 0.9 slice.13
  246.9 0.6 constant_dynamic-slice_fusion
  247.6 0.6 reshape.58
  248.2 0.0 copy-done.4
  248.3 0.9 reshape.61
  249.2 1.3 bitcast_convert_fusion
  250.5 0.0 copy-start
  250.5 1.9 copy-done
  252.4 0.0 copy-start.1
  252.4 1.5 copy-done.1
  253.9 0.0 copy-start.2
  253.9 1.4 copy-done.2
  255.4 0.0 copy-start.3
  255.4 1.3 copy-done.3
  256.6 16.0 %unpack.1 = (f32[1,1536,1152]{2,1,0:T(8,128)}, f32[1,1536,1152]{2,1,0:T(8,128)}, f32[1,1152,1536]{2,1,0:T(8,128)}, f32[768,384]{1,0:T(8,128)}, f32[768,256]{1,0:...) custom-call(s32[1]{0:T(128)} %bitcast.2.s_ref, ...), custom_call_target="tpu_custom_call" | custom-call | tf_op jit(solution)/shard_map/unpack/pallas_call | solution.py:947
  272.7 3.7 %reshape.60 = f32[768,2,512]{2,1,0:T(2,128)} reshape(f32[768,1024]{1,0:T(8,128)S(1)} %get-tuple-element.42) | data formatting | bytes 6291456 | tf_op jit(solution)/shard_map/reshape | solution.py:1006
  (3 shorter events, 0.1 us)
Async XLA Ops:
  244.0 4.1 %copy-start.4 = (bf16[128,1536]{1,0:T(8,128)(2,1)S(1)}, bf16[128,1536]{1,0:T(8,128)(2,1)}, u32[]{:S(2)}) copy-start(bf16[128,1536]{1,0:T(8,128)(2,1)} %get-tuple-element.32) | copy-start | bytes 1179652
  250.5 1.9 copy-start
  252.4 1.5 copy-start.1
  253.9 1.4 copy-start.2
  255.4 1.3 copy-start.3

commit v3 on v2

v3 whole, which is shorter than its diff:
```python
import jax
import jax.numpy as jnp
from jax import lax
from jax.experimental import pallas as pl
from jax.experimental.pallas import tpu as pltpu
from jax.sharding import PartitionSpec as P

HD = 128
SEQ = 128
NORM_EPS = 1e-06
RATE_FLOOR = 0.01
BF = jnp.bfloat16
F32 = jnp.float32
MESH = pl.DeviceIdType.MESH
NT = (((1,), (1,)), ((), ()))

D = 1536
FQ = 1152
RQ = 512
AQ = 384
SH = 32
CC = 384
HW = 768
X_AXIS = 0
Y_AXIS = 1
G1, U1, D1, G2, U2, D2, QKV, AO, IN, RO, MISC = range(11)
PLAN = {
    G1: ("r", FQ, Y_AXIS),
    U1: ("r", FQ, Y_AXIS),
    D1: ("c", FQ, X_AXIS),
    G2: ("r", FQ, X_AXIS),
    U2: ("r", FQ, X_AXIS),
    D2: ("r", FQ, Y_AXIS),
    QKV: ("r", 640, Y_AXIS),
    AO: ("c", AQ, Y_AXIS),
    IN: ("r", 1024, X_AXIS),
    RO: ("c", RQ, X_AXIS),
    MISC: ("r", HD, Y_AXIS),
}
RING_AXIS = (X_AXIS, Y_AXIS, Y_AXIS, X_AXIS, Y_AXIS)
RN1, RN2, RNA, RN2B, RCOT = range(5)
ROOM = {G2: 0, U2: 144, G1: 288, U1: 432, D1: 576, QKV: 720, IN: 800, AO: 928, RO: 976, MISC: 1040}


def mm(left, right):
    return jnp.dot(left, right, preferred_element_type=F32)


def mm_nt(left, right):
    return lax.dot_general(left, right, NT, preferred_element_type=F32)


def rms(values, gain):
    return values * lax.rsqrt(jnp.mean(values * values, -1, keepdims=True) + NORM_EPS) * gain


def rms_back(values, gain, dn):
    r = lax.rsqrt(jnp.mean(values * values, -1, keepdims=True) + NORM_EPS)
    dng = dn * gain
    dv = r * (dng - values * (r * r) * jnp.mean(dng * values, -1, keepdims=True))
    return dv, jnp.sum(dn * values * r, 0, keepdims=True)


GC = 0.7978845608028654
GA = 0.044715


def gelu(x):
    return 0.5 * x * (1.0 + jnp.tanh(GC * (x + GA * x * x * x)))


def gelu_both(x):
    th = jnp.tanh(GC * (x + GA * x * x * x))
    value = 0.5 * x * (1.0 + th)
    slope = 0.5 * (1.0 + th) + 0.5 * x * (1.0 - th * th) * GC * (1.0 + 3.0 * GA * x * x)
    return value, slope


def sigmoid(x):
    return 1.0 / (1.0 + jnp.exp(-x))


def softplus(x):
    return jnp.maximum(x, 0.0) + jnp.log(1.0 + jnp.exp(-jnp.abs(x)))


def rows_back(values, rows, k):
    return jnp.where(rows >= k, pltpu.roll(values, k, 0), 0.0)


def rows_ahead(values, rows, k):
    return jnp.where(rows < SEQ - k, pltpu.roll(values, SEQ - k, 0), 0.0)


class Item:
    pass


def whole_kernel(
    tok_ref, plan_ref, cot_ref, gain_ref, conv_ref, vec_ref,
    win, wgt, wro, wg, wu, wd, wq, wkv, wao,
    y_o, dx_o, ra, f_ffn, f_qkv, f_ao, f_in, f_ro, f_misc,
    s_in, s_gt, s_ro, s_sm, s_g, s_u, s_d, s_q, s_kv, s_ao,
    ag, sb, rb, res, x_s, n1_s, uv_s, c_s, ig_s, rg_s, a_s, h_s,
    q_s, kv_s, p_s, at_s, gate_s, up_s, hid_s, du_s, both_s,
    dkvb, gnb, yb, xb, smb,
    work, hid_t, o_t, att_t, g_t, u_t, qkv_t, in_t, misc_t,
    la1, la_o, la_a, rc1, rc_o, rc_a, l_g1, l_u1, l_g2, l_u2, l_d2, l_qkv, l_in, l_misc,
    a_d2, cs, *rest,
):
    crs, gots, fins = rest[:11], rest[11:22], rest[22:33]
    (
        wl_sem, ws_sem, wr_sem, ags_sem, agr_sem, rss_sem, rsr_sem,
        kvs_sem, kvr_sem, gns_sem, gnr_sem, dl_sem, dls_sem, dlr_sem,
        rgs_sem, rgr_sem, wk_sem, xs_sem, xr_sem, ys_sem, yr_sem, gs_sem, gr_sem, loc_sem,
        cs_sem, cr_sem,
    ) = rest[33:]
    s = lax.axis_index("section")
    t = lax.axis_index("tensor")
    d = lax.axis_index("dp")
    place = (lax.rem(d, 4), d // 4)
    peers = [lax.rem(t + k, 4) for k in range(4)]
    mine = [pl.ds(pl.multiple_of(t * SH + h * 16, 16), 16) for h in range(2)]

    def pos(base, k):
        return lax.rem(base + k, 4)

    def along(axis, k, core):
        if axis == X_AXIS:
            return (core, t, place[1] * 4 + pos(place[0], k))
        return (core, t, pos(place[1], k) * 4 + place[0])

    barrier = pltpu.get_barrier_semaphore()
    other = (1 - s, t, d)
    for k in range(1, 4):
        for target in (
            (s, peers[k], d), (1 - s, peers[k], d), along(X_AXIS, k, s), along(Y_AXIS, k, s),
        ):
            pl.semaphore_signal(barrier, inc=1, device_id=target, device_id_type=MESH)
    pl.semaphore_signal(barrier, inc=1, device_id=other, device_id_type=MESH)

    def push(src, dst, send_sem, recv_sem, target):
        return pltpu.make_async_remote_copy(
            src_ref=src, dst_ref=dst, send_sem=send_sem, recv_sem=recv_sem,
            device_id=target, device_id_type=MESH,
        )

    smb[...] = jnp.zeros((8, D), F32)
    smb[0:2, :] = gain_ref[0]
    smb[2:4, :RQ] = conv_ref[...].astype(F32)
    smb[2:4, RQ : 2 * RQ] = vec_ref[...].astype(F32)
    half_in = pl.ds(pl.multiple_of(s * HW, HW), HW)
    half_gt = pl.ds(pl.multiple_of(s * 64, 64), 64)
    moves = [
        (win, s_in.at[half_in, :]),
        (smb, s_sm.at[s]),
        (wgt, s_gt.at[half_gt, :]),
        (wro, s_ro.at[s]),
        (wg.at[0], s_g.at[s]),
        (wu.at[0], s_u.at[s]),
        (wd.at[0], s_d.at[s]),
        (wq, s_q.at[half_in, :]),
        (wkv, s_kv.at[half_in, :]),
        (wao, s_ao.at[s]),
    ]
    local = [pltpu.make_async_copy(a, b, wl_sem.at[i]) for i, (a, b) in enumerate(moves)]
    swap = [push(a, b, ws_sem.at[i], wr_sem.at[i], other) for i, (a, b) in enumerate(moves)]
    for copy in local:
        copy.start()
    pl.semaphore_wait(barrier, 13)
    for copy in swap:
        copy.start()

    def weights(*which):
        for i in which:
            local[i].wait()
            swap[i].wait_recv()


    def gather(p, h):
        return [
            push(
                ag.at[p, mine[h]], ag.at[p, mine[h]], ags_sem.at[p, h, k], agr_sem.at[p, h, k],
                (s, peers[k], d),
            )
            for k in (2, 1, 3)
        ]

    def gather_start(p, h, shard):
        ag[p, mine[h], :] = shard.astype(BF)
        for copy in gather(p, h):
            copy.start()

    def gather_wait(p):
        for h in range(2):
            for copy in gather(p, h):
                copy.wait()

    def scatter(p, h):
        return [
            push(
                sb.at[p % 2, pl.ds(pl.multiple_of(peers[k] * SH + h * 16, 16), 16)],
                rb.at[p % 2, k - 1, h * 16 : h * 16 + 16],
                rss_sem.at[p, h, k], rsr_sem.at[p, h, k], (s, peers[k], d),
            )
            for k in (2, 1, 3)
        ]

    def scatter_start(p):
        for h in range(2):
            for copy in scatter(p, h):
                copy.start()

    def scatter_wait(p, h):
        for copy in scatter(p, h):
            copy.wait()
        total = sb[p % 2, mine[h], :].astype(F32)
        for k in range(3):
            total = total + rb[p % 2, k, h * 16 : h * 16 + 16].astype(F32)
        return total

    whole = pl.ds(pl.multiple_of(t * SH, SH), SH)

    def deliver(buf, out, core, which):
        @pl.when(s == core)
        def _():
            own = pltpu.make_async_copy(buf, out.at[s, whole], dl_sem.at[which])
            own.start()
            for k in range(1, 4):
                deliver_copy(buf, out, core, which, k).start()
            own.wait()

        @pl.when(s != core)
        def _():
            for k in range(4):
                deliver_copy(buf, out, core, which, k).start()

    def deliver_copy(buf, out, core, which, k):
        return push(
            buf, out.at[s, whole], dls_sem.at[which, k], dlr_sem.at[which, s, k],
            (core, peers[k], d),
        )

    def deliver_wait(buf, out, core, which):
        def landed(sender, k):
            push(
                buf, out.at[sender, whole], dls_sem.at[which, k], dlr_sem.at[which, sender, k],
                (core, peers[k], d),
            ).wait_recv()

        @pl.when(s == core)
        def _():
            for k in range(1, 4):
                deliver_copy(buf, out, core, which, k).wait_send()
                landed(core, k)
            for k in range(4):
                landed(1 - core, k)

        @pl.when(s != core)
        def _():
            for k in range(4):
                deliver_copy(buf, out, core, which, k).wait_send()


    sends = []

    def mult(x, by):
        return pl.multiple_of(x * by, by)

    def slot(place_at):
        return pl.ds(mult(place_at, SEQ), SEQ)

    ring_got = [None] * 5

    def ring_start(g, src):
        axis = RING_AXIS[g]
        here = ra.at[g, slot(place[axis])]
        own = pltpu.make_async_copy(src, here, wk_sem.at[g])
        own.start()
        copies = [
            push(src, here, rgs_sem.at[g, k], rgr_sem.at[g, k], along(axis, k, s)) for k in range(1, 4)
        ]
        for copy in copies:
            copy.start()
        sends.extend(copies)
        ring_got[g] = [own, copies]

    in_work = [None, None]

    def ring_load(g):
        if in_work[0] == g:
            return
        ring_got[g][0].wait()
        for copy in ring_got[g][1]:
            copy.wait_recv()
        copy = pltpu.make_async_copy(ra.at[g], work, wk_sem.at[5 + g])
        copy.start()
        in_work[0] = g
        in_work[1] = copy

    def ring_use(g):
        ring_load(g)
        if in_work[1] is not None:
            in_work[1].wait()
            in_work[1] = None


    full = {QKV: f_qkv, AO: f_ao, IN: f_in, RO: f_ro, MISC: f_misc}
    owner = {G1: 0, U1: 0, D1: 0, G2: 1, U2: 1, D2: 1}
    items = []
    for i in range(11):
        it = Item()
        it.i = i
        it.style, it.total, it.axis = PLAN[i]
        it.n8 = it.total // 8
        it.m = place[it.axis]
        it.n = place[1 - it.axis]
        it.cr, it.got, it.fin = crs[i], gots[i], fins[i]
        it.acc = a_d2 if i == D2 else s_d.at[1, ROOM[i] : ROOM[i] + it.n8]
        if i in owner:
            it.full = f_ffn.at[(s if owner[i] == 0 else 1 - s) * 3 + i % 3]
            it.home = f_ffn.at[i % 3]
        else:
            it.full = full[i]
            it.home = full[i]
        it.waits = []
        items.append(it)

    def spread(i, which, source, target):
        it = items[i]
        for k in range(1, 4):
            copy = push(
                source(pos(it.m, k)), target(k), xs_sem.at[i, which, k], xr_sem.at[i, which, k],
                along(it.axis, k, s),
            )
            copy.start()
            sends.append(copy)
            it.waits.append(copy)

    def spread_rows(i, whole, into):
        it = items[i]

        def part(f):
            return whole.at[pl.ds(mult(f, 2 * it.n8), 2 * it.n8), :]

        into[:, slot(it.m)] = part(it.m)[...]
        spread(i, 0, part, lambda k: into.at[:, slot(it.m)])

    def spread_left(i, whole, into):
        it = items[i]
        into[:, slot(it.m)] = whole[...]
        spread(i, 0, lambda f: whole, lambda k: into.at[:, slot(it.m)])

    def spread_cols(i, src, into):
        it = items[i]

        def cut(f):
            return pl.ds(mult(f, CC), CC)

        into[slot(it.m), :] = src[:, cut(it.m)]
        spread(i, 1, lambda f: src.at[:, cut(f)], lambda k: into.at[slot(it.m), :])

    def arrived(it):
        for copy in it.waits:
            copy.wait_recv()
        it.waits = []

    def settle(it):
        for copy in it.waits:
            copy.wait()
        it.waits = []

    def piece(it, q):
        return it.acc.at[:, pl.ds(mult(q, CC), CC)]

    cs_busy = [None, None]
    cs_count = [0]

    def halves(i, fill):
        it = items[i]
        at = cs_count[0] % 2
        cs_count[0] += 1
        if cs_busy[at] is not None:
            cs_busy[at].wait_send()
        out = cs.at[at, : it.n8]
        fill(1 - s, out)
        copy = push(out, it.cr, cs_sem.at[i], cr_sem.at[i], other)
        copy.start()
        cs_busy[at] = copy
        it.swap = copy
        fill(s, it.acc)

    def rows_product(i, ring, left):
        it = items[i]
        arrived(it)
        ring_use(ring)

        def fill(h, ref):
            rows = left[pl.ds(mult(h, it.n8), it.n8), :]
            for j in range(4):
                cols = slice(j * CC, j * CC + CC)
                ref[:, cols] = mm(rows, work[:, cols]).astype(BF)

        halves(i, fill)

    def cols_product(i, left, right):
        it = items[i]
        arrived(it)

        def fill(h, ref):
            for q in range(4):
                rows = left[pl.ds(mult(h * 4 + q, it.n8), it.n8), :]
                ref[:, q * CC : q * CC + CC] = mm(rows, right[...]).astype(BF)

        halves(i, fill)

    def misc_sum():
        it = items[MISC]
        arrived(it)

        def fill(h, ref):
            at = pl.ds(mult(h, it.n8), it.n8)
            total = l_misc[0, at, :].astype(F32)
            for k in range(1, 4):
                total = total + l_misc[k, at, :].astype(F32)
            ref[...] = total.astype(BF)

        halves(MISC, fill)

    row_items = {
        G1: (RN2, l_g1), U1: (RN2, l_u1), G2: (RN2B, l_g2), U2: (RN2B, l_u2),
        D2: (RCOT, l_d2), QKV: (RNA, l_qkv), IN: (RN1, l_in),
    }
    col_items = {D1: (la1, rc1), AO: (la_a, rc_a), RO: (la_o, rc_o)}

    def e1(i):
        if i in row_items:
            rows_product(i, *row_items[i])
        elif i in col_items:
            cols_product(i, *col_items[i])
        else:
            misc_sum()

    def e2(i):
        it = items[i]
        it.swap.wait_recv()
        it.acc[...] = (it.acc[...].astype(F32) + it.cr[...].astype(F32)).astype(BF)
        for k in range(1, 4):
            copy = push(
                piece(it, pos(it.n, k)), it.got.at[k - 1], ys_sem.at[it.i, k], yr_sem.at[it.i, k],
                along(1 - it.axis, k, s),
            )
            copy.start()
            it.waits.append(copy)

    def rect(it, ref, f, q):
        if it.style == "r":
            return ref.at[pl.ds(mult(f * 2 + s, it.n8), it.n8), pl.ds(mult(q, CC), CC)]
        return ref.at[pl.ds(mult(s * 4 + q, it.n8), it.n8), pl.ds(mult(f, CC), CC)]

    def quarter(it, ref, f, part=None):
        if it.style == "r":
            rows = pl.ds(mult(f * 2 + s, it.n8), it.n8)
            if part is None:
                return ref.at[rows, :]
            return ref.at[rows, part * HW : part * HW + HW]
        cols = pl.ds(mult(f, CC), CC)
        if part is None:
            return ref.at[pl.ds(mult(s, 4 * it.n8), 4 * it.n8), cols]
        return ref.at[pl.ds(mult(s * 2 + part, 2 * it.n8), 2 * it.n8), cols]

    def e3(i):
        it = items[i]
        settle(it)
        total = piece(it, it.n)[...].astype(F32)
        for k in range(3):
            total = total + it.got[k].astype(F32)
        it.fin[...] = total.astype(BF)
        spot = rect(it, it.full, it.m, it.n)
        for k in range(1, 4):
            copy = push(
                it.fin, spot, gs_sem.at[i, k], gr_sem.at[i, k], along(1 - it.axis, k, s)
            )
            copy.start()
            it.waits.append(copy)
        own = pltpu.make_async_copy(it.fin, spot, loc_sem.at[i])
        own.start()
        it.waits.append(own)

    def both_ways(it, at, right, left):
        for side, part in ((1, right), (3, left)):
            copy = push(
                part, part, gs_sem.at[it.i, at + side // 2], gr_sem.at[it.i, at + side // 2],
                along(it.axis, side, s),
            )
            copy.start()
            it.waits.append(copy)

    def e4(i):
        it = items[i]
        settle(it)
        part = quarter(it, it.full, it.m)
        both_ways(it, 4, part, part)

    def e5(i):
        it = items[i]
        settle(it)
        both_ways(
            it, 6, quarter(it, it.full, pos(it.m, 3), 0), quarter(it, it.full, pos(it.m, 1), 1)
        )

    def to_other(it):
        if it.style == "c":
            rows = [pl.ds(mult(s, 4 * it.n8), 4 * it.n8)]
        else:
            rows = [pl.ds(mult(f * 2 + s, it.n8), it.n8) for f in range(4)]
        cols = pl.ds(0, D)
        if it.i in (QKV, AO, IN, RO):
            cols = pl.ds(mult(1 - s, HW), HW)
        return [
            push(
                it.full.at[r, cols], it.home.at[r, cols],
                gs_sem.at[it.i, 8 + j], gr_sem.at[it.i, 8 + j], other,
            )
            for j, r in enumerate(rows)
        ]

    def e6(i):
        it = items[i]
        settle(it)
        if i in owner:

            @pl.when(s != owner[i])
            def _():
                for copy in to_other(it):
                    copy.start()
        else:
            for copy in to_other(it):
                copy.start()

    def e7(i):
        it = items[i]
        if i in owner:

            @pl.when(s != owner[i])
            def _():
                for copy in to_other(it):
                    copy.wait_send()

            @pl.when(s == owner[i])
            def _():
                for copy in to_other(it):
                    copy.wait_recv()
        else:
            for copy in to_other(it):
                copy.wait()

    def gain(block, which):
        return s_sm[block, which : which + 1, :]

    rows = lax.broadcasted_iota(jnp.int32, (SEQ, RQ), 0)
    part = [slice(0, 16), slice(16, 32)]

    first = plan_ref[0, s] == 0
    x_s[...] = jnp.where(first, tok_ref[:SEQ, :], tok_ref[SEQ:, :])
    cot_at = pl.ds(mult(s, SEQ), SEQ)
    ring_start(RCOT, cot_ref.at[cot_at])
    weights(0, 1)
    n1 = rms(x_s[...].astype(F32), gain(0, 0)).astype(BF)
    n1_s[...] = n1
    ring_start(RN1, n1_s)
    uv_s[...] = mm(n1, s_in[...])
    taps = [s_sm[k // 2, 2 + k % 2 : 3 + k % 2, :RQ] for k in range(4)]
    vec = [s_sm[k // 2, 2 + k % 2 : 3 + k % 2, RQ : 2 * RQ] for k in range(4)]
    u = uv_s[:, :RQ]
    c = vec[0] + taps[0] * u
    for k in range(1, 4):
        c = c + taps[k] * rows_back(u, rows, k)
    c_s[...] = c
    weights(2, 3)
    for head in range(4):
        cols = slice(head * HD, head * HD + HD)
        cb = c_s[:, cols].astype(BF)
        ig_s[:, cols] = sigmoid(mm(cb, s_gt[:, cols]) + vec[1][:, cols])
        rg_s[:, cols] = sigmoid(
            mm(cb, s_gt[:, RQ + head * HD : RQ + head * HD + HD]) + vec[2][:, cols]
        )
    speed = softplus(vec[3])
    a = jnp.exp(-8.0 * rg_s[...] * speed)
    a_s[...] = a
    run = jnp.sqrt(jnp.maximum(1.0 - a * a, RATE_FLOOR)) * ig_s[...] * c_s[...]
    step = 1
    while step < SEQ:
        run = run + a * rows_back(run, rows, step)
        if 2 * step < SEQ:
            a = a * jnp.where(rows >= step, pltpu.roll(a, step, 0), 1.0)
        step *= 2
    h_s[...] = run
    o = (run * gelu(uv_s[:, RQ:])).astype(BF)
    for half in range(2):
        sb[0, :, half * HW : half * HW + HW] = mm(o, s_ro[half]).astype(BF)
    scatter_start(0)
    o_t[...] = o.T
    spread_left(RO, o_t, la_o)
    for h in range(2):
        x1 = x_s[mine[h], :].astype(F32) + scatter_wait(0, h)
        res[0, part[h]] = x1
        gather_start(0, h, rms(x1, gain(0, 1)))

    def ffn_forward(block, p_in, p_out):
        n2 = ag[p_in]
        for j in range(3):
            cols = slice(j * CC, j * CC + CC)
            gate = mm(n2, s_g[block, :, cols])
            up = mm(n2, s_u[block, :, cols])
            gate_s[block, :, cols] = gate
            up_s[block, :, cols] = up
            hid_s[:, cols] = (gelu(gate) * up).astype(BF)
        if block == 0:
            weights(6)
        hid = hid_s[...]
        for j in range(4):
            cols = slice(j * CC, j * CC + CC)
            sb[p_out % 2, :, cols] = mm(hid, s_d[block, :, cols]).astype(BF)
        scatter_start(p_out)
        hid_t[block] = hid_s[...].T

    weights(4, 5)
    gather_wait(0)
    ring_start(RN2, ag.at[0])
    ffn_forward(0, 0, 1)
    spread_left(D1, hid_t.at[0], la1)
    for h in range(2):
        mid = (res[0, part[h]] + scatter_wait(1, h)).astype(BF).astype(F32)
        res[1, part[h]] = mid
        gather_start(1, h, rms(mid, gain(1, 0)))
    weights(7, 8, 9)

    gather_wait(1)
    ring_start(RNA, ag.at[1])
    na = ag[1]
    q_s[...] = mm(na, s_q[...]).astype(BF)
    kv_s[...] = mm(na, s_kv[...]).astype(BF)
    keys = kv_s[:, :HD]
    vals = kv_s[:, HD:]
    allowed = lax.broadcasted_iota(jnp.int32, (SEQ, SEQ), 1) <= lax.broadcasted_iota(
        jnp.int32, (SEQ, SEQ), 0
    )
    for head in range(3):
        cols = slice(head * HD, head * HD + HD)
        score = jnp.where(allowed, mm_nt(q_s[:, cols], keys) * HD ** (-0.5), -1e30)
        expo = jnp.exp(score - jnp.max(score, -1, keepdims=True))
        p = expo / jnp.sum(expo, -1, keepdims=True)
        p_s[head] = p
        at_s[:, cols] = mm(p.astype(BF), vals).astype(BF)
    att = at_s[...]
    for half in range(2):
        sb[0, :, half * HW : half * HW + HW] = mm(att, s_ao[half]).astype(BF)
    scatter_start(2)
    att_t[...] = att.T
    spread_left(AO, att_t, la_a)
    for h in range(2):
        x1 = res[1, part[h]] + scatter_wait(2, h)
        res[2, part[h]] = x1
        gather_start(2, h, rms(x1, gain(1, 1)))
    gather_wait(2)
    ring_start(RN2B, ag.at[2])
    ffn_forward(1, 2, 3)
    spread_rows(D2, hid_t.at[1], l_d2)
    ring_load(RCOT)
    for h in range(2):
        yb[part[h], :] = (res[2, part[h]] + scatter_wait(3, h)).astype(BF)
    deliver(yb, y_o, 1, 0)

    def ffn_backward(block, dF, p_out):
        for j in range(3):
            cols = slice(j * CC, j * CC + CC)
            dhid = mm_nt(dF, s_d[block, cols, :])
            value, slope = gelu_both(gate_s[block, :, cols])
            hid_s[:, cols] = (dhid * up_s[block, :, cols] * slope).astype(BF)
            du_s[:, cols] = (dhid * value).astype(BF)
        dg = hid_s[...]
        du = du_s[...]
        for j in range(4):
            cols = slice(j * CC, j * CC + CC)
            sb[p_out % 2, :, cols] = (
                mm_nt(dg, s_g[block, cols, :]) + mm_nt(du, s_u[block, cols, :])
            ).astype(BF)
        scatter_start(p_out)
        g_t[block] = dg.T
        spread_rows(G2 if block else G1, g_t.at[block], l_g2 if block else l_g1)
        u_t[block] = du.T
        spread_rows(U2 if block else U1, u_t.at[block], l_u2 if block else l_u1)

    cot = cot_ref[cot_at, :]
    ffn_backward(1, cot, 4)
    e1(D2)
    e2(D2)
    gg11 = []
    for h in range(2):
        dv, gg = rms_back(res[2, part[h]], gain(1, 1), scatter_wait(4, h))
        gg11.append(gg)
        own = pl.ds(pl.multiple_of(s * SEQ + t * SH + h * 16, 16), 16)
        dx1 = cot_ref[own, :].astype(F32) + dv
        res[3, part[h]] = dx1
        gather_start(3, h, dx1)
    e1(G2)

    gather_wait(3)
    spread_cols(AO, ag.at[3], rc_a)
    dA = ag[3]
    datt_s = both_s.at[:, :AQ]
    dq_s = both_s.at[:, AQ : 2 * AQ]
    datt_s[...] = (mm_nt(dA[:, :HW], s_ao[0]) + mm_nt(dA[:, HW:], s_ao[1])).astype(BF)
    dk = jnp.zeros((SEQ, HD), F32)
    dw = jnp.zeros((SEQ, HD), F32)
    for head in range(3):
        cols = slice(head * HD, head * HD + HD)
        p = p_s[head]
        datt = datt_s[:, cols]
        dpr = mm_nt(datt, kv_s[:, HD:])
        dw = dw + mm(p.astype(BF).T, datt)
        ds = (p * (dpr - jnp.sum(p * dpr, -1, keepdims=True)) * HD ** (-0.5)).astype(BF)
        dq_s[:, cols] = mm(ds, kv_s[:, :HD]).astype(BF)
        dk = dk + mm(ds.T, q_s[:, cols])
    dkvb[0, :, :HD] = dk.astype(BF)
    dkvb[0, :, HD:] = dw.astype(BF)
    kv_copies = [
        push(dkvb.at[0], dkvb.at[k], kvs_sem.at[k], kvr_sem.at[k], (s, peers[k], d))
        for k in range(1, 4)
    ]
    for copy in kv_copies:
        copy.start()
    dq = dq_s[...]
    for j in range(4):
        cols = slice(j * CC, j * CC + CC)
        sb[1, :, cols] = mm_nt(dq, s_q[cols, :]).astype(BF)
    scatter_start(5)
    e2(G2)
    e1(U2)
    ring_load(RNA)
    e3(D2)
    e1(AO)
    for copy in kv_copies:
        copy.wait()
    total = dkvb[0].astype(F32)
    for k in range(1, 4):
        total = total + dkvb[k].astype(F32)
    dkv_s = both_s.at[:, 2 * AQ : 2 * AQ + 256]
    dkv_s[...] = total.astype(BF)
    qkv_t[:AQ] = dq_s[...].T
    qkv_t[AQ:] = dkv_s[...].T
    spread_rows(QKV, qkv_t, l_qkv)
    e2(U2)
    gg10 = []
    for h in range(2):
        dn = scatter_wait(5, h) + mm_nt(dkv_s[mine[h], :], s_kv[...])
        dv, gg = rms_back(res[1, part[h]], gain(1, 0), dn)
        gg10.append(gg)
        big_g = (res[3, part[h]] + dv).astype(BF)
        gather_start(4, h, big_g)
        res[3, part[h]] = big_g.astype(F32)
    e2(AO)
    e3(G2)
    e4(D2)
    e1(QKV)
    ring_load(RN2)
    gather_wait(4)
    spread_cols(D1, ag.at[4], rc1)
    ffn_backward(0, ag[4], 6)
    e3(AO)
    e2(QKV)
    e3(U2)
    e1(D1)
    e4(G2)
    e4(AO)
    gg01 = []
    for h in range(2):
        dv, gg = rms_back(res[0, part[h]], gain(0, 1), scatter_wait(6, h))
        gg01.append(gg)
        dx1 = res[3, part[h]] + dv
        res[3, part[h]] = dx1
        gather_start(5, h, dx1)
    e2(D1)
    e3(QKV)

    gather_wait(5)
    spread_cols(RO, ag.at[5], rc_o)
    dA = ag[5]
    dO = mm_nt(dA[:, :HW], s_ro[0]) + mm_nt(dA[:, HW:], s_ro[1])
    value, slope = gelu_both(uv_s[:, RQ:])
    h = h_s[...]
    both_s[:, RQ:] = (dO * h * slope).astype(BF)
    e = dO * value
    a = a_s[...]
    coef = rows_ahead(a, rows, 1)
    step = 1
    while step < SEQ:
        e = e + coef * rows_ahead(e, rows, step)
        if 2 * step < SEQ:
            coef = coef * rows_ahead(coef, rows, step)
        step *= 2
    ig = ig_s[...]
    rg = rg_s[...]
    c = c_s[...]
    room = 1.0 - a * a
    m = jnp.sqrt(jnp.maximum(room, RATE_FLOOR))
    ga = e * rows_back(h, rows, 1) - jnp.where(room > RATE_FLOOR, e * ig * c * a / m, 0.0)
    dl = ga * a
    gv3 = jnp.sum(dl * rg, 0, keepdims=True) * (-8.0) * sigmoid(vec[3])
    er = -8.0 * dl * speed * rg * (1.0 - rg)
    ei = e * m * c * ig * (1.0 - ig)
    gv1 = jnp.sum(ei, 0, keepdims=True)
    gv2 = jnp.sum(er, 0, keepdims=True)
    c_s[...] = e * m * ig
    ig_s[...] = ei
    rg_s[...] = er
    for head in range(4):
        cols = slice(head * HD, head * HD + HD)
        late = slice(RQ + head * HD, RQ + head * HD + HD)
        dpin = ig_s[:, cols].astype(BF)
        dprec = rg_s[:, cols].astype(BF)
        cbt = c[:, cols].astype(BF).T
        misc_t[:, cols] = mm(cbt, dpin).astype(BF)
        misc_t[:, late] = mm(cbt, dprec).astype(BF)
        c_s[:, cols] += mm_nt(dpin, s_gt[:, cols]) + mm_nt(dprec, s_gt[:, late])
    dc = c_s[...]
    u = uv_s[:, :RQ]
    du = taps[0] * dc
    gtap = [jnp.sum(u * dc, 0, keepdims=True)]
    for k in range(1, 4):
        du = du + taps[k] * rows_ahead(dc, rows, k)
        gtap.append(jnp.sum(rows_back(u, rows, k) * dc, 0, keepdims=True))
    gv0 = jnp.sum(dc, 0, keepdims=True)
    both_s[:, :RQ] = du.astype(BF)
    both = both_s[...]
    for j in range(4):
        cols = slice(j * CC, j * CC + CC)
        sb[1, :, cols] = mm_nt(both, s_in[cols, :]).astype(BF)
    scatter_start(7)
    in_t[...] = both.T
    spread_rows(IN, in_t, l_in)
    e5(D2)
    e5(G2)
    e1(G1)
    e4(QKV)
    gg00 = []
    for h in range(2):
        dv, gg = rms_back(x_s[mine[h], :].astype(F32), gain(0, 0), scatter_wait(7, h))
        gg00.append(gg)
        xb[part[h], :] = (res[3, part[h]] + dv).astype(BF)
    deliver(xb, dx_o, 0, 1)
    gnb[0, 0:1] = gg00[0] + gg00[1]
    gnb[0, 1:2] = gg01[0] + gg01[1]
    gnb[0, 2:3] = gg10[0] + gg10[1]
    gnb[0, 3:4] = gg11[0] + gg11[1]
    gnb[0, 4:8] = jnp.zeros((4, D), F32)
    gn_copies = [
        push(gnb.at[0], gnb.at[k], gns_sem.at[k], gnr_sem.at[k], (s, peers[k], d))
        for k in range(1, 4)
    ]
    for copy in gn_copies:
        copy.start()
    e1(U1)
    ring_load(RN1)
    e2(G1)
    e1(RO)
    e2(U1)
    for copy in gn_copies:
        copy.wait()
    gains = gnb[0] + gnb[1] + gnb[2] + gnb[3]
    small = gtap + [gv0, gv1, gv2, gv3]
    for g in range(4):
        for part in range(3):
            small.append(gains[g : g + 1, part * RQ : part * RQ + RQ])
    small.append(jnp.zeros((HD - len(small), RQ), F32))
    misc_t[:, 2 * RQ :] = jnp.concatenate(small, 0).astype(BF)
    it = items[MISC]

    def misc_rows(f):
        return misc_t.at[pl.ds(mult(f, 32), 32), :]

    l_misc[0] = misc_rows(it.m)[...]
    spread(MISC, 0, misc_rows, lambda k: l_misc.at[k])
    e4(U2)
    e2(RO)
    e1(IN)
    e5(AO)
    e2(IN)
    e6(G2)
    e3(D1)
    e3(G1)
    e6(D2)
    e3(U1)
    e5(QKV)
    e1(MISC)
    e2(MISC)
    e3(RO)
    e5(U2)
    e6(AO)
    e4(G1)
    e3(IN)
    e4(U1)
    e4(D1)
    e3(MISC)
    e6(QKV)
    e4(RO)
    e6(U2)
    e5(G1)
    e5(D1)
    e4(MISC)
    e4(IN)
    e5(RO)
    e6(D1)
    e5(U1)
    e5(IN)
    e6(G1)
    e5(MISC)
    e6(RO)
    e6(U1)
    e6(IN)
    e6(MISC)
    deliver_wait(yb, y_o, 1, 0)
    deliver_wait(xb, dx_o, 0, 1)
    for copy in swap:
        copy.wait_send()
    for copy in sends + cs_busy:
        copy.wait_send()
    for i in (D2, G2, AO, U2, QKV, G1, U1, D1, RO, IN, MISC):
        e7(i)


def whole_call(tokens, plan, cot, gains, conv, vec, weights):
    vm = pl.BlockSpec(memory_space=pltpu.VMEM)
    hbm = pl.BlockSpec(memory_space=pl.ANY)
    V = pltpu.VMEM
    dma = pltpu.SemaphoreType.DMA
    crs, gots, fins = [], [], []
    for i in range(11):
        n8 = PLAN[i][1] // 8
        crs.append(V((n8, D), BF))
        gots.append(V((3, n8, CC), BF))
        fins.append(V((n8, CC), BF))
    shapes = [
        (2, SEQ, D), (2, SEQ, D), (5, 4 * SEQ, D),
        (6, FQ, D), (640, D), (AQ, D), (1024, D), (RQ, D), (HD, D),
    ]
    return pl.pallas_call(
        whole_kernel,
        name="whole",
        out_shape=[jax.ShapeDtypeStruct(shape, BF) for shape in shapes],
        in_specs=[vm, pl.BlockSpec(memory_space=pltpu.SMEM), vm, vm, vm, vm] + [hbm] * 9,
        out_specs=[hbm] * 9,
        scratch_shapes=[
            V((D, 2 * RQ), BF), V((HD, 2 * RQ), BF), V((2, RQ, HW), BF), V((2, 8, D), F32),
            V((2, D, FQ), BF), V((2, D, FQ), BF), V((2, FQ, D), BF),
            V((D, AQ), BF), V((D, 256), BF), V((2, AQ, HW), BF),
            V((6, SEQ, D), BF), V((2, SEQ, D), BF), V((2, 3, SH, D), BF), V((4, SH, D), F32),
            V((SEQ, D), BF), V((SEQ, D), BF), V((SEQ, 2 * RQ), F32),
            V((SEQ, RQ), F32), V((SEQ, RQ), F32), V((SEQ, RQ), F32), V((SEQ, RQ), F32), V((SEQ, RQ), F32),
            V((SEQ, AQ), BF), V((SEQ, 256), BF), V((3, SEQ, SEQ), F32), V((SEQ, AQ), BF),
            V((2, SEQ, FQ), F32), V((2, SEQ, FQ), F32), V((SEQ, FQ), BF),
            V((SEQ, FQ), BF), V((SEQ, 2 * RQ), BF),
            V((4, SEQ, 256), BF), V((4, 8, D), F32), V((SH, D), BF), V((SH, D), BF), V((8, D), F32),
            V((4 * SEQ, D), BF), V((2, FQ, SEQ), BF), V((RQ, SEQ), BF), V((AQ, SEQ), BF),
            V((2, FQ, SEQ), BF), V((2, FQ, SEQ), BF), V((640, SEQ), BF), V((1024, SEQ), BF), V((HD, D), BF),
            V((FQ, 512), BF), V((RQ, 512), BF), V((AQ, 512), BF),
            V((512, CC), BF), V((512, CC), BF), V((512, CC), BF),
            V((288, 512), BF), V((288, 512), BF), V((288, 512), BF), V((288, 512), BF), V((288, 512), BF),
            V((160, 512), BF), V((256, 512), BF), V((4, 32, D), BF),
            V((144, D), BF), V((2, 144, D), BF),
            *crs, *gots, *fins,
            dma((10,)), dma((10,)), dma((10,)), dma((6, 2, 4)), dma((6, 2, 4)), dma((8, 2, 4)), dma((8, 2, 4)),
            dma((4,)), dma((4,)), dma((4,)), dma((4,)), dma((2,)), dma((2, 4)), dma((2, 2, 4)),
            dma((5, 4)), dma((5, 4)), dma((10,)), dma((11, 2, 4)), dma((11, 2, 4)),
            dma((11, 4)), dma((11, 4)), dma((11, 12)), dma((11, 12)), dma((11,)), dma((11,)), dma((11,)),
        ],
        compiler_params=pltpu.CompilerParams(
            collective_id=0, has_side_effects=True, vmem_limit_bytes=63 * 2**20
        ),
    )(tokens, plan, cot, gains, conv, vec, *weights)


def unpack_kernel(
    n_ref, dx, y, ffn, qkv, ao, rin, ro, misc,
    o_bound, o_gain, o_gate, o_up, o_dn, o_in, o_gt, o_conv, o_vec, o_ro, o_q, o_kv, o_ao,
):
    i = pl.program_id(0)
    s = n_ref[0]
    straight = n_ref[1] == 0
    for j in range(2):
        mine = jnp.where(straight, dx[j], dx[1 - j])
        o_bound[0, j * SEQ : j * SEQ + SEQ, :] = jnp.where(s == 0, mine, y[j]).astype(F32)
    o_gate[0] = ffn[0].T.astype(F32)
    o_up[0] = ffn[1].T.astype(F32)
    o_dn[0] = ffn[2].astype(F32)
    part = qkv[...].T.astype(F32)
    o_q[...] = part[:, :AQ]
    o_kv[...] = part[:, AQ:]
    part = rin[...].T.astype(F32)
    o_in[:, 0, :] = part[:, :RQ]
    o_in[:, 1, :] = part[:, RQ:]

    @pl.when(i == 0)
    def _():
        o_ao[...] = ao[...].astype(F32)
        o_ro[...] = ro[...].astype(F32)
        rows = pl.ds(pl.multiple_of(s * 64, 64), 64)
        o_gt[:, 0, :] = misc[rows, :RQ].astype(F32)
        o_gt[:, 1, :] = misc[rows, RQ : 2 * RQ].astype(F32)
        small = misc[:32, 2 * RQ :].astype(F32)

        def pick(at, step):
            return jnp.where(s == 0, small[at : at + step], small[at + step : at + 2 * step])

        o_conv[...] = pick(0, 2)
        o_vec[...] = pick(4, 2)
        gains = pick(8, 6)
        for j in range(2):
            for p in range(3):
                o_gain[0, j : j + 1, p * RQ : p * RQ + RQ] = gains[j * 3 + p : j * 3 + p + 1]


def unpack_call(scalars, dx, y, ffn, qkv, ao, rin, ro, misc):
    n = 6
    wide = D // n
    part = HW // n
    sds = jax.ShapeDtypeStruct
    fixed = lambda *zero: (lambda i, s: zero)
    return pl.pallas_call(
        unpack_kernel,
        name="unpack",
        out_shape=[
            sds((1, 2 * SEQ, D), F32), sds((1, 2, D), F32),
            sds((1, D, FQ), F32), sds((1, D, FQ), F32), sds((1, FQ, D), F32),
            sds((HW, 2, RQ), F32), sds((64, 2, RQ), F32), sds((2, RQ), F32), sds((2, RQ), F32),
            sds((RQ, HW), F32), sds((HW, AQ), F32), sds((HW, 256), F32), sds((AQ, HW), F32),
        ],
        grid_spec=pltpu.PrefetchScalarGridSpec(
            num_scalar_prefetch=1,
            grid=(n,),
            in_specs=[
                pl.BlockSpec((2, SEQ, wide), lambda i, s: (0, 0, i)),
                pl.BlockSpec((2, SEQ, wide), lambda i, s: (0, 0, i)),
                pl.BlockSpec((3, FQ, wide), lambda i, s: (0, 0, i)),
                pl.BlockSpec((640, part), lambda i, s: (0, s[0] * n + i)),
                pl.BlockSpec((AQ, HW), lambda i, s: (0, s[0])),
                pl.BlockSpec((1024, part), lambda i, s: (0, s[0] * n + i)),
                pl.BlockSpec((RQ, HW), lambda i, s: (0, s[0])),
                pl.BlockSpec((HD, D), fixed(0, 0)),
            ],
            out_specs=[
                pl.BlockSpec((1, 2 * SEQ, wide), lambda i, s: (0, 0, i)),
                pl.BlockSpec((1, 2, D), fixed(0, 0, 0)),
                pl.BlockSpec((1, wide, FQ), lambda i, s: (0, i, 0)),
                pl.BlockSpec((1, wide, FQ), lambda i, s: (0, i, 0)),
                pl.BlockSpec((1, FQ, wide), lambda i, s: (0, 0, i)),
                pl.BlockSpec((part, 2, RQ), lambda i, s: (i, 0, 0)),
                pl.BlockSpec((64, 2, RQ), fixed(0, 0, 0)),
                pl.BlockSpec((2, RQ), fixed(0, 0)),
                pl.BlockSpec((2, RQ), fixed(0, 0)),
                pl.BlockSpec((RQ, HW), fixed(0, 0)),
                pl.BlockSpec((part, AQ), lambda i, s: (i, 0)),
                pl.BlockSpec((part, 256), lambda i, s: (i, 0)),
                pl.BlockSpec((AQ, HW), fixed(0, 0)),
            ],
        ),
        compiler_params=pltpu.CompilerParams(vmem_limit_bytes=62 * 2**20),
    )(scalars, dx, y, ffn, qkv, ao, rin, ro, misc)


def per_device(
    tokens, plan_order, cotangent, norm_gains, ffn_gate, ffn_up, ffn_down,
    rec_in, rec_gates, rec_conv, rec_vec, rec_out, att_q, att_kv, att_out,
):
    y, dx, _, ffn, qkv, ao, rin, ro, misc = whole_call(
        tokens, plan_order, cotangent, norm_gains, rec_conv, rec_vec,
        (
            rec_in.reshape(HW, 2 * RQ), rec_gates.reshape(64, 2 * RQ), rec_out,
            ffn_gate, ffn_up, ffn_down, att_q, att_kv, att_out,
        ),
    )
    s = lax.axis_index("section").astype(jnp.int32)
    scalars = jnp.stack([s, plan_order[0, 0]])
    return unpack_call(scalars, dx, y, ffn, qkv, ao, rin, ro, misc)


def solution(mesh):
    placed = (
        P("dp", None),
        P("dp", None),
        P("dp", None),
        P("section", None, None),
        P("section", None, "tensor"),
        P("section", None, "tensor"),
        P("section", "tensor", None),
        P("section", None, "tensor"),
        P("section", None, "tensor"),
        P("section", "tensor"),
        P("section", "tensor"),
        P("tensor", "section"),
        P("section", "tensor"),
        P("section", None),
        P("tensor", "section"),
    )
    return jax.shard_map(
        per_device,
        mesh=mesh,
        in_specs=placed,
        out_specs=(
            P("section", "dp", None),
            P("section", None, None),
            P("section", None, "tensor"),
            P("section", None, "tensor"),
            P("section", "tensor", None),
            P("section", None, "tensor"),
            P("section", None, "tensor"),
            P("section", "tensor"),
            P("section", "tensor"),
            P("tensor", "section"),
            P("section", "tensor"),
            P("section", None),
            P("tensor", "section"),
        ),
        check_vma=False,
    )
```

time: 277 us -> 234 us (0.84)
  Pallas kernels: 254 us -> 227 us
  local copies, waits for them, and re-layouts: 17.5 us -> 4.54 us
    pallas_call x1, Pallas kernels: 238 us -> 208 us  [whole_call(): pl.pallas_call(whole_kernel, name='whole', out_shape=[jax.ShapeDtypeStruc...]
    unnamed x12 -> x2, local copies, waits for them, and re-layouts: 10.7 us -> 4.54 us
    reshape x3 -> x0, local copies, waits for them, and re-layouts: 5.27 us -> none  [the longest x1 3.73 us: per_device(): g_in.reshape(HW, 2, RQ)]
    pallas_call x1, Pallas kernels: 16 us -> 18.9 us  [unpack_call(): pl.pallas_call(unpack_kernel, name='unpack', out_shape=[sds((1, 2 * SEQ,...]
where the time goes in v3:
time: 234 us; the launch traced here: 233 us
  Pallas kernels  227 us (97%)
  local copies, waits for them, and re-layouts  4.54 us (2%)
    pallas_call x1, Pallas kernels, whole_call(): pl.pallas_call(whole_kernel, name='whole', out_shape=[jax.ShapeDtypeStruc...  208 us
    pallas_call x1, Pallas kernels, unpack_call(): pl.pallas_call(unpack_kernel, name='unpack', out_shape=[sds((1, 2 * SEQ,...  18.9 us

profile of v3, /device:TPU:1, one launch (start us, length us, event | category | flops | bytes accessed | tf_op | source)
XLA Modules:
  0.0 233.5 jit_solution(2135076215263275645)
XLA Ops:
  0.6 1.3 pad_add_fusion.n_ref
  2.0 1.6 copy.29
  3.5 3.0 %copy.28 = bf16[96,8,2,512]{3,1,2,0:T(8,128)(2,1)} copy(bf16[96,8,2,512]{3,2,1,0:T(2,128)(2,1)} %bitcast.8) | data formatting | bytes 3145728
  6.5 207.9 %whole.1 = (bf16[2,128,1536]{2,1,0:T(8,128)(2,1)}, bf16[2,128,1536]{2,1,0:T(8,128)(2,1)}, bf16[5,512,1536]{2,1,0:T(8,128)(2,1)}, bf16[6,1152,1536]{2,1,0:T(8,128...) custom-call(bf16[256,1536]{1,0:T(8,128)(2,1)} %tok_ref.1, ...), custom_call_target="tpu_custom_call" | custom-call | tf_op jit(solution)/shard_map/whole/pallas_call | solution.py:948
  214.4 18.9 %unpack.1 = (f32[1,256,1536]{2,1,0:T(8,128)}, f32[1,2,1536]{2,1,0:T(2,128)}, f32[1,1536,1152]{2,1,0:T(8,128)}, f32[1,1536,1152]{2,1,0:T(8,128)}, f32[1,1152,1536...) custom-call(s32[2]{0:T(128)} %pad_add_fusion.n_ref, ...), custom_call_target="tpu_custom_call" | custom-call | tf_op jit(solution)/shard_map/unpack/pallas_call | solution.py:1030

commit v4 on v3

--- a/solution.py
+++ b/solution.py
@@ -39,6 +39,7 @@
 }
 RING_AXIS = (X_AXIS, Y_AXIS, Y_AXIS, X_AXIS, Y_AXIS)
 RN1, RN2, RNA, RN2B, RCOT = range(5)
+DIRECT = (U2, D2, AO, MISC,)
 ROOM = {G2: 0, U2: 144, G1: 288, U1: 432, D1: 576, QKV: 720, IN: 800, AO: 928, RO: 976, MISC: 1040}
 
 
@@ -120,7 +121,14 @@
     d = lax.axis_index("dp")
     place = (lax.rem(d, 4), d // 4)
     peers = [lax.rem(t + k, 4) for k in range(4)]
-    mine = [pl.ds(pl.multiple_of(t * SH + h * 16, 16), 16) for h in range(2)]
+    def own_rows(h):
+        return pl.ds(pl.multiple_of(h * 64 + t * 16, 16), 16)
+
+    mine = [own_rows(h) for h in range(2)]
+
+    def half_of(h):
+        return pl.ds(pl.multiple_of(h * 64, 64), 64)
+
 
     def pos(base, k):
         return lax.rem(base + k, 4)
@@ -177,10 +185,12 @@
             swap[i].wait_recv()
 
 
+    sub = [slice(0, 16), slice(16, 32)]
+
     def gather(p, h):
         return [
             push(
-                ag.at[p, mine[h]], ag.at[p, mine[h]], ags_sem.at[p, h, k], agr_sem.at[p, h, k],
+                ag.at[p, own_rows(h)], ag.at[p, own_rows(h)], ags_sem.at[p, h, k], agr_sem.at[p, h, k],
                 (s, peers[k], d),
             )
             for k in (2, 1, 3)
@@ -191,23 +201,22 @@
         for copy in gather(p, h):
             copy.start()
 
-    def gather_wait(p):
-        for h in range(2):
-            for copy in gather(p, h):
-                copy.wait()
+    def gather_wait(p, h):
+        for copy in gather(p, h):
+            copy.wait()
 
     def scatter(p, h):
         return [
             push(
-                sb.at[p % 2, pl.ds(pl.multiple_of(peers[k] * SH + h * 16, 16), 16)],
-                rb.at[p % 2, k - 1, h * 16 : h * 16 + 16],
+                sb.at[p % 2, pl.ds(pl.multiple_of(h * 64 + peers[k] * 16, 16), 16)],
+                rb.at[p % 2, k - 1, pl.ds(pl.multiple_of(h * 16, 16), 16)],
                 rss_sem.at[p, h, k], rsr_sem.at[p, h, k], (s, peers[k], d),
             )
             for k in (2, 1, 3)
         ]
 
-    def scatter_start(p):
-        for h in range(2):
+    def scatter_start(p, *halves):
+        for h in halves:
             for copy in scatter(p, h):
                 copy.start()
 
@@ -219,47 +228,54 @@
             total = total + rb[p % 2, k, h * 16 : h * 16 + 16].astype(F32)
         return total
 
-    whole = pl.ds(pl.multiple_of(t * SH, SH), SH)
+    def deliver_copy(buf, out, core, which, k, h):
+        return push(
+            buf.at[sub[h]], out.at[s, mine[h]], dls_sem.at[which, k, h],
+            dlr_sem.at[which, s, k, h], (core, peers[k], d),
+        )
 
     def deliver(buf, out, core, which):
         @pl.when(s == core)
         def _():
-            own = pltpu.make_async_copy(buf, out.at[s, whole], dl_sem.at[which])
-            own.start()
+            own = [
+                pltpu.make_async_copy(buf.at[sub[h]], out.at[s, mine[h]], dl_sem.at[which, h])
+                for h in range(2)
+            ]
+            for copy in own:
+                copy.start()
             for k in range(1, 4):
-                deliver_copy(buf, out, core, which, k).start()
-            own.wait()
+                for h in range(2):
+                    deliver_copy(buf, out, core, which, k, h).start()
+            for copy in own:
+                copy.wait()
 
         @pl.when(s != core)
         def _():
             for k in range(4):
-                deliver_copy(buf, out, core, which, k).start()
-
-    def deliver_copy(buf, out, core, which, k):
-        return push(
-            buf, out.at[s, whole], dls_sem.at[which, k], dlr_sem.at[which, s, k],
-            (core, peers[k], d),
-        )
+                for h in range(2):
+                    deliver_copy(buf, out, core, which, k, h).start()
 
     def deliver_wait(buf, out, core, which):
-        def landed(sender, k):
+        def landed(sender, k, h):
             push(
-                buf, out.at[sender, whole], dls_sem.at[which, k], dlr_sem.at[which, sender, k],
-                (core, peers[k], d),
+                buf.at[sub[h]], out.at[sender, mine[h]], dls_sem.at[which, k, h],
+                dlr_sem.at[which, sender, k, h], (core, peers[k], d),
             ).wait_recv()
 
-        @pl.when(s == core)
-        def _():
-            for k in range(1, 4):
-                deliver_copy(buf, out, core, which, k).wait_send()
-                landed(core, k)
-            for k in range(4):
-                landed(1 - core, k)
-
-        @pl.when(s != core)
-        def _():
-            for k in range(4):
-                deliver_copy(buf, out, core, which, k).wait_send()
+        for h in range(2):
+
+            @pl.when(s == core)
+            def _(h=h):
+                for k in range(1, 4):
+                    deliver_copy(buf, out, core, which, k, h).wait_send()
+                    landed(core, k, h)
+                for k in range(4):
+                    landed(1 - core, k, h)
+
+            @pl.when(s != core)
+            def _(h=h):
+                for k in range(4):
+                    deliver_copy(buf, out, core, which, k, h).wait_send()
 
 
     sends = []
@@ -272,18 +288,36 @@
 
     ring_got = [None] * 5
 
-    def ring_start(g, src):
+    def ring_make(g, src):
         axis = RING_AXIS[g]
         here = ra.at[g, slot(place[axis])]
-        own = pltpu.make_async_copy(src, here, wk_sem.at[g])
-        own.start()
+        stay = pltpu.make_async_copy(src, here, wk_sem.at[g])
         copies = [
-            push(src, here, rgs_sem.at[g, k], rgr_sem.at[g, k], along(axis, k, s)) for k in range(1, 4)
+            push(src, here, rgs_sem.at[g, k], rgr_sem.at[g, k], along(axis, k, s)) for k in (1, 3)
         ]
-        for copy in copies:
+        sends.extend(copies)
+        ring_got[g] = [stay, copies]
+
+    def ring_go(g):
+        ring_got[g][0].start()
+        for copy in ring_got[g][1]:
             copy.start()
+
+    def ring_start(g, src):
+        ring_make(g, src)
+        ring_go(g)
+
+    def ring_pass(g):
+        axis = RING_AXIS[g]
+        copies = []
+        for j, (side, back) in enumerate(((1, 3), (3, 1))):
+            ring_got[g][1][j].wait_recv()
+            rows = ra.at[g, pl.ds(mult(pos(place[axis], back) * 2 + j, 64), 64)]
+            copy = push(rows, rows, rgs_sem.at[g, 2 * j], rgr_sem.at[g, 2 * j], along(axis, side, s))
+            copy.start()
+            copies.append(copy)
         sends.extend(copies)
-        ring_got[g] = [own, copies]
+        ring_got[g][1] = copies
 
     in_work = [None, None]
 
@@ -441,22 +475,50 @@
         else:
             misc_sum()
 
+    def cut_of(it):
+        return {144: 80, 80: 48, 128: 64, 48: 32, 64: 32}[it.n8]
+
+    def sides(it, at, axis, right, left):
+        for j, (side, (src, dst)) in enumerate(((1, right), (3, left))):
+            copy = push(src, dst, ys_sem.at[it.i, at + j], yr_sem.at[it.i, at + j], along(axis, side, s))
+            copy.start()
+            it.waits.append(copy)
+
     def e2(i):
         it = items[i]
         it.swap.wait_recv()
         it.acc[...] = (it.acc[...].astype(F32) + it.cr[...].astype(F32)).astype(BF)
-        for k in range(1, 4):
-            copy = push(
-                piece(it, pos(it.n, k)), it.got.at[k - 1], ys_sem.at[it.i, k], yr_sem.at[it.i, k],
-                along(1 - it.axis, k, s),
-            )
-            copy.start()
-            it.waits.append(copy)
-
-    def rect(it, ref, f, q):
-        if it.style == "r":
-            return ref.at[pl.ds(mult(f * 2 + s, it.n8), it.n8), pl.ds(mult(q, CC), CC)]
-        return ref.at[pl.ds(mult(s * 4 + q, it.n8), it.n8), pl.ds(mult(f, CC), CC)]
+        if i in DIRECT:
+            for k in range(1, 4):
+                copy = push(
+                    piece(it, pos(it.n, k)), it.got.at[k - 1], ys_sem.at[i, k], yr_sem.at[i, k],
+                    along(1 - it.axis, k, s),
+                )
+                copy.start()
+                it.waits.append(copy)
+            return
+        cut = cut_of(it)
+        far = piece(it, pos(it.n, 2))
+        sides(
+            it, 0, 1 - it.axis, (far.at[:cut], it.got.at[0, :cut]), (far.at[cut:], it.got.at[0, cut:])
+        )
+
+    def e2r(i):
+        it = items[i]
+        if i in DIRECT:
+            return
+        settle(it)
+        cut = cut_of(it)
+        right = piece(it, pos(it.n, 1))
+        left = piece(it, pos(it.n, 3))
+        right[:cut] = (right[:cut].astype(F32) + it.got[0, :cut].astype(F32)).astype(BF)
+        left[cut:] = (left[cut:].astype(F32) + it.got[0, cut:].astype(F32)).astype(BF)
+        sides(it, 2, 1 - it.axis, (right, it.got.at[1]), (left, it.got.at[2]))
+
+    def rect(it, ref, f, q, lo=0, n=None):
+        block, at = (f * 2 + s, q) if it.style == "r" else (s * 4 + q, f)
+        rows = pl.ds(pl.multiple_of(block * it.n8 + lo, 16), n or it.n8)
+        return ref.at[rows, pl.ds(mult(at, CC), CC)]
 
     def quarter(it, ref, f, part=None):
         if it.style == "r":
@@ -473,19 +535,32 @@
         it = items[i]
         settle(it)
         total = piece(it, it.n)[...].astype(F32)
-        for k in range(3):
+        for k in range(3) if i in DIRECT else (1, 2):
             total = total + it.got[k].astype(F32)
         it.fin[...] = total.astype(BF)
         spot = rect(it, it.full, it.m, it.n)
-        for k in range(1, 4):
-            copy = push(
-                it.fin, spot, gs_sem.at[i, k], gr_sem.at[i, k], along(1 - it.axis, k, s)
-            )
-            copy.start()
-            it.waits.append(copy)
         own = pltpu.make_async_copy(it.fin, spot, loc_sem.at[i])
         own.start()
         it.waits.append(own)
+        if i in DIRECT:
+            for k in range(1, 4):
+                copy = push(
+                    it.fin, spot, gs_sem.at[i, k], gr_sem.at[i, k], along(1 - it.axis, k, s)
+                )
+                copy.start()
+                it.waits.append(copy)
+            return
+        sides(it, 4, 1 - it.axis, (it.fin, spot), (it.fin, spot))
+
+    def e3r(i):
+        it = items[i]
+        if i in DIRECT:
+            return
+        settle(it)
+        cut = cut_of(it)
+        left = rect(it, it.full, it.m, pos(it.n, 3), 0, cut)
+        right = rect(it, it.full, it.m, pos(it.n, 1), cut, it.n8 - cut)
+        sides(it, 6, 1 - it.axis, (left, left), (right, right))
 
     def both_ways(it, at, right, left):
         for side, part in ((1, right), (3, left)):
@@ -559,7 +634,6 @@
         return s_sm[block, which : which + 1, :]
 
     rows = lax.broadcasted_iota(jnp.int32, (SEQ, RQ), 0)
-    part = [slice(0, 16), slice(16, 32)]
 
     first = plan_ref[0, s] == 0
     x_s[...] = jnp.where(first, tok_ref[:SEQ, :], tok_ref[SEQ:, :])
@@ -599,114 +673,137 @@
     o = (run * gelu(uv_s[:, RQ:])).astype(BF)
     for half in range(2):
         sb[0, :, half * HW : half * HW + HW] = mm(o, s_ro[half]).astype(BF)
-    scatter_start(0)
+    scatter_start(0, 0, 1)
     o_t[...] = o.T
     spread_left(RO, o_t, la_o)
     for h in range(2):
         x1 = x_s[mine[h], :].astype(F32) + scatter_wait(0, h)
-        res[0, part[h]] = x1
+        res[0, sub[h]] = x1
         gather_start(0, h, rms(x1, gain(0, 1)))
 
-    def ffn_forward(block, p_in, p_out):
-        n2 = ag[p_in]
-        for j in range(3):
-            cols = slice(j * CC, j * CC + CC)
-            gate = mm(n2, s_g[block, :, cols])
-            up = mm(n2, s_u[block, :, cols])
-            gate_s[block, :, cols] = gate
-            up_s[block, :, cols] = up
-            hid_s[:, cols] = (gelu(gate) * up).astype(BF)
-        if block == 0:
-            weights(6)
-        hid = hid_s[...]
-        for j in range(4):
-            cols = slice(j * CC, j * CC + CC)
-            sb[p_out % 2, :, cols] = mm(hid, s_d[block, :, cols]).astype(BF)
-        scatter_start(p_out)
+    def ffn_forward(block, p_in, p_out, ring):
+        ring_make(ring, ag.at[p_in])
+
+        def one(h, carry):
+            gather_wait(p_in, h)
+            half = half_of(h)
+            n2 = ag[p_in, half, :]
+
+            @pl.when(h == 1)
+            def _():
+                ring_go(ring)
+
+            for j in range(3):
+                cols = slice(j * CC, j * CC + CC)
+                gate = mm(n2, s_g[block, :, cols])
+                up = mm(n2, s_u[block, :, cols])
+                gate_s[block, half, cols] = gate
+                up_s[block, half, cols] = up
+                hid_s[half, cols] = (gelu(gate) * up).astype(BF)
+            if block == 0:
+
+                @pl.when(h == 0)
+                def _():
+                    weights(6)
+
+            hid = hid_s[half, :]
+            for j in range(4):
+                cols = slice(j * CC, j * CC + CC)
+                sb[p_out % 2, half, cols] = mm(hid, s_d[block, :, cols]).astype(BF)
+            scatter_start(p_out, h)
+            return carry
+
+        lax.fori_loop(0, 2, one, 0)
         hid_t[block] = hid_s[...].T
 
     weights(4, 5)
-    gather_wait(0)
-    ring_start(RN2, ag.at[0])
-    ffn_forward(0, 0, 1)
+    ffn_forward(0, 0, 1, RN2)
     spread_left(D1, hid_t.at[0], la1)
+    ring_pass(RCOT)
+    ring_pass(RN1)
     for h in range(2):
-        mid = (res[0, part[h]] + scatter_wait(1, h)).astype(BF).astype(F32)
-        res[1, part[h]] = mid
+        mid = (res[0, sub[h]] + scatter_wait(1, h)).astype(BF).astype(F32)
+        res[1, sub[h]] = mid
         gather_start(1, h, rms(mid, gain(1, 0)))
     weights(7, 8, 9)
 
-    gather_wait(1)
-    ring_start(RNA, ag.at[1])
-    na = ag[1]
-    q_s[...] = mm(na, s_q[...]).astype(BF)
-    kv_s[...] = mm(na, s_kv[...]).astype(BF)
-    keys = kv_s[:, :HD]
-    vals = kv_s[:, HD:]
-    allowed = lax.broadcasted_iota(jnp.int32, (SEQ, SEQ), 1) <= lax.broadcasted_iota(
-        jnp.int32, (SEQ, SEQ), 0
-    )
-    for head in range(3):
-        cols = slice(head * HD, head * HD + HD)
-        score = jnp.where(allowed, mm_nt(q_s[:, cols], keys) * HD ** (-0.5), -1e30)
-        expo = jnp.exp(score - jnp.max(score, -1, keepdims=True))
-        p = expo / jnp.sum(expo, -1, keepdims=True)
-        p_s[head] = p
-        at_s[:, cols] = mm(p.astype(BF), vals).astype(BF)
+    p_s[:, :64, 64:] = jnp.zeros((3, 64, 64), F32)
+    for h in range(2):
+        gather_wait(1, h)
+        if h == 1:
+            ring_start(RNA, ag.at[1])
+        half = slice(h * 64, h * 64 + 64)
+        n = 64 * h + 64
+        na = ag[1, half]
+        q_s[half] = mm(na, s_q[...]).astype(BF)
+        kv_s[half] = mm(na, s_kv[...]).astype(BF)
+        keys = kv_s[:n, :HD]
+        vals = kv_s[:n, HD:]
+        col = lax.broadcasted_iota(jnp.int32, (64, n), 1)
+        row = lax.broadcasted_iota(jnp.int32, (64, n), 0) + 64 * h
+        for head in range(3):
+            cols = slice(head * HD, head * HD + HD)
+            score = jnp.where(col <= row, mm_nt(q_s[half, cols], keys) * HD ** (-0.5), -1e30)
+            expo = jnp.exp(score - jnp.max(score, -1, keepdims=True))
+            p = expo / jnp.sum(expo, -1, keepdims=True)
+            p_s[head, half, :n] = p
+            at_s[half, cols] = mm(p.astype(BF), vals).astype(BF)
+        for c in range(2):
+            sb[0, half, c * HW : c * HW + HW] = mm(at_s[half], s_ao[c]).astype(BF)
+        scatter_start(2, h)
     att = at_s[...]
-    for half in range(2):
-        sb[0, :, half * HW : half * HW + HW] = mm(att, s_ao[half]).astype(BF)
-    scatter_start(2)
     att_t[...] = att.T
     spread_left(AO, att_t, la_a)
+    ring_pass(RN2)
     for h in range(2):
-        x1 = res[1, part[h]] + scatter_wait(2, h)
-        res[2, part[h]] = x1
+        x1 = res[1, sub[h]] + scatter_wait(2, h)
+        res[2, sub[h]] = x1
         gather_start(2, h, rms(x1, gain(1, 1)))
-    gather_wait(2)
-    ring_start(RN2B, ag.at[2])
-    ffn_forward(1, 2, 3)
+    ffn_forward(1, 2, 3, RN2B)
     spread_rows(D2, hid_t.at[1], l_d2)
     ring_load(RCOT)
-    for h in range(2):
-        yb[part[h], :] = (res[2, part[h]] + scatter_wait(3, h)).astype(BF)
-    deliver(yb, y_o, 1, 0)
-
-    def ffn_backward(block, dF, p_out):
+
+    def ffn_back_rows(block, half, dF, p_out):
         for j in range(3):
             cols = slice(j * CC, j * CC + CC)
             dhid = mm_nt(dF, s_d[block, cols, :])
-            value, slope = gelu_both(gate_s[block, :, cols])
-            hid_s[:, cols] = (dhid * up_s[block, :, cols] * slope).astype(BF)
-            du_s[:, cols] = (dhid * value).astype(BF)
-        dg = hid_s[...]
-        du = du_s[...]
+            value, slope = gelu_both(gate_s[block, half, cols])
+            hid_s[half, cols] = (dhid * up_s[block, half, cols] * slope).astype(BF)
+            du_s[half, cols] = (dhid * value).astype(BF)
+        dg = hid_s[half, :]
+        du = du_s[half, :]
         for j in range(4):
             cols = slice(j * CC, j * CC + CC)
-            sb[p_out % 2, :, cols] = (
+            sb[p_out % 2, half, cols] = (
                 mm_nt(dg, s_g[block, cols, :]) + mm_nt(du, s_u[block, cols, :])
             ).astype(BF)
-        scatter_start(p_out)
-        g_t[block] = dg.T
+
+    def ffn_back_send(block):
+        g_t[block] = hid_s[...].T
         spread_rows(G2 if block else G1, g_t.at[block], l_g2 if block else l_g1)
-        u_t[block] = du.T
+        u_t[block] = du_s[...].T
         spread_rows(U2 if block else U1, u_t.at[block], l_u2 if block else l_u1)
 
-    cot = cot_ref[cot_at, :]
-    ffn_backward(1, cot, 4)
+    ffn_back_rows(1, pl.ds(0, SEQ), cot_ref[cot_at, :], 4)
+    scatter_start(4, 0, 1)
+    ffn_back_send(1)
+    for h in range(2):
+        yb[sub[h], :] = (res[2, sub[h]] + scatter_wait(3, h)).astype(BF)
+    ring_pass(RNA)
+    ring_pass(RN2B)
     e1(D2)
-    e2(D2)
     gg11 = []
     for h in range(2):
-        dv, gg = rms_back(res[2, part[h]], gain(1, 1), scatter_wait(4, h))
+        dv, gg = rms_back(res[2, sub[h]], gain(1, 1), scatter_wait(4, h))
         gg11.append(gg)
-        own = pl.ds(pl.multiple_of(s * SEQ + t * SH + h * 16, 16), 16)
+        own = pl.ds(pl.multiple_of(s * SEQ + h * 64 + t * 16, 16), 16)
         dx1 = cot_ref[own, :].astype(F32) + dv
-        res[3, part[h]] = dx1
+        res[3, sub[h]] = dx1
         gather_start(3, h, dx1)
-    e1(G2)
-
-    gather_wait(3)
+    e2(D2)
+
+    gather_wait(3, 0)
+    gather_wait(3, 1)
     spread_cols(AO, ag.at[3], rc_a)
     dA = ag[3]
     datt_s = both_s.at[:, :AQ]
@@ -735,12 +832,11 @@
     for j in range(4):
         cols = slice(j * CC, j * CC + CC)
         sb[1, :, cols] = mm_nt(dq, s_q[cols, :]).astype(BF)
-    scatter_start(5)
-    e2(G2)
+    scatter_start(5, 0, 1)
+    e1(G2)
     e1(U2)
     ring_load(RNA)
     e3(D2)
-    e1(AO)
     for copy in kv_copies:
         copy.wait()
     total = dkvb[0].astype(F32)
@@ -751,40 +847,71 @@
     qkv_t[:AQ] = dq_s[...].T
     qkv_t[AQ:] = dkv_s[...].T
     spread_rows(QKV, qkv_t, l_qkv)
+    e1(AO)
+    e2(G2)
     e2(U2)
     gg10 = []
     for h in range(2):
         dn = scatter_wait(5, h) + mm_nt(dkv_s[mine[h], :], s_kv[...])
-        dv, gg = rms_back(res[1, part[h]], gain(1, 0), dn)
+        dv, gg = rms_back(res[1, sub[h]], gain(1, 0), dn)
         gg10.append(gg)
-        big_g = (res[3, part[h]] + dv).astype(BF)
+        big_g = (res[3, sub[h]] + dv).astype(BF)
         gather_start(4, h, big_g)
-        res[3, part[h]] = big_g.astype(F32)
+        res[3, sub[h]] = big_g.astype(F32)
     e2(AO)
-    e3(G2)
-    e4(D2)
     e1(QKV)
     ring_load(RN2)
-    gather_wait(4)
-    spread_cols(D1, ag.at[4], rc1)
-    ffn_backward(0, ag[4], 6)
+    e2r(G2)
+
+    it = items[D1]
+    cols_at = [pl.ds(mult(pos(it.m, k), CC), CC) for k in range(4)]
+    d1_copies = [
+        push(
+            ag.at[4, :, cols_at[k]], rc1.at[slot(it.m), :], xs_sem.at[D1, 1, k], xr_sem.at[D1, 1, k],
+            along(it.axis, k, s),
+        )
+        for k in range(1, 4)
+    ]
+    d1_rows = slot(it.m)
+
+    def back_half(h, carry):
+        gather_wait(4, h)
+
+        @pl.when(h == 1)
+        def _():
+            rc1[d1_rows, :] = ag[4, :, cols_at[0]]
+            for copy in d1_copies:
+                copy.start()
+
+        ffn_back_rows(0, half_of(h), ag[4, half_of(h), :], 6)
+        scatter_start(6, h)
+        return carry
+
+    lax.fori_loop(0, 2, back_half, 0)
+    it.waits += d1_copies
+    sends.extend(d1_copies)
+    ffn_back_send(0)
+    e3(G2)
+    e3(U2)
     e3(AO)
     e2(QKV)
-    e3(U2)
-    e1(D1)
-    e4(G2)
-    e4(AO)
     gg01 = []
     for h in range(2):
-        dv, gg = rms_back(res[0, part[h]], gain(0, 1), scatter_wait(6, h))
+        dv, gg = rms_back(res[0, sub[h]], gain(0, 1), scatter_wait(6, h))
         gg01.append(gg)
-        dx1 = res[3, part[h]] + dv
-        res[3, part[h]] = dx1
+        dx1 = res[3, sub[h]] + dv
+        res[3, sub[h]] = dx1
         gather_start(5, h, dx1)
+    e2r(QKV)
+    e1(D1)
+    e1(G1)
     e2(D1)
     e3(QKV)
-
-    gather_wait(5)
+    e1(U1)
+    ring_load(RN1)
+
+    gather_wait(5, 0)
+    gather_wait(5, 1)
     spread_cols(RO, ag.at[5], rc_o)
     dA = ag[5]
     dO = mm_nt(dA[:, :HW], s_ro[0]) + mm_nt(dA[:, HW:], s_ro[1])
@@ -837,18 +964,22 @@
     for j in range(4):
         cols = slice(j * CC, j * CC + CC)
         sb[1, :, cols] = mm_nt(both, s_in[cols, :]).astype(BF)
-    scatter_start(7)
+    scatter_start(7, 0, 1)
     in_t[...] = both.T
     spread_rows(IN, in_t, l_in)
-    e5(D2)
-    e5(G2)
-    e1(G1)
-    e4(QKV)
+    e3r(QKV)
+    e3r(G2)
+    e2(G1)
+    e2(U1)
+    e4(AO)
+    e1(RO)
+    e2r(D1)
+    e4(U2)
     gg00 = []
     for h in range(2):
         dv, gg = rms_back(x_s[mine[h], :].astype(F32), gain(0, 0), scatter_wait(7, h))
         gg00.append(gg)
-        xb[part[h], :] = (res[3, part[h]] + dv).astype(BF)
+        xb[sub[h], :] = (res[3, sub[h]] + dv).astype(BF)
     deliver(xb, dx_o, 0, 1)
     gnb[0, 0:1] = gg00[0] + gg00[1]
     gnb[0, 1:2] = gg01[0] + gg01[1]
@@ -861,11 +992,16 @@
     ]
     for copy in gn_copies:
         copy.start()
-    e1(U1)
-    ring_load(RN1)
-    e2(G1)
-    e1(RO)
-    e2(U1)
+    e2(RO)
+    e1(IN)
+    e2r(G1)
+    e2r(U1)
+    e4(QKV)
+    e5(AO)
+    e3(D1)
+    e2(IN)
+    e2r(RO)
+    deliver(yb, y_o, 1, 0)
     for copy in gn_copies:
         copy.wait()
     gains = gnb[0] + gnb[1] + gnb[2] + gnb[3]
@@ -882,44 +1018,48 @@
 
     l_misc[0] = misc_rows(it.m)[...]
     spread(MISC, 0, misc_rows, lambda k: l_misc.at[k])
-    e4(U2)
-    e2(RO)
-    e1(IN)
-    e5(AO)
-    e2(IN)
-    e6(G2)
-    e3(D1)
+    e4(G2)
+    e4(D2)
+    e5(QKV)
+    e6(AO)
+    e5(U2)
+    e3r(D1)
     e3(G1)
-    e6(D2)
+    e2r(IN)
+    e3(RO)
     e3(U1)
-    e5(QKV)
     e1(MISC)
     e2(MISC)
-    e3(RO)
-    e5(U2)
-    e6(AO)
+    e5(G2)
+    e5(D2)
+    e6(U2)
+    e6(QKV)
+    e3r(G1)
+    e4(D1)
+    e3r(U1)
+    e3(IN)
+    e3(MISC)
+    e3r(RO)
+    e6(G2)
+    e6(D2)
     e4(G1)
-    e3(IN)
+    e3r(IN)
+    e4(RO)
+    e5(D1)
     e4(U1)
-    e4(D1)
-    e3(MISC)
-    e6(QKV)
-    e4(RO)
-    e6(U2)
+    e4(MISC)
     e5(G1)
-    e5(D1)
-    e4(MISC)
     e4(IN)
     e5(RO)
     e6(D1)
     e5(U1)
+    e5(MISC)
+    e6(G1)
     e5(IN)
-    e6(G1)
-    e5(MISC)
     e6(RO)
     e6(U1)
+    e6(MISC)
     e6(IN)
-    e6(MISC)
     deliver_wait(yb, y_o, 1, 0)
     deliver_wait(xb, dx_o, 0, 1)
     for copy in swap:
@@ -971,9 +1111,9 @@
             V((144, D), BF), V((2, 144, D), BF),
             *crs, *gots, *fins,
             dma((10,)), dma((10,)), dma((10,)), dma((6, 2, 4)), dma((6, 2, 4)), dma((8, 2, 4)), dma((8, 2, 4)),
-            dma((4,)), dma((4,)), dma((4,)), dma((4,)), dma((2,)), dma((2, 4)), dma((2, 2, 4)),
+            dma((4,)), dma((4,)), dma((4,)), dma((4,)), dma((2, 2)), dma((2, 4, 2)), dma((2, 2, 4, 2)),
             dma((5, 4)), dma((5, 4)), dma((10,)), dma((11, 2, 4)), dma((11, 2, 4)),
-            dma((11, 4)), dma((11, 4)), dma((11, 12)), dma((11, 12)), dma((11,)), dma((11,)), dma((11,)),
+            dma((11, 8)), dma((11, 8)), dma((11, 12)), dma((11, 12)), dma((11,)), dma((11,)), dma((11,)),
         ],
         compiler_params=pltpu.CompilerParams(
             collective_id=0, has_side_effects=True, vmem_limit_bytes=63 * 2**20
@@ -1022,7 +1162,7 @@
 
 
 def unpack_call(scalars, dx, y, ffn, qkv, ao, rin, ro, misc):
-    n = 6
+    n = 3
     wide = D // n
     part = HW // n
     sds = jax.ShapeDtypeStruct

time: 234 us -> 227 us (0.970)
  Pallas kernels: 227 us -> 221 us
    pallas_call x1, Pallas kernels: 208 us -> 204 us  [whole_call(): pl.pallas_call(whole_kernel, name='whole', out_shape=[jax.ShapeDtypeStruc...]
where the time goes in v4:
time: 227 us
  Pallas kernels  221 us (97%)
  local copies, waits for them, and re-layouts  4.54 us (2%)
    pallas_call x1, Pallas kernels, whole_call(): pl.pallas_call(whole_kernel, name='whole', out_shape=[jax.ShapeDtypeStruc...  204 us
    pallas_call x1, Pallas kernels, unpack_call(): pl.pallas_call(unpack_kernel, name='unpack', out_shape=[sds((1, 2 * SEQ,...  16.8 us

profile of v4, /device:TPU:1, one launch (start us, length us, event | category | flops | bytes accessed | tf_op | source)
XLA Modules:
  0.0 227.2 jit_solution(6510972607075675819)
XLA Ops:
  0.6 1.3 pad_add_fusion.n_ref
  2.0 1.6 copy.29
  3.5 3.0 %copy.28 = bf16[96,8,2,512]{3,1,2,0:T(8,128)(2,1)} copy(bf16[96,8,2,512]{3,2,1,0:T(2,128)(2,1)} %bitcast.8) | data formatting | bytes 3145728
  6.5 203.7 %whole.1 = (bf16[2,128,1536]{2,1,0:T(8,128)(2,1)}, bf16[2,128,1536]{2,1,0:T(8,128)(2,1)}, bf16[5,512,1536]{2,1,0:T(8,128)(2,1)}, bf16[6,1152,1536]{2,1,0:T(8,128...) custom-call(bf16[256,1536]{1,0:T(8,128)(2,1)} %tok_ref.1, ...), custom_call_target="tpu_custom_call" | custom-call | tf_op jit(solution)/shard_map/whole/pallas_call | solution.py:1088
  210.2 16.8 %unpack.1 = (f32[1,256,1536]{2,1,0:T(8,128)}, f32[1,2,1536]{2,1,0:T(2,128)}, f32[1,1536,1152]{2,1,0:T(8,128)}, f32[1,1536,1152]{2,1,0:T(8,128)}, f32[1,1152,1536...) custom-call(s32[2]{0:T(128)} %pad_add_fusion.n_ref, ...), custom_call_target="tpu_custom_call" | custom-call | tf_op jit(solution)/shard_map/unpack/pallas_call | solution.py:1170

commit v5 on v4

--- a/solution.py
+++ b/solution.py
@@ -39,7 +39,7 @@
 }
 RING_AXIS = (X_AXIS, Y_AXIS, Y_AXIS, X_AXIS, Y_AXIS)
 RN1, RN2, RNA, RN2B, RCOT = range(5)
-DIRECT = (U2, D2, AO, MISC,)
+DIRECT = (U2, QKV, AO, RO, MISC,)
 ROOM = {G2: 0, U2: 144, G1: 288, U1: 432, D1: 576, QKV: 720, IN: 800, AO: 928, RO: 976, MISC: 1040}
 
 
@@ -100,14 +100,14 @@
 def whole_kernel(
     tok_ref, plan_ref, cot_ref, gain_ref, conv_ref, vec_ref,
     win, wgt, wro, wg, wu, wd, wq, wkv, wao,
-    y_o, dx_o, ra, f_ffn, f_qkv, f_ao, f_in, f_ro, f_misc,
+    n_o, y_o, dx_o, ra, f_ffn, f_qkv, f_ao, f_in, f_ro, f_misc,
     s_in, s_gt, s_ro, s_sm, s_g, s_u, s_d, s_q, s_kv, s_ao,
     ag, sb, rb, res, x_s, n1_s, uv_s, c_s, ig_s, rg_s, a_s, h_s,
     q_s, kv_s, p_s, at_s, gate_s, up_s, hid_s, du_s, both_s,
     dkvb, gnb, yb, xb, smb,
     work, hid_t, o_t, att_t, g_t, u_t, qkv_t, in_t, misc_t,
     la1, la_o, la_a, rc1, rc_o, rc_a, l_g1, l_u1, l_g2, l_u2, l_d2, l_qkv, l_in, l_misc,
-    a_d2, cs, *rest,
+    a_d2, cs, raw_in, raw_gt, cot_s, raw_gain, raw_conv, raw_vec, in_sem, *rest,
 ):
     crs, gots, fins = rest[:11], rest[11:22], rest[22:33]
     (
@@ -138,6 +138,14 @@
             return (core, t, place[1] * 4 + pos(place[0], k))
         return (core, t, pos(place[1], k) * 4 + place[0])
 
+    entry = [
+        (win, raw_in), (wgt, raw_gt), (tok_ref, work.at[: 2 * SEQ]), (gain_ref, raw_gain),
+        (conv_ref, raw_conv), (vec_ref, raw_vec),
+        (cot_ref.at[pl.ds(pl.multiple_of(s * SEQ, SEQ), SEQ)], cot_s),
+    ]
+    entry = [pltpu.make_async_copy(a, b, in_sem.at[i]) for i, (a, b) in enumerate(entry)]
+    for copy in entry:
+        copy.start()
     barrier = pltpu.get_barrier_semaphore()
     other = (1 - s, t, d)
     for k in range(1, 4):
@@ -153,16 +161,12 @@
             device_id=target, device_id_type=MESH,
         )
 
-    smb[...] = jnp.zeros((8, D), F32)
-    smb[0:2, :] = gain_ref[0]
-    smb[2:4, :RQ] = conv_ref[...].astype(F32)
-    smb[2:4, RQ : 2 * RQ] = vec_ref[...].astype(F32)
     half_in = pl.ds(pl.multiple_of(s * HW, HW), HW)
     half_gt = pl.ds(pl.multiple_of(s * 64, 64), 64)
     moves = [
-        (win, s_in.at[half_in, :]),
+        (s_in.at[half_in, :], s_in.at[half_in, :]),
         (smb, s_sm.at[s]),
-        (wgt, s_gt.at[half_gt, :]),
+        (s_gt.at[half_gt, :], s_gt.at[half_gt, :]),
         (wro, s_ro.at[s]),
         (wg.at[0], s_g.at[s]),
         (wu.at[0], s_u.at[s]),
@@ -173,15 +177,32 @@
     ]
     local = [pltpu.make_async_copy(a, b, wl_sem.at[i]) for i, (a, b) in enumerate(moves)]
     swap = [push(a, b, ws_sem.at[i], wr_sem.at[i], other) for i, (a, b) in enumerate(moves)]
-    for copy in local:
+    for copy in local[3:]:
         copy.start()
+    entry[0].wait()
+    s_in[half_in, :] = raw_in[...].reshape(HW, 2 * RQ)
+    entry[1].wait()
+    s_gt[half_gt, :] = raw_gt[...].reshape(64, 2 * RQ)
+    for copy in entry[3:6]:
+        copy.wait()
+    smb[...] = jnp.zeros((8, D), F32)
+    smb[0:2, :] = raw_gain[0]
+    smb[2:4, :RQ] = raw_conv[...].astype(F32)
+    smb[2:4, RQ : 2 * RQ] = raw_vec[...].astype(F32)
+    s_sm[s] = smb[...]
+    entry[2].wait()
+    x_s[...] = jnp.where(plan_ref[0, s] == 0, work[:SEQ, :], work[SEQ : 2 * SEQ, :])
+    entry[6].wait()
+    n_o[0] = s
+    n_o[1] = plan_ref[0, 0]
     pl.semaphore_wait(barrier, 13)
-    for copy in swap:
-        copy.start()
+    swap[1].start()
+    swap[0].start()
 
     def weights(*which):
         for i in which:
-            local[i].wait()
+            if i > 2:
+                local[i].wait()
             swap[i].wait_recv()
 
 
@@ -571,11 +592,49 @@
             copy.start()
             it.waits.append(copy)
 
+    def to_other(it, ks):
+        whole_c = it.style == "c" and it.i not in owner
+        copies = []
+        for k in ks:
+            f = pos(it.m, k)
+            if whole_c:
+                if k != 2:
+                    continue
+                rows = pl.ds(mult(s, 4 * it.n8), 4 * it.n8)
+            elif it.style == "c":
+                rows = pl.ds(mult(s, 4 * it.n8), 4 * it.n8)
+            else:
+                rows = pl.ds(mult(f * 2 + s, it.n8), it.n8)
+            cols = pl.ds(0, D)
+            if it.i in (QKV, AO, IN, RO):
+                cols = pl.ds(mult(1 - s, HW), HW)
+            elif it.style == "c":
+                cols = pl.ds(mult(f, CC), CC)
+            copies.append(
+                push(
+                    it.full.at[rows, cols], it.home.at[rows, cols],
+                    gs_sem.at[it.i, 8 + k], gr_sem.at[it.i, 8 + k], other,
+                )
+            )
+        return copies
+
+    def home(it, *ks):
+        if it.i in owner:
+
+            @pl.when(s != owner[it.i])
+            def _():
+                for copy in to_other(it, ks):
+                    copy.start()
+        else:
+            for copy in to_other(it, ks):
+                copy.start()
+
     def e4(i):
         it = items[i]
         settle(it)
         part = quarter(it, it.full, it.m)
         both_ways(it, 4, part, part)
+        home(it, 0)
 
     def e5(i):
         it = items[i]
@@ -583,51 +642,28 @@
         both_ways(
             it, 6, quarter(it, it.full, pos(it.m, 3), 0), quarter(it, it.full, pos(it.m, 1), 1)
         )
-
-    def to_other(it):
-        if it.style == "c":
-            rows = [pl.ds(mult(s, 4 * it.n8), 4 * it.n8)]
-        else:
-            rows = [pl.ds(mult(f * 2 + s, it.n8), it.n8) for f in range(4)]
-        cols = pl.ds(0, D)
-        if it.i in (QKV, AO, IN, RO):
-            cols = pl.ds(mult(1 - s, HW), HW)
-        return [
-            push(
-                it.full.at[r, cols], it.home.at[r, cols],
-                gs_sem.at[it.i, 8 + j], gr_sem.at[it.i, 8 + j], other,
-            )
-            for j, r in enumerate(rows)
-        ]
+        home(it, 3, 1)
 
     def e6(i):
         it = items[i]
         settle(it)
+        home(it, 2)
+
+    def e7(i):
+        it = items[i]
         if i in owner:
 
             @pl.when(s != owner[i])
             def _():
-                for copy in to_other(it):
-                    copy.start()
-        else:
-            for copy in to_other(it):
-                copy.start()
-
-    def e7(i):
-        it = items[i]
-        if i in owner:
-
-            @pl.when(s != owner[i])
-            def _():
-                for copy in to_other(it):
+                for copy in to_other(it, range(4)):
                     copy.wait_send()
 
             @pl.when(s == owner[i])
             def _():
-                for copy in to_other(it):
+                for copy in to_other(it, range(4)):
                     copy.wait_recv()
         else:
-            for copy in to_other(it):
+            for copy in to_other(it, range(4)):
                 copy.wait()
 
     def gain(block, which):
@@ -635,15 +671,16 @@
 
     rows = lax.broadcasted_iota(jnp.int32, (SEQ, RQ), 0)
 
-    first = plan_ref[0, s] == 0
-    x_s[...] = jnp.where(first, tok_ref[:SEQ, :], tok_ref[SEQ:, :])
-    cot_at = pl.ds(mult(s, SEQ), SEQ)
-    ring_start(RCOT, cot_ref.at[cot_at])
-    weights(0, 1)
-    n1 = rms(x_s[...].astype(F32), gain(0, 0)).astype(BF)
-    n1_s[...] = n1
+    ring_start(RCOT, cot_s)
+    weights(1)
+    n1_s[...] = rms(x_s[...].astype(F32), gain(0, 0)).astype(BF)
+    for copy in swap[2:]:
+        copy.start()
     ring_start(RN1, n1_s)
-    uv_s[...] = mm(n1, s_in[...])
+    uv_s[...] = mm(n1_s[:, half_in], s_in[half_in, :])
+    weights(0)
+    half_other = pl.ds(mult(1 - s, HW), HW)
+    uv_s[...] += mm(n1_s[:, half_other], s_in[half_other, :])
     taps = [s_sm[k // 2, 2 + k % 2 : 3 + k % 2, :RQ] for k in range(4)]
     vec = [s_sm[k // 2, 2 + k % 2 : 3 + k % 2, RQ : 2 * RQ] for k in range(4)]
     u = uv_s[:, :RQ]
@@ -784,7 +821,7 @@
         u_t[block] = du_s[...].T
         spread_rows(U2 if block else U1, u_t.at[block], l_u2 if block else l_u1)
 
-    ffn_back_rows(1, pl.ds(0, SEQ), cot_ref[cot_at, :], 4)
+    ffn_back_rows(1, pl.ds(0, SEQ), cot_s[...], 4)
     scatter_start(4, 0, 1)
     ffn_back_send(1)
     for h in range(2):
@@ -796,8 +833,7 @@
     for h in range(2):
         dv, gg = rms_back(res[2, sub[h]], gain(1, 1), scatter_wait(4, h))
         gg11.append(gg)
-        own = pl.ds(pl.multiple_of(s * SEQ + h * 64 + t * 16, 16), 16)
-        dx1 = cot_ref[own, :].astype(F32) + dv
+        dx1 = cot_s[mine[h], :].astype(F32) + dv
         res[3, sub[h]] = dx1
         gather_start(3, h, dx1)
     e2(D2)
@@ -834,9 +870,9 @@
         sb[1, :, cols] = mm_nt(dq, s_q[cols, :]).astype(BF)
     scatter_start(5, 0, 1)
     e1(G2)
+    e2r(D2)
     e1(U2)
     ring_load(RNA)
-    e3(D2)
     for copy in kv_copies:
         copy.wait()
     total = dkvb[0].astype(F32)
@@ -849,7 +885,6 @@
     spread_rows(QKV, qkv_t, l_qkv)
     e1(AO)
     e2(G2)
-    e2(U2)
     gg10 = []
     for h in range(2):
         dn = scatter_wait(5, h) + mm_nt(dkv_s[mine[h], :], s_kv[...])
@@ -858,7 +893,9 @@
         big_g = (res[3, sub[h]] + dv).astype(BF)
         gather_start(4, h, big_g)
         res[3, sub[h]] = big_g.astype(F32)
+    e2(U2)
     e2(AO)
+    e3(D2)
     e1(QKV)
     ring_load(RN2)
     e2r(G2)
@@ -891,10 +928,11 @@
     it.waits += d1_copies
     sends.extend(d1_copies)
     ffn_back_send(0)
+    e3(U2)
     e3(G2)
-    e3(U2)
     e3(AO)
     e2(QKV)
+    e3r(D2)
     gg01 = []
     for h in range(2):
         dv, gg = rms_back(res[0, sub[h]], gain(0, 1), scatter_wait(6, h))
@@ -902,11 +940,12 @@
         dx1 = res[3, sub[h]] + dv
         res[3, sub[h]] = dx1
         gather_start(5, h, dx1)
-    e2r(QKV)
     e1(D1)
     e1(G1)
+    e3(QKV)
+    e4(AO)
     e2(D1)
-    e3(QKV)
+    e4(D2)
     e1(U1)
     ring_load(RN1)
 
@@ -967,14 +1006,11 @@
     scatter_start(7, 0, 1)
     in_t[...] = both.T
     spread_rows(IN, in_t, l_in)
-    e3r(QKV)
-    e3r(G2)
     e2(G1)
     e2(U1)
-    e4(AO)
+    e4(U2)
+    e3r(G2)
     e1(RO)
-    e2r(D1)
-    e4(U2)
     gg00 = []
     for h in range(2):
         dv, gg = rms_back(x_s[mine[h], :].astype(F32), gain(0, 0), scatter_wait(7, h))
@@ -994,13 +1030,11 @@
         copy.start()
     e2(RO)
     e1(IN)
+    e2r(U1)
     e2r(G1)
-    e2r(U1)
-    e4(QKV)
+    e2r(D1)
     e5(AO)
-    e3(D1)
     e2(IN)
-    e2r(RO)
     deliver(yb, y_o, 1, 0)
     for copy in gn_copies:
         copy.wait()
@@ -1018,48 +1052,48 @@
 
     l_misc[0] = misc_rows(it.m)[...]
     spread(MISC, 0, misc_rows, lambda k: l_misc.at[k])
+    e4(QKV)
+    e5(D2)
+    e5(U2)
     e4(G2)
-    e4(D2)
-    e5(QKV)
-    e6(AO)
-    e5(U2)
-    e3r(D1)
-    e3(G1)
-    e2r(IN)
     e3(RO)
     e3(U1)
+    e3(D1)
+    e3(G1)
+    e6(AO)
+    e2r(IN)
+    e6(U2)
     e1(MISC)
     e2(MISC)
+    e5(QKV)
     e5(G2)
-    e5(D2)
-    e6(U2)
+    e3r(U1)
+    e6(D2)
+    e4(RO)
+    e3r(G1)
+    e3(MISC)
+    e3r(D1)
+    e3(IN)
+    e6(G2)
+    e4(U1)
     e6(QKV)
-    e3r(G1)
     e4(D1)
-    e3r(U1)
-    e3(IN)
-    e3(MISC)
-    e3r(RO)
-    e6(G2)
-    e6(D2)
+    e3r(IN)
+    e5(RO)
     e4(G1)
-    e3r(IN)
-    e4(RO)
+    e4(MISC)
+    e5(U1)
+    e4(IN)
     e5(D1)
-    e4(U1)
-    e4(MISC)
+    e6(RO)
     e5(G1)
-    e4(IN)
-    e5(RO)
+    e5(MISC)
+    e5(IN)
+    e6(U1)
     e6(D1)
-    e5(U1)
-    e5(MISC)
     e6(G1)
-    e5(IN)
-    e6(RO)
-    e6(U1)
+    e6(IN)
     e6(MISC)
-    e6(IN)
     deliver_wait(yb, y_o, 1, 0)
     deliver_wait(xb, dx_o, 0, 1)
     for copy in swap:
@@ -1071,7 +1105,7 @@
 
 
 def whole_call(tokens, plan, cot, gains, conv, vec, weights):
-    vm = pl.BlockSpec(memory_space=pltpu.VMEM)
+    sm = pl.BlockSpec(memory_space=pltpu.SMEM)
     hbm = pl.BlockSpec(memory_space=pl.ANY)
     V = pltpu.VMEM
     dma = pltpu.SemaphoreType.DMA
@@ -1088,9 +1122,10 @@
     return pl.pallas_call(
         whole_kernel,
         name="whole",
-        out_shape=[jax.ShapeDtypeStruct(shape, BF) for shape in shapes],
-        in_specs=[vm, pl.BlockSpec(memory_space=pltpu.SMEM), vm, vm, vm, vm] + [hbm] * 9,
-        out_specs=[hbm] * 9,
+        out_shape=[jax.ShapeDtypeStruct((2,), jnp.int32)]
+        + [jax.ShapeDtypeStruct(shape, BF) for shape in shapes],
+        in_specs=[hbm, sm] + [hbm] * 13,
+        out_specs=[sm] + [hbm] * 9,
         scratch_shapes=[
             V((D, 2 * RQ), BF), V((HD, 2 * RQ), BF), V((2, RQ, HW), BF), V((2, 8, D), F32),
             V((2, D, FQ), BF), V((2, D, FQ), BF), V((2, FQ, D), BF),
@@ -1109,6 +1144,8 @@
             V((288, 512), BF), V((288, 512), BF), V((288, 512), BF), V((288, 512), BF), V((288, 512), BF),
             V((160, 512), BF), V((256, 512), BF), V((4, 32, D), BF),
             V((144, D), BF), V((2, 144, D), BF),
+            V((HW, 2, RQ), BF), V((64, 2, RQ), BF), V((SEQ, D), BF),
+            V((1, 2, D), F32), V((2, RQ), BF), V((2, RQ), BF), dma((7,)),
             *crs, *gots, *fins,
             dma((10,)), dma((10,)), dma((10,)), dma((6, 2, 4)), dma((6, 2, 4)), dma((8, 2, 4)), dma((8, 2, 4)),
             dma((4,)), dma((4,)), dma((4,)), dma((4,)), dma((2, 2)), dma((2, 4, 2)), dma((2, 2, 4, 2)),
@@ -1116,7 +1153,7 @@
             dma((11, 8)), dma((11, 8)), dma((11, 12)), dma((11, 12)), dma((11,)), dma((11,)), dma((11,)),
         ],
         compiler_params=pltpu.CompilerParams(
-            collective_id=0, has_side_effects=True, vmem_limit_bytes=63 * 2**20
+            collective_id=0, has_side_effects=True, vmem_limit_bytes=64 * 2**20 - 2**17
         ),
     )(tokens, plan, cot, gains, conv, vec, *weights)
 
@@ -1213,15 +1250,13 @@
     tokens, plan_order, cotangent, norm_gains, ffn_gate, ffn_up, ffn_down,
     rec_in, rec_gates, rec_conv, rec_vec, rec_out, att_q, att_kv, att_out,
 ):
-    y, dx, _, ffn, qkv, ao, rin, ro, misc = whole_call(
+    scalars, y, dx, _, ffn, qkv, ao, rin, ro, misc = whole_call(
         tokens, plan_order, cotangent, norm_gains, rec_conv, rec_vec,
         (
-            rec_in.reshape(HW, 2 * RQ), rec_gates.reshape(64, 2 * RQ), rec_out,
+            rec_in, rec_gates, rec_out,
             ffn_gate, ffn_up, ffn_down, att_q, att_kv, att_out,
         ),
     )
-    s = lax.axis_index("section").astype(jnp.int32)
-    scalars = jnp.stack([s, plan_order[0, 0]])
     return unpack_call(scalars, dx, y, ffn, qkv, ao, rin, ro, misc)
 
 

time: 227 us -> 220 us (0.969)
  local copies, waits for them, and re-layouts: 4.54 us -> 0 us
    unnamed x2 -> x0, local copies, waits for them, and re-layouts: 4.54 us -> none
where the time goes in v5:
time: 220 us; the launch traced here: 219 us
  Pallas kernels  219 us (100%)
    pallas_call x1, Pallas kernels, whole_call(): pl.pallas_call(whole_kernel, name='whole', out_shape=[jax.ShapeDtypeStruc...  202 us
    pallas_call x1, Pallas kernels, unpack_call(): pl.pallas_call(unpack_kernel, name='unpack', out_shape=[sds((1, 2 * SEQ,...  16.8 us

profile of v5, /device:TPU:1, one launch (start us, length us, event | category | flops | bytes accessed | tf_op | source)
XLA Modules:
  0.0 219.4 jit_solution(16341497667857005592)
XLA Ops:
  0.7 201.7 %whole.1 = (s32[2]{0:T(128)}, bf16[2,128,1536]{2,1,0:T(8,128)(2,1)}, bf16[2,128,1536]{2,1,0:T(8,128)(2,1)}, bf16[5,512,1536]{2,1,0:T(8,128)(2,1)}, bf16[6,1152,1...) custom-call(bf16[256,1536]{1,0:T(8,128)(2,1)} %tok_ref.1, ...), custom_call_target="tpu_custom_call" | custom-call | tf_op jit(solution)/shard_map/whole/pallas_call | solution.py:1122
  202.4 16.8 %unpack.1 = (f32[1,256,1536]{2,1,0:T(8,128)}, f32[1,2,1536]{2,1,0:T(2,128)}, f32[1,1536,1152]{2,1,0:T(8,128)}, f32[1,1536,1152]{2,1,0:T(8,128)}, f32[1,1152,1536...) custom-call(s32[2]{0:T(128)} %get-tuple-element.22.n_ref, ...), custom_call_target="tpu_custom_call" | custom-call | tf_op jit(solution)/shard_map/unpack/pallas_call | solution.py:1207

commit v6 on v5

--- a/solution.py
+++ b/solution.py
@@ -827,8 +827,6 @@
     for h in range(2):
         yb[sub[h], :] = (res[2, sub[h]] + scatter_wait(3, h)).astype(BF)
     ring_pass(RNA)
-    ring_pass(RN2B)
-    e1(D2)
     gg11 = []
     for h in range(2):
         dv, gg = rms_back(res[2, sub[h]], gain(1, 1), scatter_wait(4, h))
@@ -836,6 +834,8 @@
         dx1 = cot_s[mine[h], :].astype(F32) + dv
         res[3, sub[h]] = dx1
         gather_start(3, h, dx1)
+    ring_pass(RN2B)
+    e1(D2)
     e2(D2)
 
     gather_wait(3, 0)

time: 220 us -> 215 us (0.977)
  Pallas kernels: 219 us -> 214 us
    pallas_call x1, Pallas kernels: 202 us -> 197 us  [whole_call(): pl.pallas_call(whole_kernel, name='whole', out_shape=[jax.ShapeDtypeStruc...]
where the time goes in v6:
time: 215 us
  Pallas kernels  214 us (100%)
    pallas_call x1, Pallas kernels, whole_call(): pl.pallas_call(whole_kernel, name='whole', out_shape=[jax.ShapeDtypeStruc...  197 us
    pallas_call x1, Pallas kernels, unpack_call(): pl.pallas_call(unpack_kernel, name='unpack', out_shape=[sds((1, 2 * SEQ,...  16.8 us

profile of v6, /device:TPU:1, one launch (start us, length us, event | category | flops | bytes accessed | tf_op | source)
XLA Modules:
  0.0 215.1 jit_solution(2663465826284519863)
XLA Ops:
  0.7 197.4 %whole.1 = (s32[2]{0:T(128)}, bf16[2,128,1536]{2,1,0:T(8,128)(2,1)}, bf16[2,128,1536]{2,1,0:T(8,128)(2,1)}, bf16[5,512,1536]{2,1,0:T(8,128)(2,1)}, bf16[6,1152,1...) custom-call(bf16[256,1536]{1,0:T(8,128)(2,1)} %tok_ref.1, ...), custom_call_target="tpu_custom_call" | custom-call | tf_op jit(solution)/shard_map/whole/pallas_call | solution.py:1122
  198.1 16.8 %unpack.1 = (f32[1,256,1536]{2,1,0:T(8,128)}, f32[1,2,1536]{2,1,0:T(2,128)}, f32[1,1536,1152]{2,1,0:T(8,128)}, f32[1,1536,1152]{2,1,0:T(8,128)}, f32[1,1152,1536...) custom-call(s32[2]{0:T(128)} %get-tuple-element.22.n_ref, ...), custom_call_target="tpu_custom_call" | custom-call | tf_op jit(solution)/shard_map/unpack/pallas_call | solution.py:1207
